TPU v7x, 512 devices: a whole 4x4x16 slice. The times are simulated.
512 devices in a mesh: row: 64 (over z, y_hi, core), col: 8 (over x, y_lo).
Axes of the slice: x: 4, y: 4 (y_hi: 2, y_lo: 2; y = y_hi * 2 + y_lo), z: 16, core: 2. Of those that a mesh axis runs over, the one named last changes fastest.
Arguments:
- positions: float32 [3, 131072], P(None, ('row', 'col')), as said below
- velocities: float32 [3, 131072], P(None, ('row', 'col')), may hold values from -6 to 6
- old_forces: float32 [3, 131072], P(None, ('row', 'col')), may hold values from -6 to 6
- charges: float32 [131072], P(('row', 'col')), may hold values from -3 to 3
- atom_types: int32 [131072], P(('row', 'col')), may hold values from 0 to 7
- type_table: float32 [7, 8], replicated, may hold values from 0.003 to 2, as said below
- tile_pairs: int32 [64, 8, 2, 32], P('row', 'col'), may hold values from -1 to 127, as said below
Outputs:
- new_positions: float32 [3, 131072], P(None, ('row', 'col'))
- new_velocities: float32 [3, 131072], P(None, ('row', 'col'))
- new_forces: float32 [3, 131072], P(None, ('row', 'col'))
Inputs may be any that keep to these rules, and one draw needn't show every extreme that they name: `positions`: the atoms of one block lie together in a cube of its own; the blocks' cubes fill a cubic lattice in the order of the block numbers, at about 0.1 atoms per cubic angstrom. `tile_pairs`: on each device the first n slots hold distinct pairs (a, g) with a below 16 and g below 128, each a tile whose blocks' cubes lie within 12 angstrom of each other; the other slots hold -1 in both entries. n is at most 32, differs from device to device, and equals 32 on the device with the most such tiles when it has 32 or more; the list is a sampled part of each device's near tiles, not all of them. `type_table`: Rows: intrinsic radii 1 to 2, screening scales 0.15 to 0.6, neck weights 0.003 to 0.012, alpha 0.6 to 1, beta 0.3 to 0.9, gamma 0.2 to 0.6, masses 0.5 to 2.
All inputs are finite; a program needn't handle non-finite values.
Results may differ from a plain program's by a relative error of at most 0.0003.
Values sent between devices are 32-bit elements; how exact they have to be, the bound alone decides.
No kernel may reach another device: no remote copies, remote signals or barrier semaphores. Data moves between devices by JAX's collectives and lax.ppermute only.
A program may use at most 64 MiB of HBM per device.

v0:
```python
import jax
import jax.numpy as jnp
from jax import lax
from jax.sharding import PartitionSpec as P

TILE = 128
BLK_DEV = 2
GROUP = 4


CUTOFF = 12.0
COULOMB = 32.0
TIMESTEP = 0.5
OFFSET = 0.09
NECK_GAP = 0.5
NECK_WIDTH = 16.0


def joined_along(pieces, dim):
    shape = list(pieces.shape[1:])
    shape[dim] *= pieces.shape[0]
    return jnp.moveaxis(pieces, 0, dim).reshape(shape)


def copy_for_each(shard, axis):
    copies = jnp.broadcast_to(shard, (lax.axis_size(axis), *shard.shape))
    return lax.all_to_all(copies, axis, split_axis=0, concat_axis=0, tiled=True)


def gathered_copies(shard, axis, dim):
    return joined_along(copy_for_each(shard, axis), dim)


def taken_together(shard, axis):
    return copy_for_each(shard, axis).sum(axis=0)


def split_up(shard, dim, length):
    before, after = (shard.shape[:dim], shard.shape[dim + 1 :])
    return jnp.moveaxis(shard.reshape(*before, length, -1, *after), dim, 0)


def summed_on_arrival(shard, axis, dim):
    length = lax.axis_size(axis)
    pieces = lax.all_to_all(split_up(shard, dim, length), axis, 0, 0, tiled=True)
    return jnp.sum(pieces, axis=0)


def taper(dist_sq):
    taper_base = jnp.maximum(1.0 - dist_sq / (CUTOFF * CUTOFF), 0.0)
    return (taper_base * taper_base, -2.0 * taper_base / (CUTOFF * CUTOFF))


def screening(dist_sq, intrinsic, other_radius, other_scale, other_neck):
    soft_sq = dist_sq + intrinsic * intrinsic
    neck_gap = intrinsic + other_radius + NECK_GAP
    neck_off = dist_sq - neck_gap * neck_gap
    neck_bump = jnp.exp(-neck_off * neck_off / NECK_WIDTH)
    volume = other_scale * other_radius * other_radius * other_radius
    descreen = volume / (soft_sq * soft_sq) + other_neck * neck_bump
    slope = -2.0 * volume / (soft_sq * soft_sq * soft_sq) - other_neck * neck_bump * neck_off * (
        2.0 / NECK_WIDTH
    )
    weight, w_slope = taper(dist_sq)
    return (weight * descreen, w_slope * descreen + weight * slope)


def separation(coords_i, coords_j):
    offset_vec = coords_i[:, :, :, None] - coords_j[:, :, None, :]
    return (offset_vec, jnp.sum(offset_vec * offset_vec, axis=1))


def born_terms(side_i, side_j, mask):
    offset_vec, dist_sq = separation(side_i[:, 0:3], side_j[:, 0:3])
    value, slope = screening(
        dist_sq,
        side_i[:, 4][:, :, None],
        side_j[:, 4][:, None, :],
        side_j[:, 5][:, None, :],
        side_j[:, 6][:, None, :],
    )
    return jnp.sum(mask * value, axis=2)[:, None, :]


def pair_terms(side_i, side_j, mask):
    offset_vec, dist_sq = separation(side_i[:, 0:3], side_j[:, 0:3])
    charge_pair = side_i[:, 3][:, :, None] * side_j[:, 3][:, None, :]
    radius_j = side_j[:, -1][:, None, :]
    radii_prod = side_i[:, -1][:, :, None] * radius_j
    radii_exp = jnp.exp(-dist_sq / (4.0 * radii_prod))
    inv_eff = 1.0 / jnp.sqrt(dist_sq + radii_prod * radii_exp)
    inv_cube = inv_eff * inv_eff * inv_eff
    weight, w_slope = taper(dist_sq)
    d_dist = (
        mask
        * charge_pair
        * (w_slope * inv_eff - 0.5 * weight * (1.0 - 0.25 * radii_exp) * inv_cube)
    )
    d_radius = (
        mask
        * -0.5
        * weight
        * charge_pair
        * inv_cube
        * radii_exp
        * (1.0 + dist_sq / (4.0 * radii_prod))
        * radius_j
    )
    direct = 2.0 * COULOMB * jnp.sum(d_dist[:, None] * offset_vec, axis=3)
    return jnp.concatenate([direct, jnp.sum(d_radius, axis=2)[:, None, :]], axis=1)


def chain_terms(side_i, side_j, mask):
    offset_vec, dist_sq = separation(side_i[:, 0:3], side_j[:, 0:3])
    value_ij, slope_ij = screening(
        dist_sq,
        side_i[:, 4][:, :, None],
        side_j[:, 4][:, None, :],
        side_j[:, 5][:, None, :],
        side_j[:, 6][:, None, :],
    )
    value_ji, slope_ji = screening(
        dist_sq,
        side_j[:, 4][:, None, :],
        side_i[:, 4][:, :, None],
        side_i[:, 5][:, :, None],
        side_i[:, 6][:, :, None],
    )
    factor = mask * (side_i[:, -1][:, :, None] * slope_ij + side_j[:, -1][:, None, :] * slope_ji)
    return -2.0 * jnp.sum(factor[:, None] * offset_vec, axis=3)


def radius_terms(born_sum, intrinsic, coef_alpha, coef_beta, coef_gamma):
    scaled = intrinsic * born_sum
    poly_arg = (
        coef_alpha * scaled - coef_beta * scaled * scaled + coef_gamma * scaled * scaled * scaled
    )
    squash = jnp.tanh(poly_arg)
    radius = 1.0 / (1.0 / intrinsic - squash / (intrinsic + OFFSET))
    poly_slope = coef_alpha - 2.0 * coef_beta * scaled + 3.0 * coef_gamma * scaled * scaled
    radius_rate = (
        radius * radius * (1.0 - squash * squash) * poly_slope * intrinsic / (intrinsic + OFFSET)
    )
    return (radius, radius_rate)


def run_tiles(func, rows, pack_i, pack_j, tiles_i, tiles_j, live_f, self_pair, group_count):
    block_total = pack_i.shape[1]
    diagonal = jnp.eye(TILE, dtype=jnp.float32)
    block_ids = jnp.arange(block_total, dtype=jnp.int32)

    def one_turn(turn_index, summed):
        first = turn_index * GROUP
        group_i = lax.dynamic_slice_in_dim(tiles_i, first, GROUP)
        group_j = lax.dynamic_slice_in_dim(tiles_j, first, GROUP)
        group_live = lax.dynamic_slice_in_dim(live_f, first, GROUP)
        group_self = lax.dynamic_slice_in_dim(self_pair, first, GROUP)
        side_i = jnp.moveaxis(jnp.take(pack_i, group_i, axis=1), 1, 0)
        side_j = jnp.moveaxis(jnp.take(pack_j, group_j, axis=1), 1, 0)
        mask = group_live[:, None, None] * (1.0 - group_self[:, None, None] * diagonal)
        partial_sums = func(side_i, side_j, mask)
        owner = (group_i[:, None] == block_ids[None, :]).astype(jnp.float32)
        return summed + jnp.einsum(
            "gk,gra->kra", owner, partial_sums, precision=lax.Precision.HIGHEST
        )

    summed = lax.fori_loop(
        0, group_count, one_turn, jnp.zeros((block_total, rows, TILE), jnp.float32)
    )
    return jnp.moveaxis(summed, 1, 0).reshape(rows, block_total * TILE)


def body(positions, velocities, old_forces, charges, atom_types, type_table, tile_pairs):
    col_count = lax.axis_size("col")
    row_count = lax.axis_size("row")
    col_index = lax.axis_index("col")
    row_index = lax.axis_index("row")
    own_count = positions.shape[1]
    type_ids = jnp.arange(type_table.shape[1], dtype=jnp.int32)
    onehot = (atom_types[None, :] == type_ids[:, None]).astype(jnp.float32)
    params = jnp.sum(type_table[:, :, None] * onehot[None, :, :], axis=1)
    atom_mass = params[6]
    new_positions = (
        positions + TIMESTEP * velocities + TIMESTEP * TIMESTEP / (2.0 * atom_mass) * old_forces
    )
    own_data = jnp.concatenate([new_positions, charges[None, :], params[0:6]], axis=0)
    side_i = gathered_copies(own_data, "col", 1)
    side_j = gathered_copies(own_data[0:7], "row", 1)
    blocks_i = col_count * BLK_DEV
    blocks_j = row_count * BLK_DEV
    pack_i = side_i.reshape(10, blocks_i, TILE)
    pack_j = side_j.reshape(7, blocks_j, TILE)
    tile_list = tile_pairs[0, 0]
    live_slot = tile_list[0] >= 0
    tiles_i = jnp.maximum(tile_list[0], 0)
    tiles_j = jnp.maximum(tile_list[1], 0)
    global_i = row_index * blocks_i + tiles_i
    global_j = (tiles_j // BLK_DEV * col_count + col_index) * BLK_DEV + tiles_j % BLK_DEV
    self_pair = (global_i == global_j).astype(jnp.float32)
    live_f = live_slot.astype(jnp.float32)
    group_count = (jnp.sum(live_slot.astype(jnp.int32)) + GROUP - 1) // GROUP

    def tile_sweep(func, rows, data_i, data_j):
        return run_tiles(
            func, rows, data_i, data_j, tiles_i, tiles_j, live_f, self_pair, group_count
        )

    born_part = tile_sweep(born_terms, 1, pack_i, pack_j)[0]
    born_all = taken_together(born_part, "col")
    radius_i, rate_i = radius_terms(born_all, side_i[4], side_i[7], side_i[8], side_i[9])
    radius_own = lax.dynamic_slice_in_dim(radius_i, col_index * own_count, own_count)
    radius_j = gathered_copies(radius_own, "row", 0)
    with_radius_i = jnp.concatenate([pack_i, radius_i.reshape(1, blocks_i, TILE)], axis=0)
    with_radius_j = jnp.concatenate([pack_j, radius_j.reshape(1, blocks_j, TILE)], axis=0)
    pair_part = tile_sweep(pair_terms, 4, with_radius_i, with_radius_j)
    grad_all = taken_together(pair_part[3], "col")
    chain_i = (
        COULOMB * side_i[3] * side_i[3] / (2.0 * radius_i * radius_i) - COULOMB * grad_all
    ) * rate_i
    chain_own = lax.dynamic_slice_in_dim(chain_i, col_index * own_count, own_count)
    chain_j = gathered_copies(chain_own, "row", 0)
    with_chain_i = jnp.concatenate([pack_i, chain_i.reshape(1, blocks_i, TILE)], axis=0)
    with_chain_j = jnp.concatenate([pack_j, chain_j.reshape(1, blocks_j, TILE)], axis=0)
    chain_part = tile_sweep(chain_terms, 3, with_chain_i, with_chain_j)
    force_sum = pair_part[0:3] + chain_part
    new_forces = summed_on_arrival(force_sum, "col", 1)
    new_velocities = velocities + TIMESTEP / (2.0 * atom_mass) * (old_forces + new_forces)
    return (new_positions, new_velocities, new_forces)


def solution(mesh):
    return jax.shard_map(
        body,
        mesh=mesh,
        in_specs=(
            P(None, ("row", "col")),
            P(None, ("row", "col")),
            P(None, ("row", "col")),
            P(("row", "col")),
            P(("row", "col")),
            P(),
            P("row", "col", None, None),
        ),
        out_specs=(P(None, ("row", "col")), P(None, ("row", "col")), P(None, ("row", "col"))),
        check_vma=False,
    )
```

profile of v0, /device:TPU:1, one launch (start us, length us, event | category | flops | bytes accessed | tf_op | source)
XLA Modules:
  0.0 211.2 jit_solution(5079882211280808605)
XLA Ops:
  0.6 0.7 fusion.83
  1.5 0.6 copy-done.1
  2.1 0.7 copy-done.7
  2.8 0.7 broadcast_in_dim.114
  3.5 5.9 %all-to-all-start = ((f32[8,10,256]{2,1,0:T(8,128)}), f32[8,10,256]{2,1,0:T(8,128)S(1)}, u32[]{:S(2)}, u32[]{:S(2)}) async-start(f32[8,10,256]{2,1,0:T(8,128)} %broadcast_in_dim.114), calls=%async_computation | async-start | bytes 262144 | tf_op jit(solution)/shard_map/all_to_all | solution.py:27
  9.4 5.3 %all-to-all-done = f32[8,10,256]{2,1,0:T(8,128)S(1)} async-done(((f32[8,10,256]{2,1,0:T(8,128)}), f32[8,10,256]{2,1,0:T(8,128)S(1)}, u32[]{:S(2)}, u32[]{:S(2)}) %all-to-all-start) | async-done | bytes 81952 | tf_op jit(solution)/shard_map/all_to_all | solution.py:27
  14.6 0.8 broadcast_in_dim.116
  15.4 20.2 %all-to-all-start.1 = ((f32[64,7,256]{2,1,0:T(8,128)}), f32[64,7,256]{2,1,0:T(8,128)S(1)}, u32[]{:S(2)}, u32[]{:S(2)}) async-start(f32[64,7,256]{2,1,0:T(8,128)} %broadcast_in_dim.116), calls=%async_computation.1 | async-start | bytes 1048576 | tf_op jit(solution)/shard_map/all_to_all | solution.py:27
  35.7 0.6 maximum_bitcast_fusion
  37.1 32.5 %all-to-all-done.1 = f32[64,7,256]{2,1,0:T(8,128)S(1)} async-done(((f32[64,7,256]{2,1,0:T(8,128)}), f32[64,7,256]{2,1,0:T(8,128)S(1)}, u32[]{:S(2)}, u32[]{:S(2)}) %all-to-all-start.1) | async-done | bytes 458784 | tf_op jit(solution)/shard_map/all_to_all | solution.py:27
  69.7 5.0 %while.37 = (s32[]{:T(128)}, f32[16,1,128]{2,0,1:T(8,128)S(1)}, s32[]{:T(128)}, s32[32]{0:T(128)S(1)}, f32[32]{0:T(128)S(1)}, /*index=5*/f32[32]{0:T(128)S(1)}, ...) while((s32[]{:T(128)}, f32[16,1,128]{2,0,1:T(8,128)S(1)}, ...), condition=%wide.region_5.6_spmd.clone, body=%wide.region_2.5_spmd.clone.sunk | while | flops 2111618 | bytes 893399 | solution.py:167
  69.8 0.6 gather_fusion.1
  70.4 0.6 gather_fusion
  71.5 0.4 fusion.122
  72.3 0.6 gather_fusion.1
  72.9 0.6 gather_fusion
  74.7 0.7 broadcast_in_dim.118
  75.3 16.4 %all-to-all-start.2 = ((f32[8,1,2048]{2,1,0:T(1,128)}), f32[8,1,2048]{2,1,0:T(1,128)S(1)}, u32[]{:S(2)}, u32[]{:S(2)}) async-start(f32[8,1,2048]{2,1,0:T(1,128)} %broadcast_in_dim.118), calls=%async_computation.2 | async-start | bytes 131072 | tf_op jit(solution)/shard_map/all_to_all | solution.py:27
  91.8 5.1 %all-to-all-done.2 = f32[8,1,2048]{2,1,0:T(1,128)S(1)} async-done(((f32[8,1,2048]{2,1,0:T(1,128)}), f32[8,1,2048]{2,1,0:T(1,128)S(1)}, u32[]{:S(2)}, u32[]{:S(2)}) %all-to-all-start.2) | async-done | bytes 65568 | tf_op jit(solution)/shard_map/all_to_all | solution.py:27
  97.0 0.7 broadcast_in_dim.119
  97.7 7.4 %all-to-all-start.3 = ((f32[64,1,256]{2,1,0:T(1,128)}), f32[64,1,256]{2,1,0:T(1,128)S(1)}, u32[]{:S(2)}, u32[]{:S(2)}) async-start(f32[64,1,256]{2,1,0:T(1,128)} %broadcast_in_dim.119), calls=%async_computation.3 | async-start | bytes 131072 | tf_op jit(solution)/shard_map/all_to_all | solution.py:27
  105.1 15.9 %all-to-all-done.3 = f32[64,1,256]{2,1,0:T(1,128)S(1)} async-done(((f32[64,1,256]{2,1,0:T(1,128)}), f32[64,1,256]{2,1,0:T(1,128)S(1)}, u32[]{:S(2)}, u32[]{:S(2)}) %all-to-all-start.3) | async-done | bytes 65568 | tf_op jit(solution)/shard_map/all_to_all | solution.py:27
  121.1 6.5 %while.38 = (s32[]{:T(128)}, f32[16,4,128]{2,0,1:T(8,128)S(1)}, s32[]{:T(128)}, s32[32]{0:T(128)S(1)}, f32[32]{0:T(128)S(1)}, /*index=5*/f32[32]{0:T(128)S(1)}, ...) while((s32[]{:T(128)}, f32[16,4,128]{2,0,1:T(8,128)S(1)}, ...), condition=%wide.region_11.14_spmd.clone, body=%wide.region_7.13_spmd.clone.sunk | while | flops 3921026 | bytes 1511895 | solution.py:167
  121.2 0.6 gather_fusion.3
  121.9 0.6 gather_fusion.2
  123.0 0.5 fusion.130
  123.5 0.5 fusion.131
  124.5 0.6 gather_fusion.3
  125.1 0.6 gather_fusion.2
  126.2 0.5 fusion.130
  126.8 0.5 fusion.131
  127.6 0.6 broadcast_in_dim.122
  128.3 20.7 %all-to-all-start.4 = ((f32[8,1,2048]{2,1,0:T(1,128)}), f32[8,1,2048]{2,1,0:T(1,128)S(1)}, u32[]{:S(2)}, u32[]{:S(2)}) async-start(f32[8,1,2048]{2,1,0:T(1,128)} %broadcast_in_dim.122), calls=%async_computation.4 | async-start | bytes 131072 | tf_op jit(solution)/shard_map/all_to_all | solution.py:27
  149.0 5.1 %all-to-all-done.4 = f32[8,1,2048]{2,1,0:T(1,128)S(1)} async-done(((f32[8,1,2048]{2,1,0:T(1,128)}), f32[8,1,2048]{2,1,0:T(1,128)S(1)}, u32[]{:S(2)}, u32[]{:S(2)}) %all-to-all-start.4) | async-done | bytes 65568 | tf_op jit(solution)/shard_map/all_to_all | solution.py:27
  154.3 0.7 broadcast_in_dim.123
  154.9 6.6 %all-to-all-start.5 = ((f32[64,1,256]{2,1,0:T(1,128)}), f32[64,1,256]{2,1,0:T(1,128)S(1)}, u32[]{:S(2)}, u32[]{:S(2)}) async-start(f32[64,1,256]{2,1,0:T(1,128)} %broadcast_in_dim.123), calls=%async_computation.5 | async-start | bytes 131072 | tf_op jit(solution)/shard_map/all_to_all | solution.py:27
  161.6 15.8 %all-to-all-done.5 = f32[64,1,256]{2,1,0:T(1,128)S(1)} async-done(((f32[64,1,256]{2,1,0:T(1,128)}), f32[64,1,256]{2,1,0:T(1,128)S(1)}, u32[]{:S(2)}, u32[]{:S(2)}) %all-to-all-start.5) | async-done | bytes 65568 | tf_op jit(solution)/shard_map/all_to_all | solution.py:27
  177.5 6.7 %while.39 = (s32[]{:T(128)}, f32[16,3,128]{2,0,1:T(8,128)S(1)}, s32[]{:T(128)}, s32[32]{0:T(128)S(1)}, f32[32]{0:T(128)S(1)}, /*index=5*/f32[32]{0:T(128)S(1)}, ...) while((s32[]{:T(128)}, f32[16,3,128]{2,0,1:T(8,128)S(1)}, ...), condition=%wide.region_16.19_spmd.clone, body=%wide.region_13.18_spmd.clone.sunk | while | flops 4414082 | bytes 1526231 | solution.py:167
  177.7 0.6 gather_fusion.5
  178.4 0.6 gather_fusion.4
  179.5 0.6 fusion.137
  180.1 0.5 fusion.138
  181.0 0.6 gather_fusion.5
  181.7 0.6 gather_fusion.4
  182.8 0.6 fusion.137
  183.5 0.5 fusion.138
  184.3 26.3 %all_to_all.39 = f32[8,3,256]{2,1,0:T(4,128)S(1)} all-to-all(f32[8,3,256]{2,1,0:T(4,128)S(1)} %copy.69), channel_id=1, replica_groups=mesh['row'=64,'col'=8] {'col'}, dimensions={0} | all-to-all | bytes 49152 | tf_op jit(solution)/shard_map/all_to_all | solution.py:45
  210.6 0.6 multiply_add_fusion
  (146 shorter events, 7.4 us)
Async XLA Ops:
  0.6 0.7 copy-start.4
  1.3 0.7 copy-start.1
  1.3 0.7 copy-start.5
  1.4 0.7 copy-start
  2.1 0.7 copy-start.3
  2.1 0.7 copy-start.7
  3.5 11.1 %all-to-all-start = ((f32[8,10,256]{2,1,0:T(8,128)}), f32[8,10,256]{2,1,0:T(8,128)S(1)}, u32[]{:S(2)}, u32[]{:S(2)}) async-start(f32[8,10,256]{2,1,0:T(8,128)} %broadcast_in_dim.114), calls=%async_computation | async-start | bytes 262144 | tf_op jit(solution)/shard_map/all_to_all | solution.py:27
  15.4 20.2 %copy-start.6 = (s32[1,1,2,32]{3,2,1,0:T(2,128)S(1)}, s32[1,1,2,32]{3,2,1,0:T(2,128)}, u32[]{:S(2)}) copy-start(s32[1,1,2,32]{3,2,1,0:T(2,128)} %param.23) | copy-start | bytes 772
  15.4 54.2 %all-to-all-start.1 = ((f32[64,7,256]{2,1,0:T(8,128)}), f32[64,7,256]{2,1,0:T(8,128)S(1)}, u32[]{:S(2)}, u32[]{:S(2)}) async-start(f32[64,7,256]{2,1,0:T(8,128)} %broadcast_in_dim.116), calls=%async_computation.1 | async-start | bytes 1048576 | tf_op jit(solution)/shard_map/all_to_all | solution.py:27
  75.3 21.5 %all-to-all-start.2 = ((f32[8,1,2048]{2,1,0:T(1,128)}), f32[8,1,2048]{2,1,0:T(1,128)S(1)}, u32[]{:S(2)}, u32[]{:S(2)}) async-start(f32[8,1,2048]{2,1,0:T(1,128)} %broadcast_in_dim.118), calls=%async_computation.2 | async-start | bytes 131072 | tf_op jit(solution)/shard_map/all_to_all | solution.py:27
  97.7 23.3 %all-to-all-start.3 = ((f32[64,1,256]{2,1,0:T(1,128)}), f32[64,1,256]{2,1,0:T(1,128)S(1)}, u32[]{:S(2)}, u32[]{:S(2)}) async-start(f32[64,1,256]{2,1,0:T(1,128)} %broadcast_in_dim.119), calls=%async_computation.3 | async-start | bytes 131072 | tf_op jit(solution)/shard_map/all_to_all | solution.py:27
  128.3 25.8 %all-to-all-start.4 = ((f32[8,1,2048]{2,1,0:T(1,128)}), f32[8,1,2048]{2,1,0:T(1,128)S(1)}, u32[]{:S(2)}, u32[]{:S(2)}) async-start(f32[8,1,2048]{2,1,0:T(1,128)} %broadcast_in_dim.122), calls=%async_computation.4 | async-start | bytes 131072 | tf_op jit(solution)/shard_map/all_to_all | solution.py:27
  154.9 22.5 %all-to-all-start.5 = ((f32[64,1,256]{2,1,0:T(1,128)}), f32[64,1,256]{2,1,0:T(1,128)S(1)}, u32[]{:S(2)}, u32[]{:S(2)}) async-start(f32[64,1,256]{2,1,0:T(1,128)} %broadcast_in_dim.123), calls=%async_computation.5 | async-start | bytes 131072 | tf_op jit(solution)/shard_map/all_to_all | solution.py:27
  210.6 0.6 copy-start.2
where the time goes:
time: 213 us; the launch traced here: 211 us
  waiting for transfers between devices  79.7 us (37%)
  starting transfers between devices  77.1 us (36%)
  blocking collectives  26.3 us (12%)
  local copies, waits for them, and re-layouts  13.4 us (6%)
  other arithmetic  11 us (5%)
    all_to_all x6, waiting for transfers between devices, copy_for_each(): return lax.all_to_all(copies, axis, split_axis=0, concat_axis=0, tiled=True)  79.7 us
    all_to_all x6, starting transfers between devices, copy_for_each(): return lax.all_to_all(copies, axis, split_axis=0, concat_axis=0, tiled=True)  77.1 us
    all_to_all x1, blocking collectives, summed_on_arrival(): lax.all_to_all(split_up(shard, dim, length), axis, 0, 0, tiled=True)  26.3 us
  transfers between devices with their start and end apart: 6, of which 6 were waited for; matrix products, arithmetic and copies ran while one was open for 0% of the time, Pallas kernels for 0%

commit v1 on v0

v1 whole, which is shorter than its diff:
```python
import jax
import jax.numpy as jnp
from jax import lax
from jax.experimental import pallas as pl
from jax.experimental.pallas import tpu as pltpu
from jax.sharding import Mesh
from jax.sharding import PartitionSpec as P

TILE = 128
SLOTS = 32
CHUNK = 32

CUTOFF = 12.0
COULOMB = 32.0
TIMESTEP = 0.5
OFFSET = 0.09
NECK_GAP = 0.5
NECK_WIDTH = 16.0
INV_SQ = 1.0 / (CUTOFF * CUTOFF)

AXES = ("zh", "zl", "yh", "core", "x", "yl")
SIZES = (4, 4, 2, 2, 4, 2)
REP = ("zh",)
ROWS = ("zl", "yh", "core")
COLS = ("x", "yl")
N_REP, N_ROWS, N_COLS = 4, 16, 8
HELD = 2 * N_REP
I_BLOCKS = N_COLS * HELD
J_BLOCKS = N_ROWS * HELD
OWN_I = 2 * N_COLS

VMEM = pl.BlockSpec(memory_space=pltpu.VMEM)
SMEM = pl.BlockSpec(memory_space=pltpu.SMEM)


def given_to_all(shard, axes, count):
    copies = jnp.broadcast_to(shard, (count, *shard.shape))
    return lax.all_to_all(copies, axes, 0, 0, tiled=True)


def radius_terms(born_sum, intrinsic, coef_alpha, coef_beta, coef_gamma):
    scaled = intrinsic * born_sum
    poly_arg = (
        coef_alpha * scaled - coef_beta * scaled * scaled + coef_gamma * scaled * scaled * scaled
    )
    squash = jnp.tanh(poly_arg)
    radius = 1.0 / (1.0 / intrinsic - squash / (intrinsic + OFFSET))
    poly_slope = coef_alpha - 2.0 * coef_beta * scaled + 3.0 * coef_gamma * scaled * scaled
    radius_rate = (
        radius * radius * (1.0 - squash * squash) * poly_slope * intrinsic / (intrinsic + OFFSET)
    )
    return (radius, radius_rate)


def looked_up(table, types, row):
    found = jnp.zeros(types.shape, jnp.float32)
    for kind in range(table.shape[1]):
        found = jnp.where(types == float(kind), table[row, kind], found)
    return found


def folded(value):
    parts = [value[s : s + 8] for s in range(0, CHUNK, 8)]
    while len(parts) > 1:
        parts = [a + b for a, b in zip(parts[::2], parts[1::2])]
    return parts[0]


def write_mask(mask_ref):
    down = lax.broadcasted_iota(jnp.int32, (TILE, TILE), 0)
    across = lax.broadcasted_iota(jnp.int32, (TILE, TILE), 1)
    mask_ref[0] = jnp.ones((TILE, TILE), jnp.float32)
    mask_ref[1] = jnp.where(down == across, 0.0, 1.0)


def column(side_j, s, k):
    return side_j[s : s + CHUNK, k : k + 1]


def offsets(xi, yi, zi, side_j, s):
    dx = xi - column(side_j, s, 0)
    dy = yi - column(side_j, s, 1)
    dz = zi - column(side_j, s, 2)
    return dx, dy, dz, dx * dx + dy * dy + dz * dz


def born_kernel(meta, pack_i, pack_j, out_ref, acc, mask_ref):
    acc[...] = jnp.zeros_like(acc)
    write_mask(mask_ref)

    def one_list(z, _):
        def one_tile(k, _):
            ia, jb, same = meta[z, k], meta[z, SLOTS + k], meta[z, 2 * SLOTS + k]
            side_j = pack_j[jb].T
            xi, yi, zi, rho = (pack_i[ia, c : c + 1, :] for c in range(4))
            rho_sq, rho_gap = rho * rho, rho + NECK_GAP
            total = jnp.zeros((8, TILE), jnp.float32)
            for s in range(0, TILE, CHUNK):
                _, _, _, q = offsets(xi, yi, zi, side_j, s)
                base = jnp.maximum(1.0 - q * INV_SQ, 0.0)
                weight = base * base * mask_ref[same, s : s + CHUNK, :]
                soft = q + rho_sq
                gap = rho_gap + column(side_j, s, 3)
                off = q - gap * gap
                bump = jnp.exp(off * off * (-1.0 / NECK_WIDTH))
                value = column(side_j, s, 4) / (soft * soft) + column(side_j, s, 5) * bump
                total += folded(weight * value)
            acc[ia] += total
            return 0

        return lax.fori_loop(0, meta[z, 3 * SLOTS], one_tile, 0)

    lax.fori_loop(0, N_REP, one_list, 0)
    out_ref[...] = jnp.sum(acc[...], axis=1)


def pair_kernel(meta, pack_i, pack_j, rad_i, rad_j, grad_ref, direct_ref, acc, force, mask_ref):
    acc[...] = jnp.zeros_like(acc)
    force[...] = jnp.zeros_like(force)
    write_mask(mask_ref)
    own = meta[0, 3 * SLOTS + 1]

    def sweep(z, with_force):
        def one_tile(k, _):
            ia, jb, same = meta[z, k], meta[z, SLOTS + k], meta[z, 2 * SLOTS + k]
            radius_j = rad_j[0, pl.ds(jb, 1), :]
            charge_j = rad_j[1, pl.ds(jb, 1), :]
            side_j = jnp.concatenate(
                [
                    pack_j[jb, 0:3, :],
                    radius_j,
                    1.0 / radius_j,
                    charge_j,
                    charge_j * radius_j,
                    charge_j,
                ],
                axis=0,
            ).T
            xi, yi, zi = (pack_i[ia, c : c + 1, :] for c in range(3))
            radius_i = rad_i[pl.ds(ia, 1), :]
            quarter_i = 0.25 / radius_i
            total = jnp.zeros((8, TILE), jnp.float32)
            sums = [jnp.zeros((8, TILE), jnp.float32)] * 3
            for s in range(0, TILE, CHUNK):
                dx, dy, dz, q = offsets(xi, yi, zi, side_j, s)
                base = jnp.maximum(1.0 - q * INV_SQ, 0.0)
                weight = base * base * mask_ref[same, s : s + CHUNK, :]
                arg = q * (quarter_i * column(side_j, s, 4))
                decay = jnp.exp(-arg)
                inv = lax.rsqrt(q + radius_i * column(side_j, s, 3) * decay)
                weighted = weight * (inv * inv * inv)
                total += folded(weighted * (decay * (1.0 + arg) * column(side_j, s, 6)))
                if with_force:
                    slope = (-2.0 * INV_SQ) * base * inv - weighted * (0.5 - 0.125 * decay)
                    slope = slope * column(side_j, s, 5)
                    sums = [a + folded(slope * d) for a, d in zip(sums, (dx, dy, dz))]
            acc[ia] += total
            if with_force:
                at = ia // HELD * 2 + ia % 2
                for c in range(3):
                    force[at, c] += sums[c]
            return 0

        lax.fori_loop(0, meta[z, 3 * SLOTS], one_tile, 0)

    def one_list(z, _):
        @pl.when(z == own)
        def _():
            sweep(z, True)

        @pl.when(z != own)
        def _():
            sweep(z, False)

        return 0

    lax.fori_loop(0, N_REP, one_list, 0)
    grad_ref[...] = jnp.sum(acc[...], axis=1)
    direct_ref[...] = jnp.sum(force[...], axis=2)


def chain_kernel(meta, pack_i, pack_j, chain_j, out_ref, force, mask_ref):
    force[...] = jnp.zeros_like(force)
    own = meta[0, 3 * SLOTS + 1]

    def one_tile(k, _):
        ia, jb = meta[own, k], meta[own, SLOTS + k]
        rho_row = pack_j[jb, 3:4, :]
        side_j = jnp.concatenate(
            [pack_j[jb, 0:6, :], chain_j[pl.ds(jb, 1), :], rho_row * rho_row], axis=0
        ).T
        xi, yi, zi, rho, vol, neck = (pack_i[ia, c : c + 1, :] for c in range(6))
        rho_sq, rho_gap = rho * rho, rho + NECK_GAP
        sums = [jnp.zeros((8, TILE), jnp.float32)] * 6
        for s in range(0, TILE, CHUNK):
            dx, dy, dz, q = offsets(xi, yi, zi, side_j, s)
            base = jnp.maximum(1.0 - q * INV_SQ, 0.0)
            weight = base * base
            w_slope = (-2.0 * INV_SQ) * base
            gap = rho_gap + column(side_j, s, 3)
            off = q - gap * gap
            bump = jnp.exp(off * off * (-1.0 / NECK_WIDTH))
            bump_part = bump * (w_slope - weight * off * (2.0 / NECK_WIDTH))
            inv_i = 1.0 / (q + rho_sq)
            inv_j = 1.0 / (q + column(side_j, s, 7))
            slope_ij = column(side_j, s, 4) * (inv_i * inv_i) * (
                w_slope - 2.0 * weight * inv_i
            ) + column(side_j, s, 5) * bump_part
            slope_ji = vol * (inv_j * inv_j) * (w_slope - 2.0 * weight * inv_j) + neck * bump_part
            slope_ji = slope_ji * column(side_j, s, 6)
            parts = [slope_ji * d for d in (dx, dy, dz)] + [slope_ij * d for d in (dx, dy, dz)]
            sums = [a + folded(v) for a, v in zip(sums, parts)]
        at = ia // HELD * 2 + ia % 2
        for c in range(6):
            force[at, c] += sums[c]
        return 0

    lax.fori_loop(0, meta[own, 3 * SLOTS], one_tile, 0)
    out_ref[...] = jnp.sum(force[...], axis=2)


def called(kernel, shapes, scratch, *args):
    return pl.pallas_call(
        kernel,
        out_shape=[jax.ShapeDtypeStruct(s, jnp.float32) for s in shapes],
        in_specs=[SMEM] + [VMEM] * (len(args) - 1),
        out_specs=[VMEM] * len(shapes),
        scratch_shapes=[pltpu.VMEM(s, jnp.float32) for s in scratch]
        + [pltpu.VMEM((2, TILE, TILE), jnp.float32)],
        compiler_params=pltpu.CompilerParams(vmem_limit_bytes=32 * 1024 * 1024),
    )(*args)


def packed(blocks, table):
    types = blocks[:, 3:4, :]
    rho = looked_up(table, types, 0)
    scale = looked_up(table, types, 1)
    neck = looked_up(table, types, 2)
    fill = jnp.zeros(types.shape, jnp.float32)
    return jnp.concatenate(
        [blocks[:, 0:3, :], rho, scale * rho * rho * rho, neck, types, fill], axis=1
    )


def body(positions, velocities, old_forces, charges, atom_types, table, tile_pairs):
    rep_at = lax.axis_index(REP)
    row_at = lax.axis_index(ROWS)
    col_at = lax.axis_index(COLS)
    kinds = atom_types.astype(jnp.float32)
    atom_mass = looked_up(table, kinds, 6)
    new_positions = (
        positions + TIMESTEP * velocities + TIMESTEP * TIMESTEP / (2.0 * atom_mass) * old_forces
    )

    atoms = jnp.concatenate([new_positions, kinds[None, :]], axis=0)
    atoms = jnp.moveaxis(atoms.reshape(4, 2, TILE), 1, 0)
    listed = jnp.pad(tile_pairs.reshape(1, 2 * SLOTS).astype(jnp.float32), ((0, 1), (0, 64)))
    extra = jnp.concatenate([listed, charges.reshape(2, TILE)], axis=0)
    sent = jnp.concatenate([atoms, extra[None]], axis=0)
    held = given_to_all(sent, REP, N_REP)
    held_atoms = held[:, 0:2].reshape(HELD, 4, TILE)
    held_charges = held[:, 2, 2:4].reshape(HELD, TILE)
    lists = held[:, 2, 0, 0 : 2 * SLOTS].astype(jnp.int32)

    list_a, list_g = lists[:, :SLOTS], lists[:, SLOTS:]
    reps = jnp.arange(N_REP, dtype=jnp.int32)[:, None]
    live = jnp.sum((list_a >= 0).astype(jnp.int32), axis=1, keepdims=True)
    block_a, block_g = jnp.maximum(list_a, 0), jnp.maximum(list_g, 0)
    j_row = block_g // 2
    place_i = (block_a // 2 * N_REP + reps) * 2 + block_a % 2
    place_j = (j_row % N_ROWS * N_REP + j_row // N_ROWS) * 2 + block_g % 2
    same = (j_row == reps * N_ROWS + row_at) & (block_a == col_at * 2 + block_g % 2)
    tail = jnp.broadcast_to(rep_at, (N_REP, 1)).astype(jnp.int32)
    meta = jnp.concatenate([place_i, place_j, same.astype(jnp.int32), live, tail], axis=1)

    side_i = given_to_all(held_atoms, COLS, N_COLS).reshape(I_BLOCKS, 4, TILE)
    side_j = given_to_all(held_atoms, ROWS, N_ROWS).reshape(J_BLOCKS, 4, TILE)
    pack_i, pack_j = packed(side_i, table), packed(side_j, table)

    [born_part] = called(
        born_kernel, [(I_BLOCKS, TILE)], [(I_BLOCKS, 8, TILE)], meta, pack_i, pack_j
    )
    both = given_to_all(jnp.concatenate([born_part, held_charges]), COLS, N_COLS)
    born_all = jnp.sum(both[:, :I_BLOCKS], axis=0)
    charge_i = both[:, I_BLOCKS:].reshape(I_BLOCKS, TILE)
    types_i = pack_i[:, 6]
    radius_i, rate_i = radius_terms(
        born_all, pack_i[:, 3], *(looked_up(table, types_i, r) for r in (3, 4, 5))
    )
    radius_held = lax.dynamic_slice_in_dim(radius_i, col_at * HELD, HELD)
    rate_held = lax.dynamic_slice_in_dim(rate_i, col_at * HELD, HELD)
    rad_j = given_to_all(jnp.stack([radius_held, held_charges]), ROWS, N_ROWS)
    rad_j = jnp.moveaxis(rad_j, 1, 0).reshape(2, J_BLOCKS, TILE)

    grad_part, direct_part = called(
        pair_kernel,
        [(I_BLOCKS, TILE), (OWN_I, 3, TILE)],
        [(I_BLOCKS, 8, TILE), (OWN_I, 3, 8, TILE)],
        meta,
        pack_i,
        pack_j,
        radius_i,
        rad_j,
    )
    grads = lax.all_to_all(
        grad_part.reshape(N_COLS, HELD, TILE), COLS, 0, 0, tiled=True
    )
    grad_held = -0.5 * held_charges * jnp.sum(grads, axis=0)
    chain_held = (
        COULOMB * held_charges * held_charges / (2.0 * radius_held * radius_held)
        - COULOMB * grad_held
    ) * rate_held
    chain_j = given_to_all(chain_held, ROWS, N_ROWS).reshape(J_BLOCKS, TILE)

    [chain_part] = called(
        chain_kernel, [(OWN_I, 6, TILE)], [(OWN_I, 6, 8, TILE)], meta, pack_i, pack_j, chain_j
    )
    shared = jnp.concatenate([direct_part, chain_part], axis=1).reshape(N_COLS, 2, 9, TILE)
    sums = jnp.sum(lax.all_to_all(shared, COLS, 0, 0, tiled=True), axis=0)
    sums = jnp.moveaxis(sums, 0, 1).reshape(3, 3, 2 * TILE)
    chain_own = lax.dynamic_slice_in_dim(chain_held, rep_at * 2, 2).reshape(1, 2 * TILE)
    new_forces = (2.0 * COULOMB) * charges * sums[0] - 2.0 * (sums[1] + chain_own * sums[2])
    new_velocities = velocities + TIMESTEP / (2.0 * atom_mass) * (old_forces + new_forces)
    return (new_positions, new_velocities, new_forces)


def solution(mesh):
    split = Mesh(mesh.devices.reshape(SIZES), AXES)
    rows, cols = AXES[:4], AXES[4:]
    return jax.shard_map(
        body,
        mesh=split,
        in_specs=(
            P(None, AXES),
            P(None, AXES),
            P(None, AXES),
            P(AXES),
            P(AXES),
            P(),
            P(rows, cols, None, None),
        ),
        out_specs=(P(None, AXES), P(None, AXES), P(None, AXES)),
        check_vma=False,
    )
```

time: 213 us -> 224 us (1.052)
  waiting for transfers between devices: 79.7 us -> 33.6 us
  other arithmetic: 11 us -> 52 us
  Pallas kernels: 0 us -> 22.3 us
  blocking collectives: 26.3 us -> 15.5 us
  starting transfers between devices: 77.1 us -> 86.9 us
  local copies, waits for them, and re-layouts: 13.4 us -> 10.8 us
    all_to_all x6 -> x7, waiting for transfers between devices: 79.7 us -> 33.6 us  [the longest x5 23.5 us: given_to_all(): return lax.all_to_all(copies, axes, 0, 0, tiled=True)]
    pallas_call x0 -> x3, Pallas kernels: none -> 22.3 us  [called(): pl.pallas_call(kernel, out_shape=[jax.ShapeDtypeStruct(s, jnp.float32) fo...]
    select_n x18 -> x3, other arithmetic: 0.9 us -> 15.4 us  [looked_up(): found = jnp.where(types == float(kind), table[row, kind], found)]
    mul x16 -> x4, other arithmetic: 2.54 us -> 15.7 us  [the longest x2 15.7 us: packed(): scale * rho * rho * rho]
    all_to_all x1, blocking collectives: 26.3 us -> 15.5 us  [given_to_all(): return lax.all_to_all(copies, axes, 0, 0, tiled=True)]
    div x2 -> x1, other arithmetic: 0.03 us -> 9.92 us  [radius_terms(): radius = 1.0 / (1.0 / intrinsic - squash / (intrinsic + OFFSET))]
    all_to_all x6 -> x7, starting transfers between devices: 77.1 us -> 86.9 us  [the longest x5 54.2 us: given_to_all(): return lax.all_to_all(copies, axes, 0, 0, tiled=True)]
    gather x12 -> x0, local copies, waits for them, and re-layouts: 6.61 us -> none  [the longest x6 3.3 us: one_turn(): side_i = jnp.moveaxis(jnp.take(pack_i, group_i, axis=1), 1, 0)]
  transfers between devices with their start and end apart: 6 -> 7, of which waited for: 6 -> 5; matrix products, arithmetic and copies ran while one was open for 0% -> 10% of each run, Pallas kernels for 0% -> 0%
where the time goes in v1:
time: 224 us; the launch traced here: 222 us
  starting transfers between devices  86.9 us (39%)
  other arithmetic  52 us (23%)
  waiting for transfers between devices  33.6 us (15%)
  Pallas kernels  22.3 us (10%)
  blocking collectives  15.5 us (7%)
  local copies, waits for them, and re-layouts  10.8 us (5%)
    all_to_all x5, starting transfers between devices, given_to_all(): return lax.all_to_all(copies, axes, 0, 0, tiled=True)  54.2 us
    all_to_all x5, waiting for transfers between devices, given_to_all(): return lax.all_to_all(copies, axes, 0, 0, tiled=True)  23.5 us
    all_to_all x1, starting transfers between devices, body(): lax.all_to_all(grad_part.reshape(N_COLS, HELD, TILE), COLS, 0, 0, tiled=T...  23 us
    pallas_call x3, Pallas kernels, called(): pl.pallas_call(kernel, out_shape=[jax.ShapeDtypeStruct(s, jnp.float32) fo...  22.3 us
    mul x2, other arithmetic, packed(): scale * rho * rho * rho  15.7 us
    all_to_all x1, blocking collectives, given_to_all(): return lax.all_to_all(copies, axes, 0, 0, tiled=True)  15.5 us
    select_n x3, other arithmetic, looked_up(): found = jnp.where(types == float(kind), table[row, kind], found)  15.4 us
    div x1, other arithmetic, radius_terms(): radius = 1.0 / (1.0 / intrinsic - squash / (intrinsic + OFFSET))  9.92 us
  transfers between devices with their start and end apart: 7, of which 5 were waited for; matrix products, arithmetic and copies ran while one was open for 10% of the time, Pallas kernels for 0%

profile of v1, /device:TPU:1, one launch (start us, length us, event | category | flops | bytes accessed | tf_op | source)
XLA Modules:
  0.0 222.1 jit_solution(17561815101213414076)
XLA Ops:
  0.6 2.0 fusion.39
  2.7 0.0 copy-start.3
  2.7 0.0 copy-start.4
  2.7 5.0 %broadcast_divide_fusion = (f32[256]{0:T(256)S(1)}, f32[256]{0:T(256)S(1)}) fusion(f32[]{:T(128)} %bitcast.7, f32[]{:T(128)} %bitcast.6, f32[]{:T(128)} %bitcast.5, f32[]{:T(128)} %bitcast.4, f32[]{:T(128)} %bitcast.3, f32[]{:T(128)} %bitcast.2, f32[]{:T(128)} %bitcast.1, f32[]{:T(128)} %bitcast, s32[256]{0:T(256)S(1)} %copy-done.5), kind=kLoop, calls=%fused_computation.123 | loop fusion | flops 4864 | bytes 3104 | tf_op jit(solution)/shard_map/div | solution.py:323
  7.7 0.0 copy-start.2
  7.8 0.1 convert_element_type.33
  7.9 0.6 copy-done.2
  8.4 0.6 copy-done.1
  9.0 0.7 copy-done.6
  9.7 0.6 broadcast_in_dim.285
  10.3 15.8 %all-to-all-start = ((f32[4,3,4,128]{3,2,1,0:T(4,128)}), f32[4,3,4,128]{3,2,1,0:T(4,128)S(1)}, u32[]{:S(2)}, u32[]{:S(2)}) async-start(f32[4,3,4,128]{3,2,1,0:T(4,128)} %broadcast_in_dim.285), calls=%async_computation | async-start | bytes 49152 | tf_op jit(solution)/shard_map/all_to_all | solution.py:38
  26.1 0.7 fusion.38
  26.8 10.7 %all-to-all-done = f32[4,3,4,128]{3,2,1,0:T(4,128)S(1)} async-done(((f32[4,3,4,128]{3,2,1,0:T(4,128)}), f32[4,3,4,128]{3,2,1,0:T(4,128)S(1)}, u32[]{:S(2)}, u32[]{:S(2)}) %all-to-all-start) | async-done | bytes 24608 | tf_op jit(solution)/shard_map/all_to_all | solution.py:38
  37.6 0.7 broadcast_in_dim.288
  38.3 5.0 %all-to-all-start.1 = ((f32[8,8,4,128]{3,1,2,0:T(8,128)}), f32[8,8,4,128]{3,1,2,0:T(8,128)S(1)}, u32[]{:S(2)}, u32[]{:S(2)}) async-start(f32[8,8,4,128]{3,1,2,0:T(8,128)} %broadcast_in_dim.288), calls=%async_computation.1 | async-start | bytes 262144 | tf_op jit(solution)/shard_map/all_to_all | solution.py:38
  43.3 5.2 %all-to-all-done.1 = f32[8,8,4,128]{3,1,2,0:T(8,128)S(1)} async-done(((f32[8,8,4,128]{3,1,2,0:T(8,128)}), f32[8,8,4,128]{3,1,2,0:T(8,128)S(1)}, u32[]{:S(2)}, u32[]{:S(2)}) %all-to-all-start.1) | async-done | bytes 131104 | tf_op jit(solution)/shard_map/all_to_all | solution.py:38
  48.6 0.7 broadcast_in_dim.313
  49.3 9.1 %all-to-all-start.2 = ((f32[16,8,4,128]{3,2,1,0:T(4,128)}), f32[16,8,4,128]{3,2,1,0:T(4,128)S(1)}, u32[]{:S(2)}, u32[]{:S(2)}) async-start(f32[16,8,4,128]{3,2,1,0:T(4,128)} %broadcast_in_dim.313), calls=%async_computation.2 | async-start | bytes 524288 | tf_op jit(solution)/shard_map/all_to_all | solution.py:38
  58.4 0.1 convert_reduce_fusion
  58.6 0.1 copy.88
  58.7 0.1 fusion.30
  58.8 0.1 concatenate.34.meta
  58.9 0.1 copy.95
  59.0 5.0 %broadcast_add_fusion = (f32[64,128]{1,0:T(8,128)S(1)}, f32[64,1,128]{2,0,1:T(8,128)S(1)}, pred[64,1,128]{2,0,1:T(8,128)(4,1)S(1)}, pred[64,1,128]{2,0,1:T(8,128...) fusion(f32[64,1,128]{2,0,1:T(8,128)S(1)} %bitcast.135, ...), kind=kLoop, calls=%fused_computation.38 | loop fusion | flops 139264 | bytes 196640 | tf_op jit(solution)/shard_map/add | solution.py:47
  64.1 4.9 %select_select_fusion.3 = f32[64,1,128]{2,0,1:T(8,128)S(1)} fusion(pred[64,1,128]{2,0,1:T(8,128)(4,1)S(1)} %get-tuple-element.25, pred[64,1,128]{2,0,1:T(8,128)(4,1)S(1)} %get-tuple-element.24, pred[64,1,128]{2,0,1:T(8,128)(4,1)S(1)} %get-tuple-element.23, pred[64,1,128]{2,0,1:T(8,128)(4,1)S(1)} %get-tuple-element.22, ...), kind=kLoop, calls=%fused_computation.34 | loop fusion | flops 65536 | bytes 131104 | tf_op jit(solution)/shard_map/jit(_where)/select_n | solution.py:58
  69.0 5.1 %multiply_multiply_fusion.3 = f32[64,1,128]{2,0,1:T(8,128)S(1)} fusion(f32[64,1,128]{2,0,1:T(8,128)S(1)} %get-tuple-element.17, pred[64,1,128]{2,0,1:T(8,128)(4,1)S(1)} %get-tuple-element.25, pred[64,1,128]{2,0,1:T(8,128)(4,1)S(1)} %get-tuple-element.24, pred[64,1,128]{2,0,1:T(8,128)(4,1)S(1)} %get-tuple-element.23, ...), kind=kLoop, calls=%fused_computation.17 | loop fusion | flops 90112 | bytes 163872 | tf_op jit(solution)/shard_map/mul | solution.py:241
  74.1 0.3 concatenate.35.pack_i
  74.4 10.6 %multiply_multiply_fusion = (f32[128,1,128]{2,1,0:T(1,128)S(1)}, f32[128,1,128]{2,1,0:T(1,128)S(1)}, f32[128,1,128]{2,1,0:T(1,128)S(1)}) fusion(f32[]{:T(128)} %bitcast.34, f32[]{:T(128)} %bitcast.33, f32[]{:T(128)} %bitcast.32, f32[]{:T(128)} %bitcast.31, f32[]{:T(128)} %bitcast.30, f32[]{:T(128)} %bitcast.29, f32[]{:T(128)} %bitcast.28, f32[]{:T(128)} %bitcast.27, ...), kind=kLoop, calls=%fused_computation.12 | loop fusion | flops 442368 | bytes 262208 | tf_op jit(solution)/shard_map/mul | solution.py:241
  85.0 5.2 %select_select_fusion = f32[128,1,128]{2,1,0:T(1,128)S(1)} fusion(f32[]{:T(128)} %bitcast.43, f32[]{:T(128)} %bitcast.42, f32[]{:T(128)} %bitcast.41, f32[]{:T(128)} %bitcast.40, f32[]{:T(128)} %bitcast.39, f32[]{:T(128)} %bitcast.38, f32[]{:T(128)} %bitcast.37, f32[]{:T(128)} %bitcast.36, f32[128,4,128]{2,1,0:T(4,128)S(1)} %bitcast.133), kind=kLoop, calls=%fused_computation.13 | loop fusion | flops 262144 | bytes 131104 | tf_op jit(solution)/shard_map/jit(_where)/select_n | solution.py:58
  90.2 0.7 concatenate.36.pack_j
  90.9 8.8 %shard_map.94 = f32[64,128]{1,0:T(8,128)S(1)} custom-call(s32[4,98]{1,0:T(4,128)S(1)} %concatenate.34.meta, f32[64,8,128]{2,1,0:T(8,128)S(1)} %concatenate.35.pack_i, f32[128,8,128]{2,1,0:T(8,128)S(1)} %concatenate.36.pack_j), custom_call_target="tpu_custom_call" | custom-call | tf_op jit(solution)/shard_map/pallas_call | solution.py:223
  99.7 0.7 broadcast_in_dim.346
  100.5 20.9 %all-to-all-start.3 = ((f32[8,72,128]{2,1,0:T(8,128)}), f32[8,72,128]{2,1,0:T(8,128)S(1)}, u32[]{:S(2)}, u32[]{:S(2)}) async-start(f32[8,72,128]{2,1,0:T(8,128)} %broadcast_in_dim.346), calls=%async_computation.3 | async-start | bytes 589824 | tf_op jit(solution)/shard_map/all_to_all | solution.py:38
  121.3 0.7 fusion.37
  122.0 5.3 %copy_select_fusion = f32[64,1,128]{2,1,0:T(1,128)S(1)} fusion(pred[64,1,128]{2,0,1:T(8,128)(4,1)S(1)} %get-tuple-element.25, pred[64,1,128]{2,0,1:T(8,128)(4,1)S(1)} %get-tuple-element.24, pred[64,1,128]{2,0,1:T(8,128)(4,1)S(1)} %get-tuple-element.18, pred[64,1,128]{2,0,1:T(8,128)(4,1)S(1)} %get-tuple-element.19, ...), kind=kLoop, calls=%fused_computation.4 | loop fusion | flops 65536 | bytes 98336 | tf_op jit(solution)/shard_map/jit(_where)/select_n | solution.py:58
  127.3 9.9 %subtract_divide_fusion = (f32[64,128]{1,0:T(8,128)S(1)}, f32[64,128]{1,0:T(8,128)S(1)}, f32[64,128]{1,0:T(8,128)S(1)}, f32[64,1,128]{2,0,1:T(8,128)S(1)}, f32[64,128]{1,0:T(8,128)S(1)}) fusion(f32[64,1,128]{2,0,1:T(8,128)S(1)} %get-tuple-element.17, f32[64,128]{1,0:T(8,128)S(1)} %bitcast.145, f32[64,128]{1,0:T(8,128)S(1)} %slice_reduce_fusion, ...), kind=kLoop, calls=%fused_computation.25 | loop fusion | flops 245760 | bytes 360512 | tf_op jit(solution)/shard_map/div | solution.py:47
  137.3 15.5 %all_to_all.40 = f32[16,2,8,128]{3,2,1,0:T(8,128)S(1)} all-to-all(f32[16,2,8,128]{3,2,1,0:T(8,128)S(1)} %broadcast_in_dim.363), channel_id=1, replica_groups=mesh['zh'=4,'zl'=4,'yh'=2,'core'=2,'x'=4,'yl'=2] {'zl','yh','core'}, dimensions={0} | all-to-all | bytes 262144 | tf_op jit(solution)/shard_map/all_to_all | solution.py:38
  152.9 9.9 %shard_map.95 = (f32[64,128]{1,0:T(8,128)}, f32[16,3,128]{2,1,0:T(4,128)S(1)}) custom-call(s32[4,98]{1,0:T(4,128)S(1)} %concatenate.34.meta, f32[64,8,128]{2,1,0:T(8,128)S(1)} %concatenate.35.pack_i, f32[128,8,128]{2,1,0:T(8,128)S(1)} %concatenate.36.pack_j, f32[64,128]{1,0:T(8,128)S(1)} %get-tuple-element.11.rad_i, f32[2,128,128]{2,1,0:T(8,128)S(1)} %copy_bitcast_fusion.rad_j), custom_call_target="tpu_custom_call" | custom-call | tf_op jit(solution)/shard_map/pallas_call | solution.py:223
  162.8 23.0 %all-to-all-start.5 = ((f32[8,8,128]{2,1,0:T(8,128)}), f32[8,8,128]{2,1,0:T(8,128)S(1)}, u32[]{:S(2)}, u32[]{:S(2)}) async-start(f32[8,8,128]{2,1,0:T(8,128)} %bitcast.80), calls=%async_computation.5 | async-start | bytes 65536 | tf_op jit(solution)/shard_map/all_to_all | solution.py:305
  185.8 5.1 %all-to-all-done.5 = f32[8,8,128]{2,1,0:T(8,128)S(1)} async-done(((f32[8,8,128]{2,1,0:T(8,128)}), f32[8,8,128]{2,1,0:T(8,128)S(1)}, u32[]{:S(2)}, u32[]{:S(2)}) %all-to-all-start.5) | async-done | bytes 32800 | tf_op jit(solution)/shard_map/all_to_all | solution.py:305
  190.8 0.6 broadcast_in_dim.364
  191.5 3.4 %all-to-all-start.6 = ((f32[16,8,128]{2,1,0:T(8,128)}), f32[16,8,128]{2,1,0:T(8,128)S(1)}, u32[]{:S(2)}, u32[]{:S(2)}) async-start(f32[16,8,128]{2,1,0:T(8,128)} %broadcast_in_dim.364), calls=%async_computation.6 | async-start | bytes 131072 | tf_op jit(solution)/shard_map/all_to_all | solution.py:38
  194.9 7.5 %all-to-all-done.6 = f32[16,8,128]{2,1,0:T(8,128)S(1)} async-done(((f32[16,8,128]{2,1,0:T(8,128)}), f32[16,8,128]{2,1,0:T(8,128)S(1)}, u32[]{:S(2)}, u32[]{:S(2)}) %all-to-all-start.6) | async-done | bytes 65568 | tf_op jit(solution)/shard_map/all_to_all | solution.py:38
  202.4 3.6 %shard_map.96 = f32[16,6,128]{2,1,0:T(8,128)S(1)} custom-call(s32[4,98]{1,0:T(4,128)S(1)} %concatenate.34.meta, f32[64,8,128]{2,1,0:T(8,128)S(1)} %concatenate.35.pack_i, f32[128,8,128]{2,1,0:T(8,128)S(1)} %concatenate.36.pack_j, f32[128,128]{1,0:T(8,128)S(1)} %bitcast.131), custom_call_target="tpu_custom_call" | custom-call | tf_op jit(solution)/shard_map/pallas_call | solution.py:223
  206.0 0.7 copy.112
  206.6 9.7 %all-to-all-start.7 = ((f32[8,2,9,128]{3,1,2,0:T(2,128)}), f32[8,2,9,128]{3,1,2,0:T(2,128)S(1)}, u32[]{:S(2)}, u32[]{:S(2)}) async-start(f32[8,2,9,128]{3,1,2,0:T(2,128)} %copy.112), calls=%async_computation.7 | async-start | bytes 147456 | tf_op jit(solution)/shard_map/all_to_all | solution.py:319
  216.4 5.1 %all-to-all-done.7 = f32[8,2,9,128]{3,1,2,0:T(2,128)S(1)} async-done(((f32[8,2,9,128]{3,1,2,0:T(2,128)}), f32[8,2,9,128]{3,1,2,0:T(2,128)S(1)}, u32[]{:S(2)}, u32[]{:S(2)}) %all-to-all-start.7) | async-done | bytes 73760 | tf_op jit(solution)/shard_map/all_to_all | solution.py:319
  221.5 0.6 multiply_add_fusion
  (46 shorter events, 0.3 us)
Async XLA Ops:
  0.6 2.1 copy-start.5
  2.7 5.1 %copy-start.7 = (s32[1,1,2,32]{3,2,1,0:T(2,128)S(1)}, s32[1,1,2,32]{3,2,1,0:T(2,128)}, u32[]{:S(2)}) copy-start(s32[1,1,2,32]{3,2,1,0:T(2,128)} %param.13) | copy-start | bytes 772
  2.7 5.2 %copy-start.3 = (f32[3,256]{1,0:T(4,128)S(1)}, f32[3,256]{1,0:T(4,128)}, u32[]{:S(2)}) copy-start(f32[3,256]{1,0:T(4,128)} %param.8) | copy-start | bytes 9220
  2.7 5.1 %copy-start.4 = (f32[3,256]{1,0:T(4,128)S(1)}, f32[3,256]{1,0:T(4,128)}, u32[]{:S(2)}) copy-start(f32[3,256]{1,0:T(4,128)} %param.7) | copy-start | bytes 9220
  7.7 0.7 copy-start.2
  8.4 0.6 copy-start.1
  9.0 0.7 copy-start.6
  10.3 15.8 %copy-start = (f32[7,8]{1,0:T(8,128)S(1)}, f32[7,8]{1,0:T(8,128)}, u32[]{:S(2)}) copy-start(f32[7,8]{1,0:T(8,128)} %param.12) | copy-start | bytes 676
  10.3 27.2 %all-to-all-start = ((f32[4,3,4,128]{3,2,1,0:T(4,128)}), f32[4,3,4,128]{3,2,1,0:T(4,128)S(1)}, u32[]{:S(2)}, u32[]{:S(2)}) async-start(f32[4,3,4,128]{3,2,1,0:T(4,128)} %broadcast_in_dim.285), calls=%async_computation | async-start | bytes 49152 | tf_op jit(solution)/shard_map/all_to_all | solution.py:38
  38.3 10.3 %all-to-all-start.1 = ((f32[8,8,4,128]{3,1,2,0:T(8,128)}), f32[8,8,4,128]{3,1,2,0:T(8,128)S(1)}, u32[]{:S(2)}, u32[]{:S(2)}) async-start(f32[8,8,4,128]{3,1,2,0:T(8,128)} %broadcast_in_dim.288), calls=%async_computation.1 | async-start | bytes 262144 | tf_op jit(solution)/shard_map/all_to_all | solution.py:38
  49.3 25.1 %all-to-all-start.2 = ((f32[16,8,4,128]{3,2,1,0:T(4,128)}), f32[16,8,4,128]{3,2,1,0:T(4,128)S(1)}, u32[]{:S(2)}, u32[]{:S(2)}) async-start(f32[16,8,4,128]{3,2,1,0:T(4,128)} %broadcast_in_dim.313), calls=%async_computation.2 | async-start | bytes 524288 | tf_op jit(solution)/shard_map/all_to_all | solution.py:38
  100.5 26.8 %all-to-all-start.3 = ((f32[8,72,128]{2,1,0:T(8,128)}), f32[8,72,128]{2,1,0:T(8,128)S(1)}, u32[]{:S(2)}, u32[]{:S(2)}) async-start(f32[8,72,128]{2,1,0:T(8,128)} %broadcast_in_dim.346), calls=%async_computation.3 | async-start | bytes 589824 | tf_op jit(solution)/shard_map/all_to_all | solution.py:38
  162.8 28.0 %all-to-all-start.5 = ((f32[8,8,128]{2,1,0:T(8,128)}), f32[8,8,128]{2,1,0:T(8,128)S(1)}, u32[]{:S(2)}, u32[]{:S(2)}) async-start(f32[8,8,128]{2,1,0:T(8,128)} %bitcast.80), calls=%async_computation.5 | async-start | bytes 65536 | tf_op jit(solution)/shard_map/all_to_all | solution.py:305
  191.5 10.9 %all-to-all-start.6 = ((f32[16,8,128]{2,1,0:T(8,128)}), f32[16,8,128]{2,1,0:T(8,128)S(1)}, u32[]{:S(2)}, u32[]{:S(2)}) async-start(f32[16,8,128]{2,1,0:T(8,128)} %broadcast_in_dim.364), calls=%async_computation.6 | async-start | bytes 131072 | tf_op jit(solution)/shard_map/all_to_all | solution.py:38
  206.6 14.8 %all-to-all-start.7 = ((f32[8,2,9,128]{3,1,2,0:T(2,128)}), f32[8,2,9,128]{3,1,2,0:T(2,128)S(1)}, u32[]{:S(2)}, u32[]{:S(2)}) async-start(f32[8,2,9,128]{3,1,2,0:T(2,128)} %copy.112), calls=%async_computation.7 | async-start | bytes 147456 | tf_op jit(solution)/shard_map/all_to_all | solution.py:319

commit v2 on v1

v2 whole, which is shorter than its diff:
```python
import jax
import jax.numpy as jnp
from jax import lax
from jax.experimental import pallas as pl
from jax.experimental.pallas import tpu as pltpu
from jax.sharding import Mesh
from jax.sharding import PartitionSpec as P

TILE = 128
SLOTS = 32
CHUNK = 32
UNROLL = 4
LISTED = 128

CUTOFF = 12.0
COULOMB = 32.0
TIMESTEP = 0.5
OFFSET = 0.09
NECK_GAP = 0.5
NECK_WIDTH = 16.0
INV_SQ = 1.0 / (CUTOFF * CUTOFF)
LOG2E = 1.4426950408889634

AXES = ("zh", "zl", "yh", "core", "x", "yl")
SIZES = (4, 4, 2, 2, 4, 2)
REP = ("zh",)
ROWS = ("zl", "yh", "core")
COLS = ("x", "yl")
N_REP, N_ROWS, N_COLS = 4, 16, 8
HELD = 2 * N_REP
I_BLOCKS = N_COLS * HELD
J_BLOCKS = N_ROWS * HELD
OWN_I = 2 * N_COLS

VMEM = pl.BlockSpec(memory_space=pltpu.VMEM)
SMEM = pl.BlockSpec(memory_space=pltpu.SMEM)
F32 = jnp.float32


def given_to_all(shard, axes, count):
    copies = jnp.broadcast_to(shard, (count, *shard.shape))
    return lax.all_to_all(copies, axes, 0, 0, tiled=True)


def exchanged(pieces, axes):
    return lax.all_to_all(pieces, axes, 0, 0, tiled=True)


def called(kernel, outs, scratch, smem, vmem):
    return pl.pallas_call(
        kernel,
        out_shape=[jax.ShapeDtypeStruct(s, F32) for s in outs],
        in_specs=[SMEM] * len(smem) + [VMEM] * len(vmem),
        out_specs=[VMEM] * len(outs),
        scratch_shapes=[pltpu.VMEM(s, t) for s, t in scratch],
        compiler_params=pltpu.CompilerParams(vmem_limit_bytes=32 * 1024 * 1024),
    )(*smem, *vmem)


def looked_up(table, types, rows):
    found = [jnp.zeros(types.shape, F32) for _ in rows]
    for kind in range(8):
        here = types == float(kind)
        found = [jnp.where(here, table[r, kind], f) for r, f in zip(rows, found)]
    return found


def folded(value):
    parts = [value[s : s + 8] for s in range(0, CHUNK, 8)]
    while len(parts) > 1:
        parts = [a + b for a, b in zip(parts[::2], parts[1::2])]
    return parts[0]


def write_mask(mask_ref):
    down = lax.broadcasted_iota(jnp.int32, (TILE, TILE), 0)
    across = lax.broadcasted_iota(jnp.int32, (TILE, TILE), 1)
    mask_ref[0] = jnp.ones((TILE, TILE), F32)
    mask_ref[1] = jnp.where(down == across, 0.0, 1.0)


def write_spread(spread_ref):
    row = lax.broadcasted_iota(jnp.int32, spread_ref.shape, 0)
    lane = lax.broadcasted_iota(jnp.int32, spread_ref.shape, 1)
    hit = (row % 8 == lane // TILE) & (row < 24)
    spread_ref[...] = jnp.where(hit, 1.0, 0.0).astype(jnp.bfloat16)


def columns(rows, spread_ref, count):
    high = rows.astype(jnp.bfloat16).astype(F32)
    rest = rows - high
    middle = rest.astype(jnp.bfloat16).astype(F32)
    parts = jnp.concatenate([high, middle, rest - middle, jnp.zeros_like(rows)], axis=0)
    spread = lax.dot_general(
        parts.astype(jnp.bfloat16),
        spread_ref[...],
        (((0,), (0,)), ((), ())),
        preferred_element_type=F32,
    )
    return lambda s, c: spread[s : s + CHUNK, c * TILE : (c + 1) * TILE]


def offsets(xi, yi, zi, col, s):
    dx = xi - col(s, 0)
    dy = yi - col(s, 1)
    dz = zi - col(s, 2)
    return dx, dy, dz, dx * dx + dy * dy + dz * dz


def decoded(code):
    return code >> 8, (code >> 1) & 127, code & 1


def for_each_tile(meta, first, count, one_tile):
    def step(k, _):
        for add in [
            one_tile(*decoded(meta[first + k * UNROLL + u])) for u in range(UNROLL)
        ]:
            add()
        return 0

    lax.fori_loop(0, (count + UNROLL - 1) // UNROLL, step, 0)


def first_kernel(table, pos, vel, old, charge, kinds, pairs, new_ref, sent_ref, scale_ref):
    types = kinds[...].astype(F32)
    [mass] = looked_up(table, types, (6,))
    new = pos[...] + TIMESTEP * vel[...] + TIMESTEP * TIMESTEP / (2.0 * mass) * old[...]
    new_ref[...] = new
    scale_ref[...] = TIMESTEP / (2.0 * mass)
    lists = pairs[...].astype(F32)
    lists = jnp.concatenate([lists, jnp.zeros((2, TILE - SLOTS), F32)], axis=1)
    for n in range(N_REP):
        for b in range(2):
            here = slice(b * TILE, (b + 1) * TILE)
            sent_ref[n, b, 0:3, :] = new[:, here]
            sent_ref[n, b, 3:4, :] = types[:, here]
            sent_ref[n, 2, 2 + b : 3 + b, :] = charge[:, here]
        sent_ref[n, 2, 0:2, :] = lists


def born_kernel(
    meta, table, side_i, side_j, out_ref, pack_i, pack_j, acc, mask_ref, spread_ref
):
    acc[...] = jnp.zeros_like(acc)
    write_mask(mask_ref)
    write_spread(spread_ref)
    for side, pack, blocks in ((side_i, pack_i, I_BLOCKS), (side_j, pack_j, J_BLOCKS)):
        types = side[:, 3, :]
        rho, scale, neck = looked_up(table, types, (0, 1, 2))
        pack[0:blocks, 0:3, :] = side[:, 0:3, :]
        pack[0:blocks, 3, :] = rho
        pack[0:blocks, 4, :] = scale * rho * rho * rho
        pack[0:blocks, 5, :] = neck
        pack[0:blocks, 6, :] = types
        pack[0:blocks, 7, :] = types
    pack_i[I_BLOCKS] = jnp.ones((8, TILE), F32)

    def one_tile(ia, jb, same):
        col = columns(pack_j[jb], spread_ref, 6)
        xi, yi, zi, rho = (pack_i[ia, c : c + 1, :] for c in range(4))
        rho_sq, rho_gap = rho * rho, rho + NECK_GAP
        total = jnp.zeros((8, TILE), F32)
        for s in range(0, TILE, CHUNK):
            _, _, _, q = offsets(xi, yi, zi, col, s)
            base = jnp.maximum(1.0 - q * INV_SQ, 0.0)
            weight = base * base * mask_ref[same, s : s + CHUNK, :]
            inv = 1.0 / (q + rho_sq)
            gap = rho_gap + col(s, 3)
            off = q - gap * gap
            bump = jnp.exp2(off * off * (-LOG2E / NECK_WIDTH))
            total += folded(weight * (col(s, 4) * (inv * inv) + col(s, 5) * bump))

        def add():
            acc[ia] += total

        return add

    for_each_tile(meta, 0, meta[LISTED], one_tile)
    for_each_tile(meta, SLOTS, meta[LISTED + 1], one_tile)
    born = jnp.sum(acc[0:I_BLOCKS], axis=1)
    for n in range(N_COLS):
        out_ref[n] = born


def radius_kernel(meta, table, parts, pack_i, charge, radius_ref, sent_ref, rate_ref):
    col_at = meta[LISTED + 3]
    born = parts[0]
    for n in range(1, N_COLS):
        born = born + parts[n]
    rho = pack_i[0:I_BLOCKS, 3, :]
    alpha, beta, gamma = looked_up(table, pack_i[0:I_BLOCKS, 6, :], (3, 4, 5))
    scaled = rho * born
    poly = alpha * scaled - beta * scaled * scaled + gamma * scaled * scaled * scaled
    squash = jnp.tanh(poly)
    radius = 1.0 / (1.0 / rho - squash / (rho + OFFSET))
    slope = alpha - 2.0 * beta * scaled + 3.0 * gamma * scaled * scaled
    rate_ref[...] = radius * radius * (1.0 - squash * squash) * slope * rho / (rho + OFFSET)
    radius_ref[0:I_BLOCKS] = radius
    radius_ref[I_BLOCKS : I_BLOCKS + 8] = jnp.ones((8, TILE), F32)
    held = radius_ref[pl.ds(pl.multiple_of(col_at * HELD, HELD), HELD), :]
    for n in range(N_ROWS):
        sent_ref[n, 0] = held
        sent_ref[n, 1] = charge[...]


def pair_kernel(
    meta, pack_i, pack_j, rad_i, rad_j, grad_ref, direct_ref, acc, force, mask_ref, spread_ref, sides
):
    acc[...] = jnp.zeros_like(acc)
    force[...] = jnp.zeros_like(force)
    write_mask(mask_ref)
    write_spread(spread_ref)
    sides[...] = pack_j[...]
    for n in range(N_ROWS):
        here = slice(n * HELD, (n + 1) * HELD)
        sides[here, 3, :] = rad_j[n, 0]
        sides[here, 4, :] = 1.0 / rad_j[n, 0]
        sides[here, 5, :] = rad_j[n, 1]

    def one_tile(ia, jb, same, with_force):
        col = columns(sides[jb], spread_ref, 6)
        xi, yi, zi = (pack_i[ia, c : c + 1, :] for c in range(3))
        radius_i = rad_i[pl.ds(ia, 1), :]
        quarter_i = 0.25 / radius_i
        total = jnp.zeros((8, TILE), F32)
        sums = [jnp.zeros((8, TILE), F32)] * 3
        for s in range(0, TILE, CHUNK):
            dx, dy, dz, q = offsets(xi, yi, zi, col, s)
            base = jnp.maximum(1.0 - q * INV_SQ, 0.0)
            weight = base * base * mask_ref[same, s : s + CHUNK, :]
            arg = q * (quarter_i * col(s, 4))
            decay = jnp.exp2(arg * -LOG2E)
            inv = lax.rsqrt(q + radius_i * col(s, 3) * decay)
            weighted = weight * col(s, 5) * (inv * inv * inv)
            total += folded(weighted * col(s, 3) * (decay * (1.0 + arg)))
            if with_force:
                slope = (-2.0 * INV_SQ) * base * col(s, 5) * inv - weighted * (
                    0.5 - 0.125 * decay
                )
                sums = [a + folded(slope * d) for a, d in zip(sums, (dx, dy, dz))]

        def add():
            acc[ia] += total
            if with_force:
                at = ia // HELD * 2 + ia % 2
                for c in range(3):
                    force[at, c] += sums[c]

        return add

    for_each_tile(meta, 0, meta[LISTED], lambda *a: one_tile(*a, True))
    for_each_tile(meta, SLOTS, meta[LISTED + 1], lambda *a: one_tile(*a, False))
    grad_ref[...] = jnp.sum(acc[0:I_BLOCKS], axis=1)
    direct_ref[...] = jnp.sum(force[0:OWN_I], axis=2)


def factor_kernel(meta, grads, charge, radius, rate, held_ref, sent_ref):
    here = pl.ds(pl.multiple_of(meta[LISTED + 3] * HELD, HELD), HELD)
    total = grads[0]
    for n in range(1, N_COLS):
        total = total + grads[n]
    charges, radii = charge[...], radius[here, :]
    grad = -0.5 * charges * total
    held = (COULOMB * charges * charges / (2.0 * radii * radii) - COULOMB * grad) * rate[here, :]
    held_ref[...] = held
    for n in range(N_ROWS):
        sent_ref[n] = held


def chain_kernel(meta, pack_i, pack_j, chain_j, direct, out_ref, force, spread_ref, sides):
    force[...] = jnp.zeros_like(force)
    write_spread(spread_ref)
    sides[...] = pack_j[...]
    for n in range(N_ROWS):
        sides[n * HELD : (n + 1) * HELD, 6, :] = chain_j[n]

    def one_tile(ia, jb, same):
        col = columns(sides[jb], spread_ref, 7)
        xi, yi, zi, rho, vol, neck = (pack_i[ia, c : c + 1, :] for c in range(6))
        rho_sq, rho_gap = rho * rho, rho + NECK_GAP
        sums = [jnp.zeros((8, TILE), F32)] * 6
        for s in range(0, TILE, CHUNK):
            dx, dy, dz, q = offsets(xi, yi, zi, col, s)
            base = jnp.maximum(1.0 - q * INV_SQ, 0.0)
            weight = base * base
            w_slope = (-2.0 * INV_SQ) * base
            rho_j = col(s, 3)
            gap = rho_gap + rho_j
            off = q - gap * gap
            bump = jnp.exp2(off * off * (-LOG2E / NECK_WIDTH))
            bump = bump * (w_slope - weight * off * (2.0 / NECK_WIDTH))
            inv_i = 1.0 / (q + rho_sq)
            inv_j = 1.0 / (q + rho_j * rho_j)
            twice = 2.0 * weight
            slope_ij = col(s, 4) * (inv_i * inv_i) * (w_slope - twice * inv_i) + col(s, 5) * bump
            slope_ji = vol * (inv_j * inv_j) * (w_slope - twice * inv_j) + neck * bump
            slope_ji = slope_ji * col(s, 6)
            parts = [slope_ji * d for d in (dx, dy, dz)] + [slope_ij * d for d in (dx, dy, dz)]
            sums = [a + folded(v) for a, v in zip(sums, parts)]

        def add():
            at = ia // HELD * 2 + ia % 2
            for c in range(6):
                force[at, c] += sums[c]

        return add

    for_each_tile(meta, 0, meta[LISTED], one_tile)
    chain = jnp.sum(force[0:OWN_I], axis=2)
    for n in range(N_COLS):
        for b in range(2):
            out_ref[n, b, 0:3, :] = direct[2 * n + b]
            out_ref[n, b, 3:9, :] = chain[2 * n + b]


def last_kernel(meta, parts, chain, charge, vel, old, scale, vel_ref, force_ref):
    for b in range(2):
        here = slice(b * TILE, (b + 1) * TILE)
        total = parts[0, b]
        for n in range(1, N_COLS):
            total = total + parts[n, b]
        factor = chain[pl.ds(meta[LISTED + 2] * 2 + b, 1), :]
        force = (2.0 * COULOMB) * charge[:, here] * total[0:3] - 2.0 * (
            total[3:6] + factor * total[6:9]
        )
        force_ref[:, here] = force
        vel_ref[:, here] = vel[:, here] + scale[:, here] * (old[:, here] + force)


def tile_codes(lists, rep_at, row_at, col_at):
    list_a, list_g = lists[:, 0].astype(jnp.int32), lists[:, 1].astype(jnp.int32)
    reps = jnp.arange(N_REP, dtype=jnp.int32)[:, None]
    live = list_a >= 0
    counts = jnp.sum(live.astype(jnp.int32), axis=1)
    j_row = list_g // 2
    place_i = (list_a // 2 * N_REP + reps) * 2 + list_a % 2
    place_j = (j_row % N_ROWS * N_REP + j_row // N_ROWS) * 2 + list_g % 2
    same = (j_row == reps * N_ROWS + row_at) & (list_a == col_at * 2 + list_g % 2)
    none = I_BLOCKS * 256
    codes = jnp.where(live, place_i * 256 + place_j * 2 + same.astype(jnp.int32) - none, 0)
    other = jnp.arange(N_REP) != rep_at
    counted = jnp.where(other, counts, 0)
    before = jnp.sum(jnp.where(jnp.arange(N_REP)[:, None] < reps.T, counted[:, None], 0), axis=0)
    slot = jnp.arange(SLOTS, dtype=jnp.int32)[None, :]
    target = jnp.where(other[:, None], SLOTS + before[:, None] + slot, slot)
    hit = (target.reshape(1, LISTED) == jnp.arange(LISTED, dtype=jnp.int32)[:, None]) & live.reshape(1, LISTED)
    placed = none + jnp.sum(jnp.where(hit, codes.reshape(1, LISTED), 0), axis=1)
    own = jnp.sum(jnp.where(other, 0, counts))
    tail = jnp.stack([own, jnp.sum(counted), rep_at, col_at]).astype(jnp.int32)
    return jnp.concatenate([placed, tail])


def body(positions, velocities, old_forces, charges, atom_types, table, tile_pairs):
    rep_at = lax.axis_index(REP)
    row_at = lax.axis_index(ROWS)
    col_at = lax.axis_index(COLS)
    charge_row = charges.reshape(1, 2 * TILE)
    new_positions, sent, scale = called(
        first_kernel,
        [(3, 2 * TILE), (N_REP, 3, 4, TILE), (1, 2 * TILE)],
        [],
        [table],
        [
            positions,
            velocities,
            old_forces,
            charge_row,
            atom_types.reshape(1, 2 * TILE),
            tile_pairs.reshape(2, SLOTS),
        ],
    )
    held = exchanged(sent, REP)
    held_atoms = held[:, 0:2].reshape(HELD, 4, TILE)
    held_charges = held[:, 2, 2:4].reshape(HELD, TILE)
    meta = tile_codes(held[:, 2, 0:2, 0:SLOTS], rep_at, row_at, col_at)
    side_i = given_to_all(held_atoms, COLS, N_COLS).reshape(I_BLOCKS, 4, TILE)
    side_j = given_to_all(held_atoms, ROWS, N_ROWS).reshape(J_BLOCKS, 4, TILE)

    mask = ((2, TILE, TILE), F32)
    spread_6, spread_7 = (((32, n * TILE), jnp.bfloat16) for n in (6, 7))
    sums = ((I_BLOCKS + 1, 8, TILE), F32)
    sides = ((J_BLOCKS, 8, TILE), F32)
    born_parts, pack_i, pack_j = called(
        born_kernel,
        [(N_COLS, I_BLOCKS, TILE), (I_BLOCKS + 1, 8, TILE), (J_BLOCKS, 8, TILE)],
        [sums, mask, spread_6],
        [meta, table],
        [side_i, side_j],
    )
    born_parts = exchanged(born_parts, COLS)
    radius_i, sent, rate_i = called(
        radius_kernel,
        [(I_BLOCKS + 8, TILE), (N_ROWS, 2, HELD, TILE), (I_BLOCKS, TILE)],
        [],
        [meta, table],
        [born_parts, pack_i, held_charges],
    )
    rad_j = exchanged(sent, ROWS)
    grads, direct = called(
        pair_kernel,
        [(I_BLOCKS, TILE), (OWN_I, 3, TILE)],
        [sums, ((OWN_I + 1, 3, 8, TILE), F32), mask, spread_6, sides],
        [meta],
        [pack_i, pack_j, radius_i, rad_j],
    )
    grads = exchanged(grads.reshape(N_COLS, HELD, TILE), COLS)
    chain, sent = called(
        factor_kernel,
        [(HELD, TILE), (N_ROWS, HELD, TILE)],
        [],
        [meta],
        [grads, held_charges, radius_i, rate_i],
    )
    chain_j = exchanged(sent, ROWS)
    [shared] = called(
        chain_kernel,
        [(N_COLS, 2, 9, TILE)],
        [((OWN_I + 1, 6, 8, TILE), F32), spread_7, sides],
        [meta],
        [pack_i, pack_j, chain_j, direct],
    )
    parts = exchanged(shared, COLS)
    new_velocities, new_forces = called(
        last_kernel,
        [(3, 2 * TILE), (3, 2 * TILE)],
        [],
        [meta],
        [parts, chain, charge_row, velocities, old_forces, scale],
    )
    return (new_positions, new_velocities, new_forces)


def solution(mesh):
    split = Mesh(mesh.devices.reshape(SIZES), AXES)
    rows, cols = AXES[:4], AXES[4:]
    return jax.shard_map(
        body,
        mesh=split,
        in_specs=(
            P(None, AXES),
            P(None, AXES),
            P(None, AXES),
            P(AXES),
            P(AXES),
            P(),
            P(rows, cols, None, None),
        ),
        out_specs=(P(None, AXES), P(None, AXES), P(None, AXES)),
        check_vma=False,
    )
```

time: 224 us -> 146 us (0.65)
  starting transfers between devices: 86.9 us -> 33.2 us
  other arithmetic: 52 us -> 1.08 us
  blocking collectives: 15.5 us -> 47.1 us
  waiting for transfers between devices: 33.6 us -> 30.3 us
  local copies, waits for them, and re-layouts: 10.8 us -> 8.44 us
    all_to_all x5 -> x2, starting transfers between devices: 54.2 us -> 14.2 us  [given_to_all(): return lax.all_to_all(copies, axes, 0, 0, tiled=True)]
    all_to_all x1 -> x4, blocking collectives: 15.5 us -> 47.1 us  [exchanged(): return lax.all_to_all(pieces, axes, 0, 0, tiled=True)]
    mul x5 -> x0, other arithmetic: 15.7 us -> none  [the longest x2 15.7 us: packed(): scale * rho * rho * rho]
    select_n x3 -> x1, other arithmetic: 15.4 us -> 0.03 us  [tile_codes(): target = jnp.where(other[:, None], SLOTS + before[:, None] + slot, slot)]
    div x3 -> x0, other arithmetic: 14.9 us -> none  [the longest x1 9.92 us: radius_terms(): radius = 1.0 / (1.0 / intrinsic - squash / (intrinsic + OFFSET))]
    all_to_all x2, starting transfers between devices: 32.7 us -> 19 us  [exchanged(): return lax.all_to_all(pieces, axes, 0, 0, tiled=True)]
    all_to_all x5 -> x2, waiting for transfers between devices: 23.5 us -> 13.7 us  [given_to_all(): return lax.all_to_all(copies, axes, 0, 0, tiled=True)]
    all_to_all x2, waiting for transfers between devices: 10.2 us -> 16.7 us  [exchanged(): return lax.all_to_all(pieces, axes, 0, 0, tiled=True)]
  transfers between devices with their start and end apart: 7 -> 4, of which waited for: 5 -> 4; matrix products, arithmetic and copies ran while one was open for 10% -> 2% of each run, Pallas kernels for 0% -> 0%
where the time goes in v2:
time: 146 us; the launch traced here: 144 us
  blocking collectives  47.1 us (32%)
  starting transfers between devices  33.2 us (23%)
  waiting for transfers between devices  30.3 us (21%)
  Pallas kernels  23.1 us (16%)
  local copies, waits for them, and re-layouts  8.44 us (6%)
    all_to_all x4, blocking collectives, exchanged(): return lax.all_to_all(pieces, axes, 0, 0, tiled=True)  47.1 us
    pallas_call x7, Pallas kernels, called(): pl.pallas_call(kernel, out_shape=[jax.ShapeDtypeStruct(s, F32) for s in o...  23.1 us
    all_to_all x2, starting transfers between devices, exchanged(): return lax.all_to_all(pieces, axes, 0, 0, tiled=True)  19 us
    all_to_all x2, waiting for transfers between devices, exchanged(): return lax.all_to_all(pieces, axes, 0, 0, tiled=True)  16.7 us
    all_to_all x2, starting transfers between devices, given_to_all(): return lax.all_to_all(copies, axes, 0, 0, tiled=True)  14.2 us
    all_to_all x2, waiting for transfers between devices, given_to_all(): return lax.all_to_all(copies, axes, 0, 0, tiled=True)  13.7 us
    unnamed x18, local copies, waits for them, and re-layouts  4.78 us
  transfers between devices with their start and end apart: 4, of which 4 were waited for; matrix products, arithmetic and copies ran while one was open for 2% of the time, Pallas kernels for 0%

profile of v2, /device:TPU:1, one launch (start us, length us, event | category | flops | bytes accessed | tf_op | source)
XLA Modules:
  0.0 144.0 jit_solution(17708625462838014959)
XLA Ops:
  0.6 0.0 copy-start
  0.6 0.0 copy-start.5
  0.7 0.7 copy-done
  1.3 0.0 copy-done.5
  1.3 0.0 copy-start.1
  1.3 0.7 copy-done.1
  2.0 0.7 copy-done.3
  2.7 0.7 copy-done.6
  3.4 0.7 copy-done.7
  4.1 0.7 copy-done.8
  4.7 1.2 shard_map.94
  6.0 15.6 %all-to-all-start = ((f32[4,3,4,128]{3,2,1,0:T(4,128)}), f32[4,3,4,128]{3,2,1,0:T(4,128)S(1)}, u32[]{:S(2)}, u32[]{:S(2)}) async-start(f32[4,3,4,128]{3,2,1,0:T(4,128)} %get-tuple-element.19), calls=%async_computation | async-start | bytes 49152 | tf_op jit(solution)/shard_map/all_to_all | solution.py:46
  21.6 0.1 broadcast_in_dim.61
  21.7 0.1 broadcast_in_dim.62
  21.8 0.1 eq.42
  21.9 0.1 eq.43
  21.9 0.1 add.173
  22.0 0.1 add.170
  22.1 11.0 %all-to-all-done = f32[4,3,4,128]{3,2,1,0:T(4,128)S(1)} async-done(((f32[4,3,4,128]{3,2,1,0:T(4,128)}), f32[4,3,4,128]{3,2,1,0:T(4,128)S(1)}, u32[]{:S(2)}, u32[]{:S(2)}) %all-to-all-start) | async-done | bytes 24608 | tf_op jit(solution)/shard_map/all_to_all | solution.py:46
  33.1 0.2 fusion.1
  33.3 0.7 broadcast_in_dim.68
  33.9 5.0 %all-to-all-start.1 = ((f32[8,8,4,128]{3,2,1,0:T(4,128)}), f32[8,8,4,128]{3,2,1,0:T(4,128)S(1)}, u32[]{:S(2)}, u32[]{:S(2)}) async-start(f32[8,8,4,128]{3,2,1,0:T(4,128)} %broadcast_in_dim.68), calls=%async_computation.1 | async-start | bytes 262144 | tf_op jit(solution)/shard_map/all_to_all | solution.py:42
  39.0 0.7 fusion.8
  39.6 0.1 convert_element_type.37
  39.7 0.1 convert_element_type.39
  39.8 0.1 select_reduce_fusion.1
  39.9 4.3 %all-to-all-done.1 = f32[8,8,4,128]{3,2,1,0:T(4,128)S(1)} async-done(((f32[8,8,4,128]{3,2,1,0:T(4,128)}), f32[8,8,4,128]{3,2,1,0:T(4,128)S(1)}, u32[]{:S(2)}, u32[]{:S(2)}) %all-to-all-start.1) | async-done | bytes 131104 | tf_op jit(solution)/shard_map/all_to_all | solution.py:42
  44.2 0.7 broadcast_in_dim.69
  45.0 9.1 %all-to-all-start.2 = ((f32[16,8,4,128]{3,2,1,0:T(4,128)}), f32[16,8,4,128]{3,2,1,0:T(4,128)S(1)}, u32[]{:S(2)}, u32[]{:S(2)}) async-start(f32[16,8,4,128]{3,2,1,0:T(4,128)} %broadcast_in_dim.69), calls=%async_computation.2 | async-start | bytes 524288 | tf_op jit(solution)/shard_map/all_to_all | solution.py:42
  54.1 0.1 add.167
  54.2 0.1 add.168
  54.3 0.1 select_reduce_fusion
  54.4 1.4 concatenate.3.meta
  55.8 9.3 %all-to-all-done.2 = f32[16,8,4,128]{3,2,1,0:T(4,128)S(1)} async-done(((f32[16,8,4,128]{3,2,1,0:T(4,128)}), f32[16,8,4,128]{3,2,1,0:T(4,128)S(1)}, u32[]{:S(2)}, u32[]{:S(2)}) %all-to-all-start.2) | async-done | bytes 262176 | tf_op jit(solution)/shard_map/all_to_all | solution.py:42
  65.1 8.1 %shard_map.95 = (f32[8,64,128]{2,1,0:T(8,128)}, f32[65,8,128]{2,1,0:T(8,128)S(1)}, f32[128,8,128]{2,1,0:T(8,128)S(1)}) custom-call(s32[132]{0:T(256)S(1)} %concatenate.3.meta, f32[7,8]{1,0:T(8,128)S(1)} %copy-done, f32[64,4,128]{2,1,0:T(4,128)S(1)} %bitcast.15, f32[128,4,128]{2,1,0:T(4,128)S(1)} %bitcast.14), custom_call_target="tpu_custom_call" | custom-call | tf_op jit(solution)/shard_map/pallas_call | solution.py:50
  73.2 3.4 %all-to-all-start.3 = ((f32[8,64,128]{2,1,0:T(8,128)}), f32[8,64,128]{2,1,0:T(8,128)S(1)}, u32[]{:S(2)}, u32[]{:S(2)}) async-start(f32[8,64,128]{2,1,0:T(8,128)} %get-tuple-element.22), calls=%async_computation.3 | async-start | bytes 524288 | tf_op jit(solution)/shard_map/all_to_all | solution.py:46
  76.7 5.7 %all-to-all-done.3.parts = f32[8,64,128]{2,1,0:T(8,128)S(1)} async-done(((f32[8,64,128]{2,1,0:T(8,128)}), f32[8,64,128]{2,1,0:T(8,128)S(1)}, u32[]{:S(2)}, u32[]{:S(2)}) %all-to-all-start.3) | async-done | bytes 262176 | tf_op jit(solution)/shard_map/all_to_all | solution.py:46
  82.4 1.3 shard_map.96
  83.7 15.6 %all_to_all.40.rad_j = f32[16,2,8,128]{3,2,1,0:T(8,128)S(1)} all-to-all(f32[16,2,8,128]{3,2,1,0:T(8,128)S(1)} %get-tuple-element.24), channel_id=1, replica_groups=mesh['zh'=4,'zl'=4,'yh'=2,'core'=2,'x'=4,'yl'=2] {'zl','yh','core'}, dimensions={0} | all-to-all | bytes 262144 | tf_op jit(solution)/shard_map/all_to_all | solution.py:46
  99.3 7.0 %shard_map.97 = (f32[64,128]{1,0:T(8,128)S(1)}, f32[16,3,128]{2,1,0:T(4,128)S(1)}) custom-call(s32[132]{0:T(256)S(1)} %concatenate.3.meta, f32[65,8,128]{2,1,0:T(8,128)S(1)} %get-tuple-element.20.pack_i, f32[128,8,128]{2,1,0:T(8,128)S(1)} %get-tuple-element.21.pack_j, f32[72,128]{1,0:T(8,128)S(1)} %get-tuple-element.23.rad_i.radius, ...), custom_call_target="tpu_custom_call" | custom-call | tf_op jit(solution)/shard_map/pallas_call | solution.py:50
  106.3 8.4 %all_to_all.41.grads = f32[8,8,128]{2,1,0:T(8,128)S(1)} all-to-all(f32[8,8,128]{2,1,0:T(8,128)S(1)} %bitcast.18), channel_id=1, replica_groups=mesh['zh'=4,'zl'=4,'yh'=2,'core'=2,'x'=4,'yl'=2] {'x','yl'}, dimensions={0} | all-to-all | bytes 65536 | tf_op jit(solution)/shard_map/all_to_all | solution.py:46
  114.7 0.6 shard_map.98
  115.3 15.5 %all_to_all.42.chain_j = f32[16,8,128]{2,1,0:T(8,128)S(1)} all-to-all(f32[16,8,128]{2,1,0:T(8,128)S(1)} %get-tuple-element.27), channel_id=1, replica_groups=mesh['zh'=4,'zl'=4,'yh'=2,'core'=2,'x'=4,'yl'=2] {'zl','yh','core'}, dimensions={0} | all-to-all | bytes 131072 | tf_op jit(solution)/shard_map/all_to_all | solution.py:46
  130.9 3.7 %shard_map.99 = f32[8,2,9,128]{3,2,1,0:T(8,128)S(1)} custom-call(s32[132]{0:T(256)S(1)} %concatenate.3.meta, f32[65,8,128]{2,1,0:T(8,128)S(1)} %get-tuple-element.20.pack_i, f32[128,8,128]{2,1,0:T(8,128)S(1)} %get-tuple-element.21.pack_j, f32[16,8,128]{2,1,0:T(8,128)S(1)} %all_to_all.42.chain_j, f32[16,3,128]{2,1,0:T(4,128)S(1)} %get-tuple-element.28.direct), custom_call_target="tpu_custom_call" | custom-call | tf_op jit(solution)/shard_map/pallas_call | solution.py:50
  134.6 7.5 %all_to_all.43 = f32[8,2,9,128]{3,1,2,0:T(2,128)S(1)} all-to-all(f32[8,2,9,128]{3,1,2,0:T(2,128)S(1)} %copy.12), channel_id=1, replica_groups=mesh['zh'=4,'zl'=4,'yh'=2,'core'=2,'x'=4,'yl'=2] {'x','yl'}, dimensions={0} | all-to-all | bytes 147456 | tf_op jit(solution)/shard_map/all_to_all | solution.py:46
  142.1 0.7 copy-done.2
  142.8 0.0 copy-done.4
  142.8 1.2 shard_map.100
  (19 shorter events, 0.1 us)
Async XLA Ops:
  0.6 0.7 copy-start
  0.6 0.7 copy-start.5
  1.3 0.7 copy-start.1
  2.0 0.7 copy-start.3
  2.7 0.7 copy-start.6
  3.4 0.7 copy-start.7
  4.1 0.7 copy-start.8
  6.0 27.1 %all-to-all-start = ((f32[4,3,4,128]{3,2,1,0:T(4,128)}), f32[4,3,4,128]{3,2,1,0:T(4,128)S(1)}, u32[]{:S(2)}, u32[]{:S(2)}) async-start(f32[4,3,4,128]{3,2,1,0:T(4,128)} %get-tuple-element.19), calls=%async_computation | async-start | bytes 49152 | tf_op jit(solution)/shard_map/all_to_all | solution.py:46
  33.9 10.3 %all-to-all-start.1 = ((f32[8,8,4,128]{3,2,1,0:T(4,128)}), f32[8,8,4,128]{3,2,1,0:T(4,128)S(1)}, u32[]{:S(2)}, u32[]{:S(2)}) async-start(f32[8,8,4,128]{3,2,1,0:T(4,128)} %broadcast_in_dim.68), calls=%async_computation.1 | async-start | bytes 262144 | tf_op jit(solution)/shard_map/all_to_all | solution.py:42
  45.0 20.1 %all-to-all-start.2 = ((f32[16,8,4,128]{3,2,1,0:T(4,128)}), f32[16,8,4,128]{3,2,1,0:T(4,128)S(1)}, u32[]{:S(2)}, u32[]{:S(2)}) async-start(f32[16,8,4,128]{3,2,1,0:T(4,128)} %broadcast_in_dim.69), calls=%async_computation.2 | async-start | bytes 524288 | tf_op jit(solution)/shard_map/all_to_all | solution.py:42
  73.2 9.1 %all-to-all-start.3 = ((f32[8,64,128]{2,1,0:T(8,128)}), f32[8,64,128]{2,1,0:T(8,128)S(1)}, u32[]{:S(2)}, u32[]{:S(2)}) async-start(f32[8,64,128]{2,1,0:T(8,128)} %get-tuple-element.22), calls=%async_computation.3 | async-start | bytes 524288 | tf_op jit(solution)/shard_map/all_to_all | solution.py:46
  142.1 0.7 copy-start.2
  142.1 0.7 copy-start.4

commit v3 on v2

--- a/solution.py
+++ b/solution.py
@@ -11,6 +11,7 @@
 CHUNK = 32
 UNROLL = 4
 LISTED = 128
+PICKED = 2048
 
 CUTOFF = 12.0
 COULOMB = 32.0
@@ -20,6 +21,7 @@
 NECK_WIDTH = 16.0
 INV_SQ = 1.0 / (CUTOFF * CUTOFF)
 LOG2E = 1.4426950408889634
+NO_KEY = 16777216.0
 
 AXES = ("zh", "zl", "yh", "core", "x", "yl")
 SIZES = (4, 4, 2, 2, 4, 2)
@@ -37,22 +39,17 @@
 F32 = jnp.float32
 
 
-def given_to_all(shard, axes, count):
-    copies = jnp.broadcast_to(shard, (count, *shard.shape))
-    return lax.all_to_all(copies, axes, 0, 0, tiled=True)
-
-
 def exchanged(pieces, axes):
     return lax.all_to_all(pieces, axes, 0, 0, tiled=True)
 
 
-def called(kernel, outs, scratch, smem, vmem):
+def called(kernel, outs, scratch, smem, vmem, inputs=VMEM, outputs=VMEM, kind=F32):
     return pl.pallas_call(
         kernel,
-        out_shape=[jax.ShapeDtypeStruct(s, F32) for s in outs],
-        in_specs=[SMEM] * len(smem) + [VMEM] * len(vmem),
-        out_specs=[VMEM] * len(outs),
-        scratch_shapes=[pltpu.VMEM(s, t) for s, t in scratch],
+        out_shape=[jax.ShapeDtypeStruct(s, kind) for s in outs],
+        in_specs=[SMEM] * len(smem) + [inputs] * len(vmem),
+        out_specs=[outputs] * len(outs),
+        scratch_shapes=[pltpu.VMEM(*s) if isinstance(s, tuple) else s for s in scratch],
         compiler_params=pltpu.CompilerParams(vmem_limit_bytes=32 * 1024 * 1024),
     )(*smem, *vmem)
 
@@ -122,12 +119,35 @@
     lax.fori_loop(0, (count + UNROLL - 1) // UNROLL, step, 0)
 
 
-def first_kernel(table, pos, vel, old, charge, kinds, pairs, new_ref, sent_ref, scale_ref):
+def first_kernel(
+    table, pos_in, vel_in, old_in, charge_in, kinds_in, pairs_in, new_ref, sent_ref, kept_ref,
+    pos, vel, old, charge, kinds, pairs, sems
+):
+    copies = [
+        pltpu.make_async_copy(there, here, sems.at[n])
+        for n, (there, here) in enumerate(
+            (
+                (pos_in, pos),
+                (vel_in, vel),
+                (old_in, old),
+                (charge_in, charge),
+                (kinds_in, kinds),
+                (pairs_in, pairs),
+            )
+        )
+    ]
+    for copy in copies:
+        copy.start()
+    for copy in copies:
+        copy.wait()
     types = kinds[...].astype(F32)
     [mass] = looked_up(table, types, (6,))
     new = pos[...] + TIMESTEP * vel[...] + TIMESTEP * TIMESTEP / (2.0 * mass) * old[...]
+    scale = TIMESTEP / (2.0 * mass)
     new_ref[...] = new
-    scale_ref[...] = TIMESTEP / (2.0 * mass)
+    kept_ref[0:3] = vel[...] + scale * old[...]
+    kept_ref[3:4] = scale
+    kept_ref[4:5] = charge[...]
     lists = pairs[...].astype(F32)
     lists = jnp.concatenate([lists, jnp.zeros((2, TILE - SLOTS), F32)], axis=1)
     for n in range(N_REP):
@@ -139,22 +159,81 @@
         sent_ref[n, 2, 0:2, :] = lists
 
 
+def col_kernel(places, held, sent_ref):
+    lists = held[places[0], 2, 0:2, :]
+    for n in range(N_COLS):
+        for z in range(N_REP):
+            sent_ref[n, 2 * z] = held[z, 0]
+            sent_ref[n, 2 * z + 1] = held[z, 1]
+            at = z % 2 * 2
+            sent_ref[n, 8 + z // 2, at : at + 2, :] = held[z, 2, 2:4, :]
+        sent_ref[n, 10, 0:2, :] = lists
+        sent_ref[n, 10, 2:4, :] = lists
+
+
+def row_kernel(places, side_i, sent_ref):
+    rows = [
+        jnp.concatenate(
+            [side_i[4 * half + n, 10, r : r + 1, 0:SLOTS] for n in range(4)], axis=1
+        )
+        for r in range(2)
+        for half in range(2)
+    ]
+    lists = jnp.concatenate(rows, axis=0)
+    for n in range(N_ROWS):
+        for b in range(HELD):
+            sent_ref[n, b] = side_i[places[2], b]
+        sent_ref[n, HELD] = lists
+
+
+def pick_kernel(keys_ref, picked):
+    keys = keys_ref[...]
+    count = jnp.sum(jnp.where(keys < NO_KEY, 1.0, 0.0)).astype(jnp.int32)
+
+    def step(k, keys):
+        least = jnp.min(keys)
+        place = least.astype(jnp.int32) >> 12
+        picked[k] = (place >> 6) * 256 + (place & 63) * 2
+        return jnp.where(keys == least, NO_KEY, keys)
+
+    lax.fori_loop(0, count, step, keys)
+    for n in range(UNROLL):
+        picked[count + n] = 2 * N_ROWS * 256
+    picked[PICKED + UNROLL] = count
+
+
 def born_kernel(
-    meta, table, side_i, side_j, out_ref, pack_i, pack_j, acc, mask_ref, spread_ref
+    meta,
+    table,
+    side_i,
+    side_j,
+    out_ref,
+    pack_i,
+    pack_j,
+    charge_i,
+    acc,
+    mask_ref,
+    spread_ref,
 ):
     acc[...] = jnp.zeros_like(acc)
     write_mask(mask_ref)
     write_spread(spread_ref)
-    for side, pack, blocks in ((side_i, pack_i, I_BLOCKS), (side_j, pack_j, J_BLOCKS)):
-        types = side[:, 3, :]
-        rho, scale, neck = looked_up(table, types, (0, 1, 2))
-        pack[0:blocks, 0:3, :] = side[:, 0:3, :]
-        pack[0:blocks, 3, :] = rho
-        pack[0:blocks, 4, :] = scale * rho * rho * rho
-        pack[0:blocks, 5, :] = neck
-        pack[0:blocks, 6, :] = types
-        pack[0:blocks, 7, :] = types
+    for side, pack, groups in ((side_i, pack_i, N_COLS), (side_j, pack_j, N_ROWS)):
+        for n in range(groups):
+            here = slice(n * HELD, (n + 1) * HELD)
+            types = side[n, 0:HELD, 3, :]
+            rho, scale, neck = looked_up(table, types, (0, 1, 2))
+            pack[here, 0:3, :] = side[n, 0:HELD, 0:3, :]
+            pack[here, 3, :] = rho
+            pack[here, 4, :] = scale * rho * rho * rho
+            pack[here, 5, :] = neck
+            pack[here, 6, :] = types
+            pack[here, 7, :] = types
     pack_i[I_BLOCKS] = jnp.ones((8, TILE), F32)
+    pack_j[J_BLOCKS] = jnp.ones((8, TILE), F32)
+    for n in range(N_COLS):
+        charge_i[n * HELD : n * HELD + 4] = side_i[n, 8]
+        charge_i[n * HELD + 4 : (n + 1) * HELD] = side_i[n, 9]
 
     def one_tile(ia, jb, same):
         col = columns(pack_j[jb], spread_ref, 6)
@@ -183,8 +262,8 @@
         out_ref[n] = born
 
 
-def radius_kernel(meta, table, parts, pack_i, charge, radius_ref, sent_ref, rate_ref):
-    col_at = meta[LISTED + 3]
+def radius_kernel(places, table, parts, pack_i, charge, radius_ref, sent_ref, rate_ref):
+    col_at = places[2]
     born = parts[0]
     for n in range(1, N_COLS):
         born = born + parts[n]
@@ -198,20 +277,54 @@
     rate_ref[...] = radius * radius * (1.0 - squash * squash) * slope * rho / (rho + OFFSET)
     radius_ref[0:I_BLOCKS] = radius
     radius_ref[I_BLOCKS : I_BLOCKS + 8] = jnp.ones((8, TILE), F32)
-    held = radius_ref[pl.ds(pl.multiple_of(col_at * HELD, HELD), HELD), :]
+    here = pl.ds(pl.multiple_of(col_at * HELD, HELD), HELD)
+    held, charges = radius_ref[here, :], charge[here, :]
     for n in range(N_ROWS):
         sent_ref[n, 0] = held
-        sent_ref[n, 1] = charge[...]
+        sent_ref[n, 1] = charges
+
+
+def slope_kernel(meta, pack_i, pack_j, out_ref, force, spread_ref):
+    force[...] = jnp.zeros_like(force)
+    write_spread(spread_ref)
+
+    def one_tile(ia, jb, same):
+        col = columns(pack_j[jb], spread_ref, 6)
+        xi, yi, zi, rho = (pack_i[ia, c : c + 1, :] for c in range(4))
+        rho_sq, rho_gap = rho * rho, rho + NECK_GAP
+        sums = [jnp.zeros((8, TILE), F32)] * 3
+        for s in range(0, TILE, CHUNK):
+            dx, dy, dz, q = offsets(xi, yi, zi, col, s)
+            base = jnp.maximum(1.0 - q * INV_SQ, 0.0)
+            weight = base * base
+            w_slope = (-2.0 * INV_SQ) * base
+            gap = rho_gap + col(s, 3)
+            off = q - gap * gap
+            bump = jnp.exp2(off * off * (-LOG2E / NECK_WIDTH))
+            bump = bump * (w_slope - weight * off * (2.0 / NECK_WIDTH))
+            inv = 1.0 / (q + rho_sq)
+            slope = col(s, 4) * (inv * inv) * (w_slope - 2.0 * weight * inv) + col(s, 5) * bump
+            sums = [a + folded(slope * d) for a, d in zip(sums, (dx, dy, dz))]
+
+        def add():
+            at = ia // HELD * 2 + ia % 2
+            for c in range(3):
+                force[at, c] += sums[c]
+
+        return add
+
+    for_each_tile(meta, 0, meta[LISTED], one_tile)
+    out_ref[...] = jnp.sum(force[0:OWN_I], axis=2)
 
 
 def pair_kernel(
-    meta, pack_i, pack_j, rad_i, rad_j, grad_ref, direct_ref, acc, force, mask_ref, spread_ref, sides
+    meta, pack_i, pack_j, rad_i, rad_j, slopes, out_ref, acc, force, mask_ref, spread_ref, sides
 ):
     acc[...] = jnp.zeros_like(acc)
     force[...] = jnp.zeros_like(force)
     write_mask(mask_ref)
     write_spread(spread_ref)
-    sides[...] = pack_j[...]
+    sides[...] = pack_j[0:J_BLOCKS]
     for n in range(N_ROWS):
         here = slice(n * HELD, (n + 1) * HELD)
         sides[here, 3, :] = rad_j[n, 0]
@@ -251,35 +364,41 @@
 
     for_each_tile(meta, 0, meta[LISTED], lambda *a: one_tile(*a, True))
     for_each_tile(meta, SLOTS, meta[LISTED + 1], lambda *a: one_tile(*a, False))
-    grad_ref[...] = jnp.sum(acc[0:I_BLOCKS], axis=1)
-    direct_ref[...] = jnp.sum(force[0:OWN_I], axis=2)
-
-
-def factor_kernel(meta, grads, charge, radius, rate, held_ref, sent_ref):
-    here = pl.ds(pl.multiple_of(meta[LISTED + 3] * HELD, HELD), HELD)
-    total = grads[0]
-    for n in range(1, N_COLS):
-        total = total + grads[n]
-    charges, radii = charge[...], radius[here, :]
-    grad = -0.5 * charges * total
-    held = (COULOMB * charges * charges / (2.0 * radii * radii) - COULOMB * grad) * rate[here, :]
-    held_ref[...] = held
-    for n in range(N_ROWS):
-        sent_ref[n] = held
-
-
-def chain_kernel(meta, pack_i, pack_j, chain_j, direct, out_ref, force, spread_ref, sides):
+    grads = jnp.sum(acc[0:I_BLOCKS], axis=1)
+    direct = jnp.sum(force[0:OWN_I], axis=2)
+    for n in range(N_COLS):
+        out_ref[n, 0:I_BLOCKS] = grads
+        for b in range(2):
+            at = I_BLOCKS + 8 * b
+            out_ref[n, at : at + 3, :] = direct[2 * n + b]
+            out_ref[n, at + 3 : at + 6, :] = slopes[2 * n + b]
+            out_ref[n, at + 6 : at + 8, :] = slopes[2 * n + b, 0:2, :]
+
+
+def chain_kernel(
+    picked, places, pack_i, pack_j, parts, charge, radius, rate, out_ref, own_ref, force, spread_ref, sides
+):
     force[...] = jnp.zeros_like(force)
     write_spread(spread_ref)
-    sides[...] = pack_j[...]
-    for n in range(N_ROWS):
-        sides[n * HELD : (n + 1) * HELD, 6, :] = chain_j[n]
-
-    def one_tile(ia, jb, same):
-        col = columns(sides[jb], spread_ref, 7)
-        xi, yi, zi, rho, vol, neck = (pack_i[ia, c : c + 1, :] for c in range(6))
-        rho_sq, rho_gap = rho * rho, rho + NECK_GAP
-        sums = [jnp.zeros((8, TILE), F32)] * 6
+    total = parts[0]
+    for n in range(1, N_COLS):
+        total = total + parts[n]
+    charges, radii = charge[...], radius[0:I_BLOCKS]
+    grad = -0.5 * charges * total[0:I_BLOCKS]
+    chain = (COULOMB * charges * charges / (2.0 * radii * radii) - COULOMB * grad) * rate[...]
+    sides[...] = pack_i[0:I_BLOCKS]
+    sides[:, 4, :] = chain
+    first = places[2] * HELD + places[0] * 2
+    own_ref[0:16] = total[I_BLOCKS : I_BLOCKS + 16]
+    for b in range(2):
+        own_ref[16 + b : 17 + b] = sides[first + b, 4:5, :]
+
+    def one_tile(at, jb, same):
+        ib = jnp.where(at < 2 * N_ROWS, at // 2 * HELD + places[0] * 2 + at % 2, J_BLOCKS)
+        col = columns(sides[jb], spread_ref, 5)
+        xi, yi, zi, rho, vol, neck = (pack_j[ib, c : c + 1, :] for c in range(6))
+        rho_gap = rho + NECK_GAP
+        sums = [jnp.zeros((8, TILE), F32)] * 3
         for s in range(0, TILE, CHUNK):
             dx, dy, dz, q = offsets(xi, yi, zi, col, s)
             base = jnp.maximum(1.0 - q * INV_SQ, 0.0)
@@ -290,42 +409,43 @@
             off = q - gap * gap
             bump = jnp.exp2(off * off * (-LOG2E / NECK_WIDTH))
             bump = bump * (w_slope - weight * off * (2.0 / NECK_WIDTH))
-            inv_i = 1.0 / (q + rho_sq)
-            inv_j = 1.0 / (q + rho_j * rho_j)
-            twice = 2.0 * weight
-            slope_ij = col(s, 4) * (inv_i * inv_i) * (w_slope - twice * inv_i) + col(s, 5) * bump
-            slope_ji = vol * (inv_j * inv_j) * (w_slope - twice * inv_j) + neck * bump
-            slope_ji = slope_ji * col(s, 6)
-            parts = [slope_ji * d for d in (dx, dy, dz)] + [slope_ij * d for d in (dx, dy, dz)]
-            sums = [a + folded(v) for a, v in zip(sums, parts)]
+            inv = 1.0 / (q + rho_j * rho_j)
+            slope = vol * (inv * inv) * (w_slope - 2.0 * weight * inv) + neck * bump
+            slope = slope * col(s, 4)
+            sums = [a + folded(slope * d) for a, d in zip(sums, (dx, dy, dz))]
 
         def add():
-            at = ia // HELD * 2 + ia % 2
-            for c in range(6):
+            for c in range(3):
                 force[at, c] += sums[c]
 
         return add
 
-    for_each_tile(meta, 0, meta[LISTED], one_tile)
-    chain = jnp.sum(force[0:OWN_I], axis=2)
-    for n in range(N_COLS):
-        for b in range(2):
-            out_ref[n, b, 0:3, :] = direct[2 * n + b]
-            out_ref[n, b, 3:9, :] = chain[2 * n + b]
-
-
-def last_kernel(meta, parts, chain, charge, vel, old, scale, vel_ref, force_ref):
+    for_each_tile(picked, 0, picked[PICKED + UNROLL], one_tile)
+    out_ref[...] = jnp.sum(force[0 : 2 * N_ROWS], axis=2)
+
+
+def last_kernel(parts, own, kept, vel_ref, force_ref):
     for b in range(2):
         here = slice(b * TILE, (b + 1) * TILE)
         total = parts[0, b]
-        for n in range(1, N_COLS):
+        for n in range(1, N_ROWS):
             total = total + parts[n, b]
-        factor = chain[pl.ds(meta[LISTED + 2] * 2 + b, 1), :]
-        force = (2.0 * COULOMB) * charge[:, here] * total[0:3] - 2.0 * (
-            total[3:6] + factor * total[6:9]
+        force = (2.0 * COULOMB) * kept[4:5, here] * own[8 * b : 8 * b + 3, :] - 2.0 * (
+            total + own[16 + b : 17 + b, :] * own[8 * b + 3 : 8 * b + 6, :]
         )
         force_ref[:, here] = force
-        vel_ref[:, here] = vel[:, here] + scale[:, here] * (old[:, here] + force)
+        vel_ref[:, here] = kept[0:3, here] + kept[3:4, here] * force
+
+
+def transposed_keys(lists, places):
+    list_a, list_g = lists[:, 0:2].astype(jnp.int32), lists[:, 2:4].astype(jnp.int32)
+    source, half, lane = (lax.broadcasted_iota(jnp.int32, list_a.shape, n) for n in range(3))
+    j_col, j_row = half * 4 + lane // SLOTS, list_g // 2
+    mine = (list_a >= 0) & (list_a // 2 == places[2]) & (j_row % N_ROWS == places[1])
+    place_j = (j_col * N_REP + j_row // N_ROWS) * 2 + list_g % 2
+    key = ((source * 2 + list_a % 2) * I_BLOCKS + place_j) * 4096
+    key = key + (source * 2 + half) * TILE + lane
+    return jnp.where(mine, key.astype(F32), NO_KEY).reshape(2 * N_ROWS, TILE)
 
 
 def tile_codes(lists, rep_at, row_at, col_at):
@@ -355,78 +475,90 @@
     rep_at = lax.axis_index(REP)
     row_at = lax.axis_index(ROWS)
     col_at = lax.axis_index(COLS)
-    charge_row = charges.reshape(1, 2 * TILE)
-    new_positions, sent, scale = called(
+    places = jnp.stack([rep_at, row_at, col_at]).astype(jnp.int32)
+    row = (1, 2 * TILE)
+    new_positions, sent, kept = called(
         first_kernel,
-        [(3, 2 * TILE), (N_REP, 3, 4, TILE), (1, 2 * TILE)],
-        [],
+        [(3, 2 * TILE), (N_REP, 3, 4, TILE), (5, 2 * TILE)],
+        [((3, 2 * TILE), F32)] * 3
+        + [(row, F32), (row, jnp.int32), ((2, SLOTS), jnp.int32), pltpu.SemaphoreType.DMA((6,))],
         [table],
         [
             positions,
             velocities,
             old_forces,
-            charge_row,
-            atom_types.reshape(1, 2 * TILE),
+            charges.reshape(row),
+            atom_types.reshape(row),
             tile_pairs.reshape(2, SLOTS),
         ],
+        inputs=pl.BlockSpec(memory_space=pl.ANY),
     )
     held = exchanged(sent, REP)
-    held_atoms = held[:, 0:2].reshape(HELD, 4, TILE)
-    held_charges = held[:, 2, 2:4].reshape(HELD, TILE)
     meta = tile_codes(held[:, 2, 0:2, 0:SLOTS], rep_at, row_at, col_at)
-    side_i = given_to_all(held_atoms, COLS, N_COLS).reshape(I_BLOCKS, 4, TILE)
-    side_j = given_to_all(held_atoms, ROWS, N_ROWS).reshape(J_BLOCKS, 4, TILE)
+    [sent] = called(col_kernel, [(N_COLS, 11, 4, TILE)], [], [places], [held])
+    side_i = exchanged(sent, COLS)
+    [sent] = called(row_kernel, [(N_ROWS, 9, 4, TILE)], [], [places], [side_i])
+    side_j = exchanged(sent, ROWS)
 
     mask = ((2, TILE, TILE), F32)
-    spread_6, spread_7 = (((32, n * TILE), jnp.bfloat16) for n in (6, 7))
+    spread_5, spread_6 = (((32, n * TILE), jnp.bfloat16) for n in (5, 6))
     sums = ((I_BLOCKS + 1, 8, TILE), F32)
-    sides = ((J_BLOCKS, 8, TILE), F32)
-    born_parts, pack_i, pack_j = called(
+    forces = ((OWN_I + 1, 3, 8, TILE), F32)
+    born_parts, pack_i, pack_j, charge_i = called(
         born_kernel,
-        [(N_COLS, I_BLOCKS, TILE), (I_BLOCKS + 1, 8, TILE), (J_BLOCKS, 8, TILE)],
+        [
+            (N_COLS, I_BLOCKS, TILE),
+            (I_BLOCKS + 1, 8, TILE),
+            (J_BLOCKS + 1, 8, TILE),
+            (I_BLOCKS, TILE),
+        ],
         [sums, mask, spread_6],
         [meta, table],
         [side_i, side_j],
     )
     born_parts = exchanged(born_parts, COLS)
+    [slopes] = called(
+        slope_kernel, [(OWN_I, 3, TILE)], [forces, spread_6], [meta], [pack_i, pack_j]
+    )
+    [picked] = called(
+        pick_kernel,
+        [(PICKED + UNROLL + 1,)],
+        [],
+        [],
+        [transposed_keys(side_j[:, HELD], places)],
+        outputs=SMEM,
+        kind=jnp.int32,
+    )
     radius_i, sent, rate_i = called(
         radius_kernel,
         [(I_BLOCKS + 8, TILE), (N_ROWS, 2, HELD, TILE), (I_BLOCKS, TILE)],
         [],
-        [meta, table],
-        [born_parts, pack_i, held_charges],
+        [places, table],
+        [born_parts, pack_i, charge_i],
     )
     rad_j = exchanged(sent, ROWS)
-    grads, direct = called(
+    [parts] = called(
         pair_kernel,
-        [(I_BLOCKS, TILE), (OWN_I, 3, TILE)],
-        [sums, ((OWN_I + 1, 3, 8, TILE), F32), mask, spread_6, sides],
+        [(N_COLS, I_BLOCKS + 16, TILE)],
+        [sums, forces, mask, spread_6, ((J_BLOCKS, 8, TILE), F32)],
         [meta],
-        [pack_i, pack_j, radius_i, rad_j],
-    )
-    grads = exchanged(grads.reshape(N_COLS, HELD, TILE), COLS)
-    chain, sent = called(
-        factor_kernel,
-        [(HELD, TILE), (N_ROWS, HELD, TILE)],
-        [],
-        [meta],
-        [grads, held_charges, radius_i, rate_i],
-    )
-    chain_j = exchanged(sent, ROWS)
-    [shared] = called(
+        [pack_i, pack_j, radius_i, rad_j, slopes],
+    )
+    parts = exchanged(parts, COLS)
+    forces_part, own = called(
         chain_kernel,
-        [(N_COLS, 2, 9, TILE)],
-        [((OWN_I + 1, 6, 8, TILE), F32), spread_7, sides],
-        [meta],
-        [pack_i, pack_j, chain_j, direct],
-    )
-    parts = exchanged(shared, COLS)
+        [(2 * N_ROWS, 3, TILE), (18, TILE)],
+        [
+            ((2 * N_ROWS + 1, 3, 8, TILE), F32),
+            spread_5,
+            ((I_BLOCKS, 8, TILE), F32),
+        ],
+        [picked, places],
+        [pack_i, pack_j, parts, charge_i, radius_i, rate_i],
+    )
+    parts = exchanged(forces_part.reshape(N_ROWS, 2, 3, TILE), ROWS)
     new_velocities, new_forces = called(
-        last_kernel,
-        [(3, 2 * TILE), (3, 2 * TILE)],
-        [],
-        [meta],
-        [parts, chain, charge_row, velocities, old_forces, scale],
+        last_kernel, [(3, 2 * TILE), (3, 2 * TILE)], [], [], [parts, own, kept]
     )
     return (new_positions, new_velocities, new_forces)
 

time: 146 us -> 139 us (0.952)
  blocking collectives: 47.1 us -> 24.5 us
  starting transfers between devices: 33.2 us -> 42.4 us
  waiting for transfers between devices: 30.3 us -> 36.1 us
  Pallas kernels: 23.1 us -> 26.4 us
  local copies, waits for them, and re-layouts: 8.44 us -> 6.3 us
    all_to_all x2 -> x5, starting transfers between devices: 19 us -> 42.4 us  [exchanged(): return lax.all_to_all(pieces, axes, 0, 0, tiled=True)]
    all_to_all x4 -> x2, blocking collectives: 47.1 us -> 24.5 us  [exchanged(): return lax.all_to_all(pieces, axes, 0, 0, tiled=True)]
    all_to_all x2 -> x5, waiting for transfers between devices: 16.7 us -> 36.1 us  [exchanged(): return lax.all_to_all(pieces, axes, 0, 0, tiled=True)]
    all_to_all x2 -> x0, starting transfers between devices: 14.2 us -> none  [given_to_all(): return lax.all_to_all(copies, axes, 0, 0, tiled=True)]
    all_to_all x2 -> x0, waiting for transfers between devices: 13.7 us -> none  [given_to_all(): return lax.all_to_all(copies, axes, 0, 0, tiled=True)]
    pallas_call x7 -> x10, Pallas kernels: 23.1 us -> 26.4 us  [called(): pl.pallas_call(kernel, out_shape=[jax.ShapeDtypeStruct(s, kind) for s in...]
    unnamed x18 -> x14, local copies, waits for them, and re-layouts: 4.78 us -> 4.1 us
  transfers between devices with their start and end apart: 4 -> 5, of which waited for: 4 -> 5; matrix products, arithmetic and copies ran while one was open for 2% -> 2% of each run, Pallas kernels for 0% -> 3%
where the time goes in v3:
time: 139 us; the launch traced here: 138 us
  starting transfers between devices  42.4 us (31%)
  waiting for transfers between devices  36.1 us (26%)
  Pallas kernels  26.4 us (19%)
  blocking collectives  24.5 us (18%)
  local copies, waits for them, and re-layouts  6.3 us (5%)
  other arithmetic  1.44 us (1%)
    all_to_all x5, starting transfers between devices, exchanged(): return lax.all_to_all(pieces, axes, 0, 0, tiled=True)  42.4 us
    all_to_all x5, waiting for transfers between devices, exchanged(): return lax.all_to_all(pieces, axes, 0, 0, tiled=True)  36.1 us
    pallas_call x10, Pallas kernels, called(): pl.pallas_call(kernel, out_shape=[jax.ShapeDtypeStruct(s, kind) for s in...  26.4 us
    all_to_all x2, blocking collectives, exchanged(): return lax.all_to_all(pieces, axes, 0, 0, tiled=True)  24.5 us
    unnamed x14, local copies, waits for them, and re-layouts  4.1 us
  transfers between devices with their start and end apart: 5, of which 5 were waited for; matrix products, arithmetic and copies ran while one was open for 2% of the time, Pallas kernels for 3%

profile of v3, /device:TPU:1, one launch (start us, length us, event | category | flops | bytes accessed | tf_op | source)
XLA Modules:
  0.0 137.9 jit_solution(14285264175119733061)
XLA Ops:
  0.6 0.0 copy-start
  0.6 0.0 copy-start.4
  0.7 0.7 copy-done
  1.3 0.0 copy-done.4
  1.3 0.7 copy-done.1
  2.0 0.7 copy-done.2
  2.7 0.7 copy-done.3
  3.4 0.7 copy-done.5
  4.1 0.7 copy-done.6
  4.7 1.3 shard_map.94
  6.1 15.6 %all-to-all-start = ((f32[4,3,4,128]{3,2,1,0:T(4,128)}), f32[4,3,4,128]{3,2,1,0:T(4,128)S(1)}, u32[]{:S(2)}, u32[]{:S(2)}) async-start(f32[4,3,4,128]{3,2,1,0:T(4,128)} %get-tuple-element.18), calls=%async_computation | async-start | bytes 49152 | tf_op jit(solution)/shard_map/all_to_all | solution.py:43
  21.7 0.1 broadcast_in_dim.60
  21.8 0.1 broadcast_in_dim.61
  21.9 0.1 eq.62
  22.0 0.1 eq.63
  22.1 0.1 add.230
  22.1 0.1 add.227
  22.2 0.1 pad_add_fusion.places
  22.3 10.9 %all-to-all-done.held = f32[4,3,4,128]{3,2,1,0:T(4,128)S(1)} async-done(((f32[4,3,4,128]{3,2,1,0:T(4,128)}), f32[4,3,4,128]{3,2,1,0:T(4,128)S(1)}, u32[]{:S(2)}, u32[]{:S(2)}) %all-to-all-start) | async-done | bytes 24608 | tf_op jit(solution)/shard_map/all_to_all | solution.py:43
  33.2 0.2 fusion.5
  33.4 1.3 shard_map.95
  34.6 5.0 %all-to-all-start.1 = ((f32[8,11,4,128]{3,2,1,0:T(4,128)}), f32[8,11,4,128]{3,2,1,0:T(4,128)S(1)}, u32[]{:S(2)}, u32[]{:S(2)}) async-start(f32[8,11,4,128]{3,2,1,0:T(4,128)} %shard_map.95), calls=%async_computation.1 | async-start | bytes 360448 | tf_op jit(solution)/shard_map/all_to_all | solution.py:43
  39.6 0.7 fusion.12
  40.3 0.1 select_reduce_fusion.1
  40.4 4.7 %all-to-all-done.1.side_i = f32[8,11,4,128]{3,2,1,0:T(4,128)S(1)} async-done(((f32[8,11,4,128]{3,2,1,0:T(4,128)}), f32[8,11,4,128]{3,2,1,0:T(4,128)S(1)}, u32[]{:S(2)}, u32[]{:S(2)}) %all-to-all-start.1) | async-done | bytes 180256 | tf_op jit(solution)/shard_map/all_to_all | solution.py:43
  45.1 1.3 shard_map.96
  46.4 9.1 %all-to-all-start.2 = ((f32[16,9,4,128]{3,2,1,0:T(4,128)}), f32[16,9,4,128]{3,2,1,0:T(4,128)S(1)}, u32[]{:S(2)}, u32[]{:S(2)}) async-start(f32[16,9,4,128]{3,2,1,0:T(4,128)} %shard_map.96), calls=%async_computation.2 | async-start | bytes 589824 | tf_op jit(solution)/shard_map/all_to_all | solution.py:43
  55.6 0.1 convert_element_type.49
  55.7 0.1 convert_element_type.51
  55.7 0.1 add.224
  55.8 0.1 add.225
  56.0 0.1 select_reduce_fusion
  56.1 1.3 concatenate.3.meta
  57.4 9.7 %all-to-all-done.2.side_j = f32[16,9,4,128]{3,2,1,0:T(4,128)S(1)} async-done(((f32[16,9,4,128]{3,2,1,0:T(4,128)}), f32[16,9,4,128]{3,2,1,0:T(4,128)S(1)}, u32[]{:S(2)}, u32[]{:S(2)}) %all-to-all-start.2) | async-done | bytes 294944 | tf_op jit(solution)/shard_map/all_to_all | solution.py:43
  67.1 6.4 %shard_map.98 = (f32[8,64,128]{2,1,0:T(8,128)S(1)}, f32[65,8,128]{2,1,0:T(8,128)S(1)}, f32[129,8,128]{2,1,0:T(8,128)S(1)}, f32[64,128]{1,0:T(8,128)S(1)}) custom-call(s32[132]{0:T(256)S(1)} %concatenate.3.meta, f32[7,8]{1,0:T(8,128)S(1)} %copy-done, f32[8,11,4,128]{3,2,1,0:T(4,128)S(1)} %all-to-all-done.1.side_i, f32[16,9,4,128]{3,2,1,0:T(4,128)S(1)} %all-to-all-done.2.side_j), custom_call_target="tpu_custom_call" | custom-call | tf_op jit(solution)/shard_map/pallas_call | solution.py:47
  73.6 12.0 %all_to_all.35.parts = f32[8,64,128]{2,1,0:T(8,128)S(1)} all-to-all(f32[8,64,128]{2,1,0:T(8,128)S(1)} %get-tuple-element.21), channel_id=1, replica_groups=mesh['zh'=4,'zl'=4,'yh'=2,'core'=2,'x'=4,'yl'=2] {'x','yl'}, dimensions={0} | all-to-all | bytes 524288 | tf_op jit(solution)/shard_map/all_to_all | solution.py:43
  85.6 2.0 %shard_map.99 = (f32[72,128]{1,0:T(8,128)S(1)}, f32[16,2,8,128]{3,2,1,0:T(8,128)}, f32[64,128]{1,0:T(8,128)S(1)}) custom-call(s32[3]{0:T(128)S(1)} %pad_add_fusion.places, f32[7,8]{1,0:T(8,128)S(1)} %copy-done, f32[8,64,128]{2,1,0:T(8,128)S(1)} %all_to_all.35.parts, f32[65,8,128]{2,1,0:T(8,128)S(1)} %get-tuple-element.19.pack_i, ...), custom_call_target="tpu_custom_call" | custom-call | tf_op jit(solution)/shard_map/pallas_call | solution.py:47
  87.6 5.7 %all-to-all-start.4 = ((f32[16,2,8,128]{3,2,1,0:T(8,128)}), f32[16,2,8,128]{3,2,1,0:T(8,128)S(1)}, u32[]{:S(2)}, u32[]{:S(2)}) async-start(f32[16,2,8,128]{3,2,1,0:T(8,128)} %get-tuple-element.24), calls=%async_computation.4 | async-start | bytes 262144 | tf_op jit(solution)/shard_map/all_to_all | solution.py:43
  93.3 1.2 shard_map.100.slopes
  94.5 7.2 %all-to-all-done.4.rad_j = f32[16,2,8,128]{3,2,1,0:T(8,128)S(1)} async-done(((f32[16,2,8,128]{3,2,1,0:T(8,128)}), f32[16,2,8,128]{3,2,1,0:T(8,128)S(1)}, u32[]{:S(2)}, u32[]{:S(2)}) %all-to-all-start.4) | async-done | bytes 131104 | tf_op jit(solution)/shard_map/all_to_all | solution.py:43
  101.7 6.5 %shard_map.101 = f32[8,80,128]{2,1,0:T(8,128)} custom-call(s32[132]{0:T(256)S(1)} %concatenate.3.meta, f32[65,8,128]{2,1,0:T(8,128)S(1)} %get-tuple-element.19.pack_i, f32[129,8,128]{2,1,0:T(8,128)S(1)} %get-tuple-element.20.pack_j, f32[72,128]{1,0:T(8,128)S(1)} %get-tuple-element.23.rad_i.radius, f32[16,2,8,128]{3,2,1,0:T(8,128)S(1)} %all-to-all-done.4.rad_j, ...), custom_call_target="tpu_custom_call" | custom-call | tf_op jit(solution)/shard_map/pallas_call | solution.py:47
  108.1 6.8 %all-to-all-start.5 = ((f32[8,80,128]{2,1,0:T(8,128)}), f32[8,80,128]{2,1,0:T(8,128)S(1)}, u32[]{:S(2)}, u32[]{:S(2)}) async-start(f32[8,80,128]{2,1,0:T(8,128)} %shard_map.101), calls=%async_computation.5 | async-start | bytes 655360 | tf_op jit(solution)/shard_map/all_to_all | solution.py:43
  115.0 0.2 and_select_fusion.3
  115.2 2.7 %shard_map.97.picked = s32[2053]{0:T(1024)S(1)} custom-call(f32[32,128]{1,0:T(8,128)S(1)} %bitcast.14), custom_call_target="tpu_custom_call" | custom-call | tf_op jit(solution)/shard_map/pallas_call | solution.py:47
  117.9 3.6 %all-to-all-done.5.parts = f32[8,80,128]{2,1,0:T(8,128)S(1)} async-done(((f32[8,80,128]{2,1,0:T(8,128)}), f32[8,80,128]{2,1,0:T(8,128)S(1)}, u32[]{:S(2)}, u32[]{:S(2)}) %all-to-all-start.5) | async-done | bytes 327712 | tf_op jit(solution)/shard_map/all_to_all | solution.py:43
  121.6 3.1 %shard_map.102 = (f32[32,3,128]{2,1,0:T(4,128)S(1)}, f32[18,128]{1,0:T(8,128)S(1)}) custom-call(s32[2053]{0:T(1024)S(1)} %shard_map.97.picked, s32[3]{0:T(128)S(1)} %pad_add_fusion.places, f32[65,8,128]{2,1,0:T(8,128)S(1)} %get-tuple-element.19.pack_i, f32[129,8,128]{2,1,0:T(8,128)S(1)} %get-tuple-element.20.pack_j, f32[8,80,128]{2,1,0:T(8,128)S(1)} %all-to-all-done.5.parts, ...), custom_call_target="tpu_custom_call" | custom-call | tf_op jit(solution)/shard_map/pallas_call | solution.py:47
  124.8 12.5 %all_to_all.36 = f32[16,2,3,128]{3,1,2,0:T(2,128)S(1)} all-to-all(f32[16,2,3,128]{3,1,2,0:T(2,128)S(1)} %copy.12), channel_id=1, replica_groups=mesh['zh'=4,'zl'=4,'yh'=2,'core'=2,'x'=4,'yl'=2] {'zl','yh','core'}, dimensions={0} | all-to-all | bytes 98304 | tf_op jit(solution)/shard_map/all_to_all | solution.py:43
  137.2 0.6 shard_map.103
  (22 shorter events, 0.1 us)
Async XLA Ops:
  0.6 0.7 copy-start
  0.6 0.7 copy-start.4
  1.3 0.7 copy-start.1
  2.0 0.7 copy-start.2
  2.7 0.7 copy-start.3
  3.4 0.7 copy-start.5
  4.1 0.7 copy-start.6
  6.1 27.1 %all-to-all-start = ((f32[4,3,4,128]{3,2,1,0:T(4,128)}), f32[4,3,4,128]{3,2,1,0:T(4,128)S(1)}, u32[]{:S(2)}, u32[]{:S(2)}) async-start(f32[4,3,4,128]{3,2,1,0:T(4,128)} %get-tuple-element.18), calls=%async_computation | async-start | bytes 49152 | tf_op jit(solution)/shard_map/all_to_all | solution.py:43
  34.6 10.5 %all-to-all-start.1 = ((f32[8,11,4,128]{3,2,1,0:T(4,128)}), f32[8,11,4,128]{3,2,1,0:T(4,128)S(1)}, u32[]{:S(2)}, u32[]{:S(2)}) async-start(f32[8,11,4,128]{3,2,1,0:T(4,128)} %shard_map.95), calls=%async_computation.1 | async-start | bytes 360448 | tf_op jit(solution)/shard_map/all_to_all | solution.py:43
  46.4 20.7 %all-to-all-start.2 = ((f32[16,9,4,128]{3,2,1,0:T(4,128)}), f32[16,9,4,128]{3,2,1,0:T(4,128)S(1)}, u32[]{:S(2)}, u32[]{:S(2)}) async-start(f32[16,9,4,128]{3,2,1,0:T(4,128)} %shard_map.96), calls=%async_computation.2 | async-start | bytes 589824 | tf_op jit(solution)/shard_map/all_to_all | solution.py:43
  87.6 14.1 %all-to-all-start.4 = ((f32[16,2,8,128]{3,2,1,0:T(8,128)}), f32[16,2,8,128]{3,2,1,0:T(8,128)S(1)}, u32[]{:S(2)}, u32[]{:S(2)}) async-start(f32[16,2,8,128]{3,2,1,0:T(8,128)} %get-tuple-element.24), calls=%async_computation.4 | async-start | bytes 262144 | tf_op jit(solution)/shard_map/all_to_all | solution.py:43
  108.1 13.4 %all-to-all-start.5 = ((f32[8,80,128]{2,1,0:T(8,128)}), f32[8,80,128]{2,1,0:T(8,128)S(1)}, u32[]{:S(2)}, u32[]{:S(2)}) async-start(f32[8,80,128]{2,1,0:T(8,128)} %shard_map.101), calls=%async_computation.5 | async-start | bytes 655360 | tf_op jit(solution)/shard_map/all_to_all | solution.py:43

commit v4 on v3

--- a/solution.py
+++ b/solution.py
@@ -9,7 +9,7 @@
 TILE = 128
 SLOTS = 32
 CHUNK = 32
-UNROLL = 4
+UNROLL = 8
 LISTED = 128
 PICKED = 2048
 
@@ -109,14 +109,58 @@
 
 
 def for_each_tile(meta, first, count, one_tile):
-    def step(k, _):
-        for add in [
-            one_tile(*decoded(meta[first + k * UNROLL + u])) for u in range(UNROLL)
-        ]:
-            add()
-        return 0
-
-    lax.fori_loop(0, (count + UNROLL - 1) // UNROLL, step, 0)
+    def steps(begin, number, width):
+        def step(k, _):
+            at = begin + k * width
+            for add in [one_tile(*decoded(meta[at + u])) for u in range(width)]:
+                add()
+            return 0
+
+        lax.fori_loop(0, number, step, 0)
+
+    half = UNROLL // 2
+    whole = (count + half - 1) // UNROLL
+    steps(first, whole, UNROLL)
+    steps(first + whole * UNROLL, jnp.where(count > whole * UNROLL, 1, 0), half)
+
+
+def typed_spread(table, spread_ref):
+    row = lax.broadcasted_iota(jnp.int32, (48, TILE), 0)
+    for c in range(3):
+        hit = (row % 4 == c) & (row < 12)
+        spread_ref[:, c * TILE : (c + 1) * TILE] = jnp.where(hit, 1.0, 0.0).astype(jnp.bfloat16)
+    kind = (row % 8).astype(F32)
+    rho, scale, neck = looked_up(table, kind, (0, 1, 2))
+    for c, value in enumerate((rho, scale * rho * rho * rho, neck)):
+        high = value.astype(jnp.bfloat16).astype(F32)
+        rest = value - high
+        middle = rest.astype(jnp.bfloat16).astype(F32)
+        part = jnp.where(row < 24, high, jnp.where(row < 32, middle, rest - middle))
+        part = jnp.where((row >= 16) & (row < 40), part, 0.0)
+        spread_ref[:, (3 + c) * TILE : (4 + c) * TILE] = part.astype(jnp.bfloat16)
+
+
+def typed_columns(atoms, spread_ref):
+    high = atoms.astype(jnp.bfloat16).astype(F32)
+    rest = atoms - high
+    middle = rest.astype(jnp.bfloat16).astype(F32)
+    kinds = lax.broadcasted_iota(jnp.int32, (8, TILE), 0).astype(F32)
+    hot = jnp.where(atoms[3:4, :] == kinds, 1.0, 0.0)
+    parts = jnp.concatenate(
+        [high, middle, rest - middle, jnp.zeros((4, TILE), F32), hot, hot, hot, jnp.zeros((8, TILE), F32)],
+        axis=0,
+    )
+    spread = lax.dot_general(
+        parts.astype(jnp.bfloat16),
+        spread_ref[...],
+        (((0,), (0,)), ((), ())),
+        preferred_element_type=F32,
+    )
+    return lambda s, c: spread[s : s + CHUNK, c * TILE : (c + 1) * TILE]
+
+
+def j_atoms(side_j, jb):
+    return side_j[jb // HELD, jb % HELD]
 
 
 def first_kernel(
@@ -159,22 +203,15 @@
         sent_ref[n, 2, 0:2, :] = lists
 
 
-def col_kernel(places, held, sent_ref):
-    lists = held[places[0], 2, 0:2, :]
-    for n in range(N_COLS):
-        for z in range(N_REP):
-            sent_ref[n, 2 * z] = held[z, 0]
-            sent_ref[n, 2 * z + 1] = held[z, 1]
-            at = z % 2 * 2
-            sent_ref[n, 8 + z // 2, at : at + 2, :] = held[z, 2, 2:4, :]
-        sent_ref[n, 10, 0:2, :] = lists
-        sent_ref[n, 10, 2:4, :] = lists
-
-
 def row_kernel(places, side_i, sent_ref):
     rows = [
         jnp.concatenate(
-            [side_i[4 * half + n, 10, r : r + 1, 0:SLOTS] for n in range(4)], axis=1
+            [
+                side_i[4 * half + n, places[0], 2, r : r + 1, 0:SLOTS]
+                for n in range(4)
+            ],
+            axis=1,
+
         )
         for r in range(2)
         for half in range(2)
@@ -182,7 +219,7 @@
     lists = jnp.concatenate(rows, axis=0)
     for n in range(N_ROWS):
         for b in range(HELD):
-            sent_ref[n, b] = side_i[places[2], b]
+            sent_ref[n, b] = side_i[places[2], b // 2, b % 2]
         sent_ref[n, HELD] = lists
 
 
@@ -202,41 +239,37 @@
     picked[PICKED + UNROLL] = count
 
 
-def born_kernel(
-    meta,
-    table,
-    side_i,
-    side_j,
-    out_ref,
-    pack_i,
-    pack_j,
-    charge_i,
-    acc,
-    mask_ref,
-    spread_ref,
-):
+def packed(table, pack, count, more):
+    types = pack[0:count, 3, :]
+    found = looked_up(table, types, (0, 1, 2) + more)
+    rho = found[0]
+    pack[0:count, 3, :] = rho
+    pack[0:count, 4, :] = found[1] * rho * rho * rho
+    pack[0:count, 5, :] = found[2]
+    return rho, found[3:]
+
+
+def pack_kernel(table, side_i, pack_i, charge_i, more_i):
+    for n in range(N_COLS):
+        for z in range(N_REP):
+            at = n * HELD + 2 * z
+            for b in range(2):
+                pack_i[at + b, 0:4, :] = side_i[n, z, b]
+                pack_i[at + b, 4:8, :] = side_i[n, z, b]
+            charge_i[at : at + 2] = side_i[n, z, 2, 2:4, :]
+    pack_i[I_BLOCKS] = jnp.ones((8, TILE), F32)
+    rho, more = packed(table, pack_i, I_BLOCKS, (3, 4, 5))
+    for n, value in enumerate((*more, 1.0 / rho, 1.0 / (rho + OFFSET))):
+        more_i[n] = value
+
+
+def born_kernel(meta, table, pack_i, side_j, out_ref, acc, mask_ref, spread_ref):
     acc[...] = jnp.zeros_like(acc)
     write_mask(mask_ref)
-    write_spread(spread_ref)
-    for side, pack, groups in ((side_i, pack_i, N_COLS), (side_j, pack_j, N_ROWS)):
-        for n in range(groups):
-            here = slice(n * HELD, (n + 1) * HELD)
-            types = side[n, 0:HELD, 3, :]
-            rho, scale, neck = looked_up(table, types, (0, 1, 2))
-            pack[here, 0:3, :] = side[n, 0:HELD, 0:3, :]
-            pack[here, 3, :] = rho
-            pack[here, 4, :] = scale * rho * rho * rho
-            pack[here, 5, :] = neck
-            pack[here, 6, :] = types
-            pack[here, 7, :] = types
-    pack_i[I_BLOCKS] = jnp.ones((8, TILE), F32)
-    pack_j[J_BLOCKS] = jnp.ones((8, TILE), F32)
-    for n in range(N_COLS):
-        charge_i[n * HELD : n * HELD + 4] = side_i[n, 8]
-        charge_i[n * HELD + 4 : (n + 1) * HELD] = side_i[n, 9]
+    typed_spread(table, spread_ref)
 
     def one_tile(ia, jb, same):
-        col = columns(pack_j[jb], spread_ref, 6)
+        col = typed_columns(j_atoms(side_j, jb), spread_ref)
         xi, yi, zi, rho = (pack_i[ia, c : c + 1, :] for c in range(4))
         rho_sq, rho_gap = rho * rho, rho + NECK_GAP
         total = jnp.zeros((8, TILE), F32)
@@ -262,34 +295,40 @@
         out_ref[n] = born
 
 
-def radius_kernel(places, table, parts, pack_i, charge, radius_ref, sent_ref, rate_ref):
-    col_at = places[2]
+def radius_kernel(places, parts, pack_i, more_i, charge, radius_ref, sent_ref, rate_ref):
     born = parts[0]
     for n in range(1, N_COLS):
         born = born + parts[n]
     rho = pack_i[0:I_BLOCKS, 3, :]
-    alpha, beta, gamma = looked_up(table, pack_i[0:I_BLOCKS, 6, :], (3, 4, 5))
+    alpha, beta, gamma, inv_rho, inv_offset = (more_i[n] for n in range(5))
     scaled = rho * born
     poly = alpha * scaled - beta * scaled * scaled + gamma * scaled * scaled * scaled
     squash = jnp.tanh(poly)
-    radius = 1.0 / (1.0 / rho - squash / (rho + OFFSET))
+    radius = 1.0 / (inv_rho - squash * inv_offset)
     slope = alpha - 2.0 * beta * scaled + 3.0 * gamma * scaled * scaled
-    rate_ref[...] = radius * radius * (1.0 - squash * squash) * slope * rho / (rho + OFFSET)
+    rate_ref[...] = radius * radius * (1.0 - squash * squash) * slope * rho * inv_offset
     radius_ref[0:I_BLOCKS] = radius
     radius_ref[I_BLOCKS : I_BLOCKS + 8] = jnp.ones((8, TILE), F32)
-    here = pl.ds(pl.multiple_of(col_at * HELD, HELD), HELD)
+    here = pl.ds(pl.multiple_of(places[2] * HELD, HELD), HELD)
     held, charges = radius_ref[here, :], charge[here, :]
     for n in range(N_ROWS):
         sent_ref[n, 0] = held
         sent_ref[n, 1] = charges
 
 
-def slope_kernel(meta, pack_i, pack_j, out_ref, force, spread_ref):
+def slope_kernel(meta, table, pack_i, side_j, out_ref, own_j, force, spread_ref):
     force[...] = jnp.zeros_like(force)
-    write_spread(spread_ref)
+    typed_spread(table, spread_ref)
+    for n in range(N_ROWS):
+        for b in range(2):
+            block = side_j[n, meta[LISTED + 2] * 2 + b]
+            own_j[2 * n + b, 0:4, :] = block
+            own_j[2 * n + b, 4:8, :] = block
+    own_j[2 * N_ROWS] = jnp.ones((8, TILE), F32)
+    packed(table, own_j, 2 * N_ROWS, ())
 
     def one_tile(ia, jb, same):
-        col = columns(pack_j[jb], spread_ref, 6)
+        col = typed_columns(j_atoms(side_j, jb), spread_ref)
         xi, yi, zi, rho = (pack_i[ia, c : c + 1, :] for c in range(4))
         rho_sq, rho_gap = rho * rho, rho + NECK_GAP
         sums = [jnp.zeros((8, TILE), F32)] * 3
@@ -318,15 +357,16 @@
 
 
 def pair_kernel(
-    meta, pack_i, pack_j, rad_i, rad_j, slopes, out_ref, acc, force, mask_ref, spread_ref, sides
+    meta, pack_i, side_j, rad_i, rad_j, slopes, out_ref, acc, force, mask_ref, spread_ref, sides
 ):
     acc[...] = jnp.zeros_like(acc)
     force[...] = jnp.zeros_like(force)
     write_mask(mask_ref)
     write_spread(spread_ref)
-    sides[...] = pack_j[0:J_BLOCKS]
     for n in range(N_ROWS):
         here = slice(n * HELD, (n + 1) * HELD)
+        sides[here, 0:4, :] = side_j[n, 0:HELD]
+        sides[here, 4:8, :] = side_j[n, 0:HELD]
         sides[here, 3, :] = rad_j[n, 0]
         sides[here, 4, :] = 1.0 / rad_j[n, 0]
         sides[here, 5, :] = rad_j[n, 1]
@@ -376,7 +416,7 @@
 
 
 def chain_kernel(
-    picked, places, pack_i, pack_j, parts, charge, radius, rate, out_ref, own_ref, force, spread_ref, sides
+    picked, places, pack_i, own_j, parts, charge, radius, rate, out_ref, own_ref, force, spread_ref, sides
 ):
     force[...] = jnp.zeros_like(force)
     write_spread(spread_ref)
@@ -394,9 +434,8 @@
         own_ref[16 + b : 17 + b] = sides[first + b, 4:5, :]
 
     def one_tile(at, jb, same):
-        ib = jnp.where(at < 2 * N_ROWS, at // 2 * HELD + places[0] * 2 + at % 2, J_BLOCKS)
         col = columns(sides[jb], spread_ref, 5)
-        xi, yi, zi, rho, vol, neck = (pack_j[ib, c : c + 1, :] for c in range(6))
+        xi, yi, zi, rho, vol, neck = (own_j[at, c : c + 1, :] for c in range(6))
         rho_gap = rho + NECK_GAP
         sums = [jnp.zeros((8, TILE), F32)] * 3
         for s in range(0, TILE, CHUNK):
@@ -491,34 +530,40 @@
             atom_types.reshape(row),
             tile_pairs.reshape(2, SLOTS),
         ],
-        inputs=pl.BlockSpec(memory_space=pl.ANY),
+        inputs=pl.BlockSpec(memory_space=pltpu.HBM),
     )
     held = exchanged(sent, REP)
     meta = tile_codes(held[:, 2, 0:2, 0:SLOTS], rep_at, row_at, col_at)
-    [sent] = called(col_kernel, [(N_COLS, 11, 4, TILE)], [], [places], [held])
-    side_i = exchanged(sent, COLS)
+    side_i = exchanged(jnp.broadcast_to(held, (N_COLS, *held.shape)), COLS)
     [sent] = called(row_kernel, [(N_ROWS, 9, 4, TILE)], [], [places], [side_i])
     side_j = exchanged(sent, ROWS)
 
     mask = ((2, TILE, TILE), F32)
     spread_5, spread_6 = (((32, n * TILE), jnp.bfloat16) for n in (5, 6))
+    typed = ((48, 6 * TILE), jnp.bfloat16)
     sums = ((I_BLOCKS + 1, 8, TILE), F32)
     forces = ((OWN_I + 1, 3, 8, TILE), F32)
-    born_parts, pack_i, pack_j, charge_i = called(
+    pack_i, charge_i, more_i = called(
+        pack_kernel,
+        [(I_BLOCKS + 1, 8, TILE), (I_BLOCKS, TILE), (5, I_BLOCKS, TILE)],
+        [],
+        [table],
+        [side_i],
+    )
+    [born_parts] = called(
         born_kernel,
-        [
-            (N_COLS, I_BLOCKS, TILE),
-            (I_BLOCKS + 1, 8, TILE),
-            (J_BLOCKS + 1, 8, TILE),
-            (I_BLOCKS, TILE),
-        ],
-        [sums, mask, spread_6],
+        [(N_COLS, I_BLOCKS, TILE)],
+        [sums, mask, typed],
         [meta, table],
-        [side_i, side_j],
+        [pack_i, side_j],
     )
     born_parts = exchanged(born_parts, COLS)
-    [slopes] = called(
-        slope_kernel, [(OWN_I, 3, TILE)], [forces, spread_6], [meta], [pack_i, pack_j]
+    slopes, own_j = called(
+        slope_kernel,
+        [(OWN_I, 3, TILE), (2 * N_ROWS + 1, 8, TILE)],
+        [forces, typed],
+        [meta, table],
+        [pack_i, side_j],
     )
     [picked] = called(
         pick_kernel,
@@ -533,8 +578,8 @@
         radius_kernel,
         [(I_BLOCKS + 8, TILE), (N_ROWS, 2, HELD, TILE), (I_BLOCKS, TILE)],
         [],
-        [places, table],
-        [born_parts, pack_i, charge_i],
+        [places],
+        [born_parts, pack_i, more_i, charge_i],
     )
     rad_j = exchanged(sent, ROWS)
     [parts] = called(
@@ -542,7 +587,7 @@
         [(N_COLS, I_BLOCKS + 16, TILE)],
         [sums, forces, mask, spread_6, ((J_BLOCKS, 8, TILE), F32)],
         [meta],
-        [pack_i, pack_j, radius_i, rad_j, slopes],
+        [pack_i, side_j, radius_i, rad_j, slopes],
     )
     parts = exchanged(parts, COLS)
     forces_part, own = called(
@@ -554,7 +599,7 @@
             ((I_BLOCKS, 8, TILE), F32),
         ],
         [picked, places],
-        [pack_i, pack_j, parts, charge_i, radius_i, rate_i],
+        [pack_i, own_j, parts, charge_i, radius_i, rate_i],
     )
     parts = exchanged(forces_part.reshape(N_ROWS, 2, 3, TILE), ROWS)
     new_velocities, new_forces = called(

time: 139 us -> 132 us (0.950)
  waiting for transfers between devices: 36.1 us -> 33.3 us
  starting transfers between devices: 42.4 us -> 39.9 us
  blocking collectives: 24.5 us -> 22.6 us
    all_to_all x5, waiting for transfers between devices: 36.1 us -> 33.3 us  [exchanged(): return lax.all_to_all(pieces, axes, 0, 0, tiled=True)]
    all_to_all x5, starting transfers between devices: 42.4 us -> 39.9 us  [exchanged(): return lax.all_to_all(pieces, axes, 0, 0, tiled=True)]
    all_to_all x2, blocking collectives: 24.5 us -> 22.6 us  [exchanged(): return lax.all_to_all(pieces, axes, 0, 0, tiled=True)]
  transfers between devices with their start and end apart: 5 -> 5, of which waited for: 5 -> 5; matrix products, arithmetic and copies ran while one was open for 2% -> 3% of each run, Pallas kernels for 3% -> 5%
where the time goes in v4:
time: 132 us; the launch traced here: 131 us
  starting transfers between devices  39.9 us (30%)
  waiting for transfers between devices  33.3 us (25%)
  Pallas kernels  25.8 us (20%)
  blocking collectives  22.6 us (17%)
  local copies, waits for them, and re-layouts  7.07 us (5%)
  other arithmetic  1.46 us (1%)
    all_to_all x5, starting transfers between devices, exchanged(): return lax.all_to_all(pieces, axes, 0, 0, tiled=True)  39.9 us
    all_to_all x5, waiting for transfers between devices, exchanged(): return lax.all_to_all(pieces, axes, 0, 0, tiled=True)  33.3 us
    pallas_call x10, Pallas kernels, called(): pl.pallas_call(kernel, out_shape=[jax.ShapeDtypeStruct(s, kind) for s in...  25.8 us
    all_to_all x2, blocking collectives, exchanged(): return lax.all_to_all(pieces, axes, 0, 0, tiled=True)  22.6 us
    unnamed x14, local copies, waits for them, and re-layouts  4.1 us
  transfers between devices with their start and end apart: 5, of which 5 were waited for; matrix products, arithmetic and copies ran while one was open for 3% of the time, Pallas kernels for 5%

profile of v4, /device:TPU:1, one launch (start us, length us, event | category | flops | bytes accessed | tf_op | source)
XLA Modules:
  0.0 130.8 jit_solution(3103445258656308255)
XLA Ops:
  0.6 0.0 copy-start
  0.7 0.7 copy-done
  1.3 0.0 copy-done.4
  1.3 0.7 copy-done.1
  2.0 0.7 copy-done.2
  2.7 0.7 copy-done.3
  3.4 0.7 copy-done.5
  4.1 0.7 copy-done.6
  4.7 1.3 shard_map.94
  6.1 15.6 %all-to-all-start = ((f32[4,3,4,128]{3,2,1,0:T(4,128)}), f32[4,3,4,128]{3,2,1,0:T(4,128)S(1)}, u32[]{:S(2)}, u32[]{:S(2)}) async-start(f32[4,3,4,128]{3,2,1,0:T(4,128)} %get-tuple-element.19), calls=%async_computation | async-start | bytes 49152 | tf_op jit(solution)/shard_map/all_to_all | solution.py:43
  21.7 0.1 eq.62
  21.8 0.1 eq.63
  21.9 0.1 add.230
  22.0 0.1 broadcast_in_dim.64
  22.0 0.1 broadcast_in_dim.65
  22.1 0.1 add.227
  22.2 0.1 pad_add_fusion.places
  22.3 10.9 %all-to-all-done = f32[4,3,4,128]{3,2,1,0:T(4,128)S(1)} async-done(((f32[4,3,4,128]{3,2,1,0:T(4,128)}), f32[4,3,4,128]{3,2,1,0:T(4,128)S(1)}, u32[]{:S(2)}, u32[]{:S(2)}) %all-to-all-start) | async-done | bytes 24608 | tf_op jit(solution)/shard_map/all_to_all | solution.py:43
  33.2 0.2 fusion.5
  33.4 0.7 broadcast_in_dim.62
  34.1 5.0 %all-to-all-start.1 = ((f32[8,4,3,4,128]{4,3,2,1,0:T(4,128)}), f32[8,4,3,4,128]{4,3,2,1,0:T(4,128)S(1)}, u32[]{:S(2)}, u32[]{:S(2)}) async-start(f32[8,4,3,4,128]{4,3,2,1,0:T(4,128)} %broadcast_in_dim.62), calls=%async_computation.1 | async-start | bytes 393216 | tf_op jit(solution)/shard_map/all_to_all | solution.py:43
  39.1 0.7 fusion.12
  39.8 0.1 select_reduce_fusion.1
  39.9 4.7 %all-to-all-done.1.side_i = f32[8,4,3,4,128]{4,3,2,1,0:T(4,128)S(1)} async-done(((f32[8,4,3,4,128]{4,3,2,1,0:T(4,128)}), f32[8,4,3,4,128]{4,3,2,1,0:T(4,128)S(1)}, u32[]{:S(2)}, u32[]{:S(2)}) %all-to-all-start.1) | async-done | bytes 196640 | tf_op jit(solution)/shard_map/all_to_all | solution.py:43
  44.6 1.3 %shard_map.95 = f32[16,9,4,128]{3,2,1,0:T(4,128)} custom-call(s32[3]{0:T(128)S(1)} %pad_add_fusion.places, f32[8,4,3,4,128]{4,3,2,1,0:T(4,128)S(1)} %all-to-all-done.1.side_i), custom_call_target="tpu_custom_call" | custom-call | tf_op jit(solution)/shard_map/pallas_call | solution.py:47
  46.0 9.1 %all-to-all-start.2 = ((f32[16,9,4,128]{3,2,1,0:T(4,128)}), f32[16,9,4,128]{3,2,1,0:T(4,128)S(1)}, u32[]{:S(2)}, u32[]{:S(2)}) async-start(f32[16,9,4,128]{3,2,1,0:T(4,128)} %shard_map.95), calls=%async_computation.2 | async-start | bytes 589824 | tf_op jit(solution)/shard_map/all_to_all | solution.py:43
  55.1 0.1 convert_element_type.49
  55.2 0.1 convert_element_type.51
  55.3 0.1 add.224
  55.3 0.1 add.225
  55.5 0.1 select_reduce_fusion
  55.6 1.4 %concatenate.3.meta = s32[132]{0:T(256)S(1)} concatenate(s32[128]{0:T(128)S(1)} %broadcast_add_fusion, s32[1]{0:T(128)} %bitcast.9, s32[1]{0:T(128)} %bitcast.10, s32[1]{0:T(128)} %bitcast.3, s32[1]{0:T(128)} %bitcast.5), dimensions={0} | concatenate | bytes 1056 | tf_op jit(solution)/shard_map/concatenate | solution.py:510
  57.0 1.8 %shard_map.97 = (f32[65,8,128]{2,1,0:T(8,128)S(1)}, f32[64,128]{1,0:T(8,128)S(1)}, f32[5,64,128]{2,1,0:T(8,128)S(1)}) custom-call(f32[7,8]{1,0:T(8,128)S(1)} %copy-done, f32[8,4,3,4,128]{4,3,2,1,0:T(4,128)S(1)} %all-to-all-done.1.side_i), custom_call_target="tpu_custom_call" | custom-call | tf_op jit(solution)/shard_map/pallas_call | solution.py:47
  58.8 7.9 %all-to-all-done.2.side_j = f32[16,9,4,128]{3,2,1,0:T(4,128)S(1)} async-done(((f32[16,9,4,128]{3,2,1,0:T(4,128)}), f32[16,9,4,128]{3,2,1,0:T(4,128)S(1)}, u32[]{:S(2)}, u32[]{:S(2)}) %all-to-all-start.2) | async-done | bytes 294944 | tf_op jit(solution)/shard_map/all_to_all | solution.py:43
  66.6 5.4 %shard_map.99 = f32[8,64,128]{2,1,0:T(8,128)S(1)} custom-call(s32[132]{0:T(256)S(1)} %concatenate.3.meta, f32[7,8]{1,0:T(8,128)S(1)} %copy-done, f32[65,8,128]{2,1,0:T(8,128)S(1)} %get-tuple-element.20.pack_i, f32[16,9,4,128]{3,2,1,0:T(4,128)S(1)} %all-to-all-done.2.side_j), custom_call_target="tpu_custom_call" | custom-call | tf_op jit(solution)/shard_map/pallas_call | solution.py:47
  72.1 8.5 %all_to_all.35.parts = f32[8,64,128]{2,1,0:T(8,128)S(1)} all-to-all(f32[8,64,128]{2,1,0:T(8,128)S(1)} %shard_map.99), channel_id=1, replica_groups=mesh['zh'=4,'zl'=4,'yh'=2,'core'=2,'x'=4,'yl'=2] {'x','yl'}, dimensions={0} | all-to-all | bytes 524288 | tf_op jit(solution)/shard_map/all_to_all | solution.py:43
  80.6 1.3 shard_map.100
  81.9 6.6 %all-to-all-start.4 = ((f32[16,2,8,128]{3,2,1,0:T(8,128)}), f32[16,2,8,128]{3,2,1,0:T(8,128)S(1)}, u32[]{:S(2)}, u32[]{:S(2)}) async-start(f32[16,2,8,128]{3,2,1,0:T(8,128)} %get-tuple-element.25), calls=%async_computation.4 | async-start | bytes 262144 | tf_op jit(solution)/shard_map/all_to_all | solution.py:43
  88.5 1.9 %shard_map.98 = (f32[16,3,128]{2,1,0:T(4,128)S(1)}, f32[33,8,128]{2,1,0:T(8,128)S(1)}) custom-call(s32[132]{0:T(256)S(1)} %concatenate.3.meta, f32[7,8]{1,0:T(8,128)S(1)} %copy-done, f32[65,8,128]{2,1,0:T(8,128)S(1)} %get-tuple-element.20.pack_i, f32[16,9,4,128]{3,2,1,0:T(4,128)S(1)} %all-to-all-done.2.side_j), custom_call_target="tpu_custom_call" | custom-call | tf_op jit(solution)/shard_map/pallas_call | solution.py:47
  90.4 6.5 %all-to-all-done.4.rad_j = f32[16,2,8,128]{3,2,1,0:T(8,128)S(1)} async-done(((f32[16,2,8,128]{3,2,1,0:T(8,128)}), f32[16,2,8,128]{3,2,1,0:T(8,128)S(1)}, u32[]{:S(2)}, u32[]{:S(2)}) %all-to-all-start.4) | async-done | bytes 131104 | tf_op jit(solution)/shard_map/all_to_all | solution.py:43
  96.9 7.0 %shard_map.101 = f32[8,80,128]{2,1,0:T(8,128)} custom-call(s32[132]{0:T(256)S(1)} %concatenate.3.meta, f32[65,8,128]{2,1,0:T(8,128)S(1)} %get-tuple-element.20.pack_i, f32[16,9,4,128]{3,2,1,0:T(4,128)S(1)} %all-to-all-done.2.side_j, f32[72,128]{1,0:T(8,128)S(1)} %get-tuple-element.24.rad_i.radius, f32[16,2,8,128]{3,2,1,0:T(8,128)S(1)} %all-to-all-done.4.rad_j, ...), custom_call_target="tpu_custom_call" | custom-call | tf_op jit(solution)/shard_map/pallas_call | solution.py:47
  103.9 3.4 %all-to-all-start.5 = ((f32[8,80,128]{2,1,0:T(8,128)}), f32[8,80,128]{2,1,0:T(8,128)S(1)}, u32[]{:S(2)}, u32[]{:S(2)}) async-start(f32[8,80,128]{2,1,0:T(8,128)} %shard_map.101), calls=%async_computation.5 | async-start | bytes 655360 | tf_op jit(solution)/shard_map/all_to_all | solution.py:43
  107.4 0.2 and_select_fusion.3
  107.6 2.4 %shard_map.96.picked = s32[2057]{0:T(1024)S(1)} custom-call(f32[32,128]{1,0:T(8,128)S(1)} %bitcast.14), custom_call_target="tpu_custom_call" | custom-call | tf_op jit(solution)/shard_map/pallas_call | solution.py:47
  110.1 3.3 %all-to-all-done.5.parts = f32[8,80,128]{2,1,0:T(8,128)S(1)} async-done(((f32[8,80,128]{2,1,0:T(8,128)}), f32[8,80,128]{2,1,0:T(8,128)S(1)}, u32[]{:S(2)}, u32[]{:S(2)}) %all-to-all-start.5) | async-done | bytes 327712 | tf_op jit(solution)/shard_map/all_to_all | solution.py:43
  113.3 2.8 %shard_map.102 = (f32[32,3,128]{2,1,0:T(4,128)S(1)}, f32[18,128]{1,0:T(8,128)S(1)}) custom-call(s32[2057]{0:T(1024)S(1)} %shard_map.96.picked, s32[3]{0:T(128)S(1)} %pad_add_fusion.places, f32[65,8,128]{2,1,0:T(8,128)S(1)} %get-tuple-element.20.pack_i, f32[33,8,128]{2,1,0:T(8,128)S(1)} %get-tuple-element.21.own_j, f32[8,80,128]{2,1,0:T(8,128)S(1)} %all-to-all-done.5.parts, ...), custom_call_target="tpu_custom_call" | custom-call | tf_op jit(solution)/shard_map/pallas_call | solution.py:47
  116.1 14.0 %all_to_all.36 = f32[16,2,3,128]{3,1,2,0:T(2,128)S(1)} all-to-all(f32[16,2,3,128]{3,1,2,0:T(2,128)S(1)} %copy.12), channel_id=1, replica_groups=mesh['zh'=4,'zl'=4,'yh'=2,'core'=2,'x'=4,'yl'=2] {'zl','yh','core'}, dimensions={0} | all-to-all | bytes 98304 | tf_op jit(solution)/shard_map/all_to_all | solution.py:43
  130.2 0.6 shard_map.103
  (23 shorter events, 0.1 us)
Async XLA Ops:
  0.6 0.7 copy-start
  0.6 0.7 copy-start.4
  1.3 0.7 copy-start.1
  2.0 0.7 copy-start.2
  2.7 0.7 copy-start.3
  3.4 0.7 copy-start.5
  4.1 0.7 copy-start.6
  6.1 27.1 %all-to-all-start = ((f32[4,3,4,128]{3,2,1,0:T(4,128)}), f32[4,3,4,128]{3,2,1,0:T(4,128)S(1)}, u32[]{:S(2)}, u32[]{:S(2)}) async-start(f32[4,3,4,128]{3,2,1,0:T(4,128)} %get-tuple-element.19), calls=%async_computation | async-start | bytes 49152 | tf_op jit(solution)/shard_map/all_to_all | solution.py:43
  34.1 10.6 %all-to-all-start.1 = ((f32[8,4,3,4,128]{4,3,2,1,0:T(4,128)}), f32[8,4,3,4,128]{4,3,2,1,0:T(4,128)S(1)}, u32[]{:S(2)}, u32[]{:S(2)}) async-start(f32[8,4,3,4,128]{4,3,2,1,0:T(4,128)} %broadcast_in_dim.62), calls=%async_computation.1 | async-start | bytes 393216 | tf_op jit(solution)/shard_map/all_to_all | solution.py:43
  46.0 20.7 %all-to-all-start.2 = ((f32[16,9,4,128]{3,2,1,0:T(4,128)}), f32[16,9,4,128]{3,2,1,0:T(4,128)S(1)}, u32[]{:S(2)}, u32[]{:S(2)}) async-start(f32[16,9,4,128]{3,2,1,0:T(4,128)} %shard_map.95), calls=%async_computation.2 | async-start | bytes 589824 | tf_op jit(solution)/shard_map/all_to_all | solution.py:43
  81.9 15.1 %all-to-all-start.4 = ((f32[16,2,8,128]{3,2,1,0:T(8,128)}), f32[16,2,8,128]{3,2,1,0:T(8,128)S(1)}, u32[]{:S(2)}, u32[]{:S(2)}) async-start(f32[16,2,8,128]{3,2,1,0:T(8,128)} %get-tuple-element.25), calls=%async_computation.4 | async-start | bytes 262144 | tf_op jit(solution)/shard_map/all_to_all | solution.py:43
  103.9 9.4 %all-to-all-start.5 = ((f32[8,80,128]{2,1,0:T(8,128)}), f32[8,80,128]{2,1,0:T(8,128)S(1)}, u32[]{:S(2)}, u32[]{:S(2)}) async-start(f32[8,80,128]{2,1,0:T(8,128)} %shard_map.101), calls=%async_computation.5 | async-start | bytes 655360 | tf_op jit(solution)/shard_map/all_to_all | solution.py:43

commit v5 on v4

--- a/solution.py
+++ b/solution.py
@@ -32,7 +32,6 @@
 HELD = 2 * N_REP
 I_BLOCKS = N_COLS * HELD
 J_BLOCKS = N_ROWS * HELD
-OWN_I = 2 * N_COLS
 
 VMEM = pl.BlockSpec(memory_space=pltpu.VMEM)
 SMEM = pl.BlockSpec(memory_space=pltpu.SMEM)
@@ -163,37 +162,16 @@
     return side_j[jb // HELD, jb % HELD]
 
 
-def first_kernel(
-    table, pos_in, vel_in, old_in, charge_in, kinds_in, pairs_in, new_ref, sent_ref, kept_ref,
-    pos, vel, old, charge, kinds, pairs, sems
-):
-    copies = [
-        pltpu.make_async_copy(there, here, sems.at[n])
-        for n, (there, here) in enumerate(
-            (
-                (pos_in, pos),
-                (vel_in, vel),
-                (old_in, old),
-                (charge_in, charge),
-                (kinds_in, kinds),
-                (pairs_in, pairs),
-            )
-        )
-    ]
-    for copy in copies:
-        copy.start()
-    for copy in copies:
-        copy.wait()
-    types = kinds[...].astype(F32)
+def first_kernel(table, joined, new_ref, sent_ref, kept_ref):
+    pos, vel, old = joined[0:3], joined[3:6], joined[6:9]
+    charge, types, lists = joined[9:10], joined[10:11], joined[11:13, 0:TILE]
     [mass] = looked_up(table, types, (6,))
-    new = pos[...] + TIMESTEP * vel[...] + TIMESTEP * TIMESTEP / (2.0 * mass) * old[...]
+    new = pos + TIMESTEP * vel + TIMESTEP * TIMESTEP / (2.0 * mass) * old
     scale = TIMESTEP / (2.0 * mass)
     new_ref[...] = new
-    kept_ref[0:3] = vel[...] + scale * old[...]
+    kept_ref[0:3] = vel + scale * old
     kept_ref[3:4] = scale
-    kept_ref[4:5] = charge[...]
-    lists = pairs[...].astype(F32)
-    lists = jnp.concatenate([lists, jnp.zeros((2, TILE - SLOTS), F32)], axis=1)
+    kept_ref[4:5] = charge
     for n in range(N_REP):
         for b in range(2):
             here = slice(b * TILE, (b + 1) * TILE)
@@ -289,13 +267,12 @@
         return add
 
     for_each_tile(meta, 0, meta[LISTED], one_tile)
-    for_each_tile(meta, SLOTS, meta[LISTED + 1], one_tile)
     born = jnp.sum(acc[0:I_BLOCKS], axis=1)
     for n in range(N_COLS):
         out_ref[n] = born
 
 
-def radius_kernel(places, parts, pack_i, more_i, charge, radius_ref, sent_ref, rate_ref):
+def radius_kernel(places, parts, pack_i, more_i, charge, ready, radius_ref, sent_ref, rate_ref):
     born = parts[0]
     for n in range(1, N_COLS):
         born = born + parts[n]
@@ -316,20 +293,20 @@
         sent_ref[n, 1] = charges
 
 
-def slope_kernel(meta, table, pack_i, side_j, out_ref, own_j, force, spread_ref):
+def slope_kernel(picked, places, table, pack_i, side_j, out_ref, own_j, force, spread_ref):
     force[...] = jnp.zeros_like(force)
-    typed_spread(table, spread_ref)
+    write_spread(spread_ref)
     for n in range(N_ROWS):
         for b in range(2):
-            block = side_j[n, meta[LISTED + 2] * 2 + b]
+            block = side_j[n, places[0] * 2 + b]
             own_j[2 * n + b, 0:4, :] = block
             own_j[2 * n + b, 4:8, :] = block
     own_j[2 * N_ROWS] = jnp.ones((8, TILE), F32)
     packed(table, own_j, 2 * N_ROWS, ())
 
-    def one_tile(ia, jb, same):
-        col = typed_columns(j_atoms(side_j, jb), spread_ref)
-        xi, yi, zi, rho = (pack_i[ia, c : c + 1, :] for c in range(4))
+    def one_tile(at, jb, same):
+        col = columns(pack_i[jb], spread_ref, 6)
+        xi, yi, zi, rho = (own_j[at, c : c + 1, :] for c in range(4))
         rho_sq, rho_gap = rho * rho, rho + NECK_GAP
         sums = [jnp.zeros((8, TILE), F32)] * 3
         for s in range(0, TILE, CHUNK):
@@ -346,21 +323,58 @@
             sums = [a + folded(slope * d) for a, d in zip(sums, (dx, dy, dz))]
 
         def add():
-            at = ia // HELD * 2 + ia % 2
             for c in range(3):
                 force[at, c] += sums[c]
 
         return add
 
-    for_each_tile(meta, 0, meta[LISTED], one_tile)
-    out_ref[...] = jnp.sum(force[0:OWN_I], axis=2)
+    for_each_tile(picked, 0, picked[PICKED + UNROLL], one_tile)
+    out_ref[...] = jnp.sum(force[0 : 2 * N_ROWS], axis=2)
+
+
+def direct_kernel(
+    picked, places, own_j, pack_i, rad_j, radius_i, charge_i, out_ref, force, spread_ref, sides, own
+):
+    force[...] = jnp.zeros_like(force)
+    write_spread(spread_ref)
+    sides[...] = pack_i[0:I_BLOCKS]
+    radii = radius_i[0:I_BLOCKS]
+    sides[:, 3, :] = radii
+    sides[:, 4, :] = 1.0 / radii
+    sides[:, 5, :] = charge_i[...]
+    own[...] = jnp.ones_like(own)
+    for n in range(N_ROWS):
+        own[2 * n : 2 * n + 2] = rad_j[n, 0, pl.ds(places[0] * 2, 2), :]
+
+    def one_tile(at, jb, same):
+        col = columns(sides[jb], spread_ref, 6)
+        xi, yi, zi = (own_j[at, c : c + 1, :] for c in range(3))
+        radius = own[pl.ds(at, 1), :]
+        quarter = 0.25 / radius
+        sums = [jnp.zeros((8, TILE), F32)] * 3
+        for s in range(0, TILE, CHUNK):
+            dx, dy, dz, q = offsets(xi, yi, zi, col, s)
+            base = jnp.maximum(1.0 - q * INV_SQ, 0.0)
+            decay = jnp.exp2(q * (quarter * col(s, 4)) * -LOG2E)
+            inv = lax.rsqrt(q + radius * col(s, 3) * decay)
+            slope = (-2.0 * INV_SQ) * base - base * base * (inv * inv) * (0.5 - 0.125 * decay)
+            slope = slope * (inv * col(s, 5))
+            sums = [a + folded(slope * d) for a, d in zip(sums, (dx, dy, dz))]
+
+        def add():
+            for c in range(3):
+                force[at, c] += sums[c]
+
+        return add
+
+    for_each_tile(picked, 0, picked[PICKED + UNROLL], one_tile)
+    out_ref[...] = jnp.sum(force[0 : 2 * N_ROWS], axis=2)
 
 
 def pair_kernel(
-    meta, pack_i, side_j, rad_i, rad_j, slopes, out_ref, acc, force, mask_ref, spread_ref, sides
+    meta, pack_i, side_j, rad_i, rad_j, ready, out_ref, acc, mask_ref, spread_ref, sides
 ):
     acc[...] = jnp.zeros_like(acc)
-    force[...] = jnp.zeros_like(force)
     write_mask(mask_ref)
     write_spread(spread_ref)
     for n in range(N_ROWS):
@@ -371,15 +385,14 @@
         sides[here, 4, :] = 1.0 / rad_j[n, 0]
         sides[here, 5, :] = rad_j[n, 1]
 
-    def one_tile(ia, jb, same, with_force):
+    def one_tile(ia, jb, same):
         col = columns(sides[jb], spread_ref, 6)
         xi, yi, zi = (pack_i[ia, c : c + 1, :] for c in range(3))
         radius_i = rad_i[pl.ds(ia, 1), :]
         quarter_i = 0.25 / radius_i
         total = jnp.zeros((8, TILE), F32)
-        sums = [jnp.zeros((8, TILE), F32)] * 3
         for s in range(0, TILE, CHUNK):
-            dx, dy, dz, q = offsets(xi, yi, zi, col, s)
+            _, _, _, q = offsets(xi, yi, zi, col, s)
             base = jnp.maximum(1.0 - q * INV_SQ, 0.0)
             weight = base * base * mask_ref[same, s : s + CHUNK, :]
             arg = q * (quarter_i * col(s, 4))
@@ -387,36 +400,20 @@
             inv = lax.rsqrt(q + radius_i * col(s, 3) * decay)
             weighted = weight * col(s, 5) * (inv * inv * inv)
             total += folded(weighted * col(s, 3) * (decay * (1.0 + arg)))
-            if with_force:
-                slope = (-2.0 * INV_SQ) * base * col(s, 5) * inv - weighted * (
-                    0.5 - 0.125 * decay
-                )
-                sums = [a + folded(slope * d) for a, d in zip(sums, (dx, dy, dz))]
 
         def add():
             acc[ia] += total
-            if with_force:
-                at = ia // HELD * 2 + ia % 2
-                for c in range(3):
-                    force[at, c] += sums[c]
 
         return add
 
-    for_each_tile(meta, 0, meta[LISTED], lambda *a: one_tile(*a, True))
-    for_each_tile(meta, SLOTS, meta[LISTED + 1], lambda *a: one_tile(*a, False))
+    for_each_tile(meta, 0, meta[LISTED], one_tile)
     grads = jnp.sum(acc[0:I_BLOCKS], axis=1)
-    direct = jnp.sum(force[0:OWN_I], axis=2)
     for n in range(N_COLS):
-        out_ref[n, 0:I_BLOCKS] = grads
-        for b in range(2):
-            at = I_BLOCKS + 8 * b
-            out_ref[n, at : at + 3, :] = direct[2 * n + b]
-            out_ref[n, at + 3 : at + 6, :] = slopes[2 * n + b]
-            out_ref[n, at + 6 : at + 8, :] = slopes[2 * n + b, 0:2, :]
+        out_ref[n] = grads
 
 
 def chain_kernel(
-    picked, places, pack_i, own_j, parts, charge, radius, rate, out_ref, own_ref, force, spread_ref, sides
+    picked, places, pack_i, own_j, parts, charge, radius, rate, direct, slopes, out_ref, own_ref, force, spread_ref, sides
 ):
     force[...] = jnp.zeros_like(force)
     write_spread(spread_ref)
@@ -424,14 +421,13 @@
     for n in range(1, N_COLS):
         total = total + parts[n]
     charges, radii = charge[...], radius[0:I_BLOCKS]
-    grad = -0.5 * charges * total[0:I_BLOCKS]
+    grad = -0.5 * charges * total
     chain = (COULOMB * charges * charges / (2.0 * radii * radii) - COULOMB * grad) * rate[...]
     sides[...] = pack_i[0:I_BLOCKS]
     sides[:, 4, :] = chain
     first = places[2] * HELD + places[0] * 2
-    own_ref[0:16] = total[I_BLOCKS : I_BLOCKS + 16]
     for b in range(2):
-        own_ref[16 + b : 17 + b] = sides[first + b, 4:5, :]
+        own_ref[b : b + 1] = sides[first + b, 4:5, :]
 
     def one_tile(at, jb, same):
         col = columns(sides[jb], spread_ref, 5)
@@ -460,17 +456,24 @@
         return add
 
     for_each_tile(picked, 0, picked[PICKED + UNROLL], one_tile)
-    out_ref[...] = jnp.sum(force[0 : 2 * N_ROWS], axis=2)
+    chained = jnp.sum(force[0 : 2 * N_ROWS], axis=2)
+    for n in range(N_ROWS):
+        for b in range(2):
+            at = 2 * n + b
+            for c, value in enumerate((chained, direct, slopes)):
+                out_ref[n, 12 * b + 4 * c : 12 * b + 4 * c + 3, :] = value[at]
+                out_ref[n, 12 * b + 4 * c + 3 : 12 * b + 4 * c + 4, :] = value[at, 0:1, :]
 
 
 def last_kernel(parts, own, kept, vel_ref, force_ref):
+    total = parts[0]
+    for n in range(1, N_ROWS):
+        total = total + parts[n]
     for b in range(2):
         here = slice(b * TILE, (b + 1) * TILE)
-        total = parts[0, b]
-        for n in range(1, N_ROWS):
-            total = total + parts[n, b]
-        force = (2.0 * COULOMB) * kept[4:5, here] * own[8 * b : 8 * b + 3, :] - 2.0 * (
-            total + own[16 + b : 17 + b, :] * own[8 * b + 3 : 8 * b + 6, :]
+        chained, direct, slopes = (total[12 * b + 4 * c : 12 * b + 4 * c + 3] for c in range(3))
+        force = (2.0 * COULOMB) * kept[4:5, here] * direct - 2.0 * (
+            chained + own[b : b + 1, :] * slopes
         )
         force_ref[:, here] = force
         vel_ref[:, here] = kept[0:3, here] + kept[3:4, here] * force
@@ -487,7 +490,7 @@
     return jnp.where(mine, key.astype(F32), NO_KEY).reshape(2 * N_ROWS, TILE)
 
 
-def tile_codes(lists, rep_at, row_at, col_at):
+def tile_codes(lists, row_at, col_at):
     list_a, list_g = lists[:, 0].astype(jnp.int32), lists[:, 1].astype(jnp.int32)
     reps = jnp.arange(N_REP, dtype=jnp.int32)[:, None]
     live = list_a >= 0
@@ -497,17 +500,13 @@
     place_j = (j_row % N_ROWS * N_REP + j_row // N_ROWS) * 2 + list_g % 2
     same = (j_row == reps * N_ROWS + row_at) & (list_a == col_at * 2 + list_g % 2)
     none = I_BLOCKS * 256
-    codes = jnp.where(live, place_i * 256 + place_j * 2 + same.astype(jnp.int32) - none, 0)
-    other = jnp.arange(N_REP) != rep_at
-    counted = jnp.where(other, counts, 0)
-    before = jnp.sum(jnp.where(jnp.arange(N_REP)[:, None] < reps.T, counted[:, None], 0), axis=0)
-    slot = jnp.arange(SLOTS, dtype=jnp.int32)[None, :]
-    target = jnp.where(other[:, None], SLOTS + before[:, None] + slot, slot)
-    hit = (target.reshape(1, LISTED) == jnp.arange(LISTED, dtype=jnp.int32)[:, None]) & live.reshape(1, LISTED)
+    codes = place_i * 256 + place_j * 2 + same.astype(jnp.int32) - none
+    before = jnp.sum(jnp.where(reps < reps.T, counts[:, None], 0), axis=0)
+    target = before[:, None] + jnp.arange(SLOTS, dtype=jnp.int32)[None, :]
+    target = jnp.where(live, target, -1).reshape(1, LISTED)
+    hit = target == jnp.arange(LISTED, dtype=jnp.int32)[:, None]
     placed = none + jnp.sum(jnp.where(hit, codes.reshape(1, LISTED), 0), axis=1)
-    own = jnp.sum(jnp.where(other, 0, counts))
-    tail = jnp.stack([own, jnp.sum(counted), rep_at, col_at]).astype(jnp.int32)
-    return jnp.concatenate([placed, tail])
+    return jnp.concatenate([placed, jnp.sum(counts)[None]]).astype(jnp.int32)
 
 
 def body(positions, velocities, old_forces, charges, atom_types, table, tile_pairs):
@@ -516,24 +515,26 @@
     col_at = lax.axis_index(COLS)
     places = jnp.stack([rep_at, row_at, col_at]).astype(jnp.int32)
     row = (1, 2 * TILE)
-    new_positions, sent, kept = called(
-        first_kernel,
-        [(3, 2 * TILE), (N_REP, 3, 4, TILE), (5, 2 * TILE)],
-        [((3, 2 * TILE), F32)] * 3
-        + [(row, F32), (row, jnp.int32), ((2, SLOTS), jnp.int32), pltpu.SemaphoreType.DMA((6,))],
-        [table],
+    joined = jnp.concatenate(
         [
             positions,
             velocities,
             old_forces,
             charges.reshape(row),
-            atom_types.reshape(row),
-            tile_pairs.reshape(2, SLOTS),
+            atom_types.reshape(row).astype(F32),
+            jnp.pad(tile_pairs.reshape(2, SLOTS).astype(F32), ((0, 0), (0, 2 * TILE - SLOTS))),
         ],
-        inputs=pl.BlockSpec(memory_space=pltpu.HBM),
+        axis=0,
+    )
+    new_positions, sent, kept = called(
+        first_kernel,
+        [(3, 2 * TILE), (N_REP, 3, 4, TILE), (5, 2 * TILE)],
+        [],
+        [table],
+        [joined],
     )
     held = exchanged(sent, REP)
-    meta = tile_codes(held[:, 2, 0:2, 0:SLOTS], rep_at, row_at, col_at)
+    meta = tile_codes(held[:, 2, 0:2, 0:SLOTS], row_at, col_at)
     side_i = exchanged(jnp.broadcast_to(held, (N_COLS, *held.shape)), COLS)
     [sent] = called(row_kernel, [(N_ROWS, 9, 4, TILE)], [], [places], [side_i])
     side_j = exchanged(sent, ROWS)
@@ -542,7 +543,8 @@
     spread_5, spread_6 = (((32, n * TILE), jnp.bfloat16) for n in (5, 6))
     typed = ((48, 6 * TILE), jnp.bfloat16)
     sums = ((I_BLOCKS + 1, 8, TILE), F32)
-    forces = ((OWN_I + 1, 3, 8, TILE), F32)
+    forces = ((2 * N_ROWS + 1, 3, 8, TILE), F32)
+    held_sides = ((I_BLOCKS, 8, TILE), F32)
     pack_i, charge_i, more_i = called(
         pack_kernel,
         [(I_BLOCKS + 1, 8, TILE), (I_BLOCKS, TILE), (5, I_BLOCKS, TILE)],
@@ -558,13 +560,6 @@
         [pack_i, side_j],
     )
     born_parts = exchanged(born_parts, COLS)
-    slopes, own_j = called(
-        slope_kernel,
-        [(OWN_I, 3, TILE), (2 * N_ROWS + 1, 8, TILE)],
-        [forces, typed],
-        [meta, table],
-        [pack_i, side_j],
-    )
     [picked] = called(
         pick_kernel,
         [(PICKED + UNROLL + 1,)],
@@ -579,29 +574,39 @@
         [(I_BLOCKS + 8, TILE), (N_ROWS, 2, HELD, TILE), (I_BLOCKS, TILE)],
         [],
         [places],
-        [born_parts, pack_i, more_i, charge_i],
+        [born_parts, pack_i, more_i, charge_i, picked],
     )
     rad_j = exchanged(sent, ROWS)
-    [parts] = called(
+    slopes, own_j = called(
+        slope_kernel,
+        [(2 * N_ROWS, 3, TILE), (2 * N_ROWS + 1, 8, TILE)],
+        [forces, spread_6],
+        [picked, places, table],
+        [pack_i, side_j],
+    )
+    [grads] = called(
         pair_kernel,
-        [(N_COLS, I_BLOCKS + 16, TILE)],
-        [sums, forces, mask, spread_6, ((J_BLOCKS, 8, TILE), F32)],
+        [(N_COLS, I_BLOCKS, TILE)],
+        [sums, mask, spread_6, ((J_BLOCKS, 8, TILE), F32)],
         [meta],
         [pack_i, side_j, radius_i, rad_j, slopes],
     )
-    parts = exchanged(parts, COLS)
-    forces_part, own = called(
+    grads = exchanged(grads, COLS)
+    [direct] = called(
+        direct_kernel,
+        [(2 * N_ROWS, 3, TILE)],
+        [forces, spread_6, held_sides, ((2 * N_ROWS + 8, TILE), F32)],
+        [picked, places],
+        [own_j, pack_i, rad_j, radius_i, charge_i],
+    )
+    parts, own = called(
         chain_kernel,
-        [(2 * N_ROWS, 3, TILE), (18, TILE)],
-        [
-            ((2 * N_ROWS + 1, 3, 8, TILE), F32),
-            spread_5,
-            ((I_BLOCKS, 8, TILE), F32),
-        ],
+        [(N_ROWS, 24, TILE), (2, TILE)],
+        [forces, spread_5, held_sides],
         [picked, places],
-        [pack_i, own_j, parts, charge_i, radius_i, rate_i],
-    )
-    parts = exchanged(forces_part.reshape(N_ROWS, 2, 3, TILE), ROWS)
+        [pack_i, own_j, grads, charge_i, radius_i, rate_i, direct, slopes],
+    )
+    parts = exchanged(parts, ROWS)
     new_velocities, new_forces = called(
         last_kernel, [(3, 2 * TILE), (3, 2 * TILE)], [], [], [parts, own, kept]
     )

time: 132 us -> 134 us (1.015)
  starting transfers between devices: 39.9 us -> 45.7 us
  blocking collectives: 22.6 us -> 17.7 us
  local copies, waits for them, and re-layouts: 7.07 us -> 2.72 us
  waiting for transfers between devices: 33.3 us -> 37.1 us
    all_to_all x5 -> x6, starting transfers between devices: 39.9 us -> 45.7 us  [exchanged(): return lax.all_to_all(pieces, axes, 0, 0, tiled=True)]
    all_to_all x2 -> x1, blocking collectives: 22.6 us -> 17.7 us  [exchanged(): return lax.all_to_all(pieces, axes, 0, 0, tiled=True)]
    all_to_all x5 -> x6, waiting for transfers between devices: 33.3 us -> 37.1 us  [exchanged(): return lax.all_to_all(pieces, axes, 0, 0, tiled=True)]
    unnamed x14 -> x10, local copies, waits for them, and re-layouts: 4.1 us -> 0.69 us
    pallas_call x10 -> x11, Pallas kernels: 25.8 us -> 26.9 us  [called(): pl.pallas_call(kernel, out_shape=[jax.ShapeDtypeStruct(s, kind) for s in...]
  transfers between devices with their start and end apart: 5 -> 6, of which waited for: 5 -> 6; matrix products, arithmetic and copies ran while one was open for 3% -> 2% of each run, Pallas kernels for 5% -> 7%
where the time goes in v5:
time: 134 us
  starting transfers between devices  45.7 us (34%)
  waiting for transfers between devices  37.1 us (28%)
  Pallas kernels  26.9 us (20%)
  blocking collectives  17.7 us (13%)
  local copies, waits for them, and re-layouts  2.72 us (2%)
  other arithmetic  2.61 us (2%)
    all_to_all x6, starting transfers between devices, exchanged(): return lax.all_to_all(pieces, axes, 0, 0, tiled=True)  45.7 us
    all_to_all x6, waiting for transfers between devices, exchanged(): return lax.all_to_all(pieces, axes, 0, 0, tiled=True)  37.1 us
    pallas_call x11, Pallas kernels, called(): pl.pallas_call(kernel, out_shape=[jax.ShapeDtypeStruct(s, kind) for s in...  26.9 us
    all_to_all x1, blocking collectives, exchanged(): return lax.all_to_all(pieces, axes, 0, 0, tiled=True)  17.7 us
  transfers between devices with their start and end apart: 6, of which 6 were waited for; matrix products, arithmetic and copies ran while one was open for 2% of the time, Pallas kernels for 7%

profile of v5, /device:TPU:1, one launch (start us, length us, event | category | flops | bytes accessed | tf_op | source)
XLA Modules:
  0.0 133.6 jit_solution(17675424033199756840)
XLA Ops:
  0.6 0.0 copy-start.4
  0.6 0.7 convert_bitcast_fusion
  1.3 0.0 copy-done.4
  1.3 0.0 copy-start.1
  1.4 0.0 copy-start.3
  1.4 0.6 copy-done.2
  2.0 0.0 copy-done.1
  2.0 0.0 copy-done.3
  2.0 0.8 concatenate.6.joined
  2.9 0.0 copy-done
  2.9 1.2 shard_map.94
  4.1 15.6 %all-to-all-start = ((f32[4,3,4,128]{3,2,1,0:T(4,128)}), f32[4,3,4,128]{3,2,1,0:T(4,128)S(1)}, u32[]{:S(2)}, u32[]{:S(2)}) async-start(f32[4,3,4,128]{3,2,1,0:T(4,128)} %get-tuple-element.19), calls=%async_computation | async-start | bytes 49152 | tf_op jit(solution)/shard_map/all_to_all | solution.py:42
  19.8 0.1 eq.62
  19.9 0.1 eq.63
  20.0 0.1 add.217
  20.0 0.1 pad_add_fusion.1.places
  20.1 11.1 %all-to-all-done = f32[4,3,4,128]{3,2,1,0:T(4,128)S(1)} async-done(((f32[4,3,4,128]{3,2,1,0:T(4,128)}), f32[4,3,4,128]{3,2,1,0:T(4,128)S(1)}, u32[]{:S(2)}, u32[]{:S(2)}) %all-to-all-start) | async-done | bytes 24608 | tf_op jit(solution)/shard_map/all_to_all | solution.py:42
  31.2 0.7 broadcast_in_dim.41
  31.9 5.0 %all-to-all-start.1 = ((f32[8,4,3,4,128]{4,3,2,1,0:T(4,128)}), f32[8,4,3,4,128]{4,3,2,1,0:T(4,128)S(1)}, u32[]{:S(2)}, u32[]{:S(2)}) async-start(f32[8,4,3,4,128]{4,3,2,1,0:T(4,128)} %broadcast_in_dim.41), calls=%async_computation.1 | async-start | bytes 393216 | tf_op jit(solution)/shard_map/all_to_all | solution.py:42
  36.9 5.5 %all-to-all-done.1.side_i = f32[8,4,3,4,128]{4,3,2,1,0:T(4,128)S(1)} async-done(((f32[8,4,3,4,128]{4,3,2,1,0:T(4,128)}), f32[8,4,3,4,128]{4,3,2,1,0:T(4,128)S(1)}, u32[]{:S(2)}, u32[]{:S(2)}) %all-to-all-start.1) | async-done | bytes 196640 | tf_op jit(solution)/shard_map/all_to_all | solution.py:42
  42.5 1.4 %shard_map.95 = f32[16,9,4,128]{3,2,1,0:T(4,128)} custom-call(s32[3]{0:T(128)S(1)} %pad_add_fusion.1.places, f32[8,4,3,4,128]{4,3,2,1,0:T(4,128)S(1)} %all-to-all-done.1.side_i), custom_call_target="tpu_custom_call" | custom-call | tf_op jit(solution)/shard_map/pallas_call | solution.py:46
  43.8 9.1 %all-to-all-start.2 = ((f32[16,9,4,128]{3,2,1,0:T(4,128)}), f32[16,9,4,128]{3,2,1,0:T(4,128)S(1)}, u32[]{:S(2)}, u32[]{:S(2)}) async-start(f32[16,9,4,128]{3,2,1,0:T(4,128)} %shard_map.95), calls=%async_computation.2 | async-start | bytes 589824 | tf_op jit(solution)/shard_map/all_to_all | solution.py:42
  53.0 0.7 fusion.12
  53.7 0.1 select_reduce_fusion.1
  53.8 0.1 iota_add_fusion
  53.8 0.1 add.215
  53.9 0.1 convert_element_type.66
  54.0 0.1 convert_element_type.69
  54.1 0.1 select_reduce_fusion
  54.2 0.6 pad_add_fusion.meta
  54.8 1.8 %shard_map.97 = (f32[65,8,128]{2,1,0:T(8,128)S(1)}, f32[64,128]{1,0:T(8,128)S(1)}, f32[5,64,128]{2,1,0:T(8,128)S(1)}) custom-call(f32[7,8]{1,0:T(8,128)S(1)} %copy-done, f32[8,4,3,4,128]{4,3,2,1,0:T(4,128)S(1)} %all-to-all-done.1.side_i), custom_call_target="tpu_custom_call" | custom-call | tf_op jit(solution)/shard_map/pallas_call | solution.py:46
  56.6 7.9 %all-to-all-done.2.side_j = f32[16,9,4,128]{3,2,1,0:T(4,128)S(1)} async-done(((f32[16,9,4,128]{3,2,1,0:T(4,128)}), f32[16,9,4,128]{3,2,1,0:T(4,128)S(1)}, u32[]{:S(2)}, u32[]{:S(2)}) %all-to-all-start.2) | async-done | bytes 294944 | tf_op jit(solution)/shard_map/all_to_all | solution.py:42
  64.5 5.4 %shard_map.99 = f32[8,64,128]{2,1,0:T(8,128)} custom-call(s32[129]{0:T(256)S(1)} %pad_add_fusion.meta, f32[7,8]{1,0:T(8,128)S(1)} %copy-done, f32[65,8,128]{2,1,0:T(8,128)S(1)} %get-tuple-element.20.pack_i, f32[16,9,4,128]{3,2,1,0:T(4,128)S(1)} %all-to-all-done.2.side_j), custom_call_target="tpu_custom_call" | custom-call | tf_op jit(solution)/shard_map/pallas_call | solution.py:46
  69.9 3.4 %all-to-all-start.3 = ((f32[8,64,128]{2,1,0:T(8,128)}), f32[8,64,128]{2,1,0:T(8,128)S(1)}, u32[]{:S(2)}, u32[]{:S(2)}) async-start(f32[8,64,128]{2,1,0:T(8,128)} %shard_map.99), calls=%async_computation.3 | async-start | bytes 524288 | tf_op jit(solution)/shard_map/all_to_all | solution.py:42
  73.3 0.2 and_select_fusion.3
  73.6 2.2 %shard_map.96.picked.ready = s32[2057]{0:T(1024)S(1)} custom-call(f32[32,128]{1,0:T(8,128)S(1)} %bitcast.13), custom_call_target="tpu_custom_call" | custom-call | tf_op jit(solution)/shard_map/pallas_call | solution.py:46
  75.8 3.3 %all-to-all-done.3.parts = f32[8,64,128]{2,1,0:T(8,128)S(1)} async-done(((f32[8,64,128]{2,1,0:T(8,128)}), f32[8,64,128]{2,1,0:T(8,128)S(1)}, u32[]{:S(2)}, u32[]{:S(2)}) %all-to-all-start.3) | async-done | bytes 262176 | tf_op jit(solution)/shard_map/all_to_all | solution.py:42
  79.0 1.3 shard_map.100
  80.3 8.6 %all-to-all-start.4 = ((f32[16,2,8,128]{3,2,1,0:T(8,128)}), f32[16,2,8,128]{3,2,1,0:T(8,128)S(1)}, u32[]{:S(2)}, u32[]{:S(2)}) async-start(f32[16,2,8,128]{3,2,1,0:T(8,128)} %get-tuple-element.25), calls=%async_computation.4 | async-start | bytes 262144 | tf_op jit(solution)/shard_map/all_to_all | solution.py:42
  88.9 2.6 %shard_map.98 = (f32[32,3,128]{2,1,0:T(4,128)S(1)}, f32[33,8,128]{2,1,0:T(8,128)S(1)}) custom-call(s32[2057]{0:T(1024)S(1)} %shard_map.96.picked.ready, s32[3]{0:T(128)S(1)} %pad_add_fusion.1.places, f32[7,8]{1,0:T(8,128)S(1)} %copy-done, f32[65,8,128]{2,1,0:T(8,128)S(1)} %get-tuple-element.20.pack_i, f32[16,9,4,128]{3,2,1,0:T(4,128)S(1)} %all-to-all-done.2.side_j), custom_call_target="tpu_custom_call" | custom-call | tf_op jit(solution)/shard_map/pallas_call | solution.py:46
  91.5 5.9 %all-to-all-done.4.rad_j = f32[16,2,8,128]{3,2,1,0:T(8,128)S(1)} async-done(((f32[16,2,8,128]{3,2,1,0:T(8,128)}), f32[16,2,8,128]{3,2,1,0:T(8,128)S(1)}, u32[]{:S(2)}, u32[]{:S(2)}) %all-to-all-start.4) | async-done | bytes 131104 | tf_op jit(solution)/shard_map/all_to_all | solution.py:42
  97.3 5.8 %shard_map.101 = f32[8,64,128]{2,1,0:T(8,128)} custom-call(s32[129]{0:T(256)S(1)} %pad_add_fusion.meta, f32[65,8,128]{2,1,0:T(8,128)S(1)} %get-tuple-element.20.pack_i, f32[16,9,4,128]{3,2,1,0:T(4,128)S(1)} %all-to-all-done.2.side_j, f32[72,128]{1,0:T(8,128)S(1)} %get-tuple-element.24.rad_i.radius_i.radius, f32[16,2,8,128]{3,2,1,0:T(8,128)S(1)} %all-to-all-done.4.rad_j, ...), custom_call_target="tpu_custom_call" | custom-call | tf_op jit(solution)/shard_map/pallas_call | solution.py:46
  103.2 3.9 %all-to-all-start.5 = ((f32[8,64,128]{2,1,0:T(8,128)}), f32[8,64,128]{2,1,0:T(8,128)S(1)}, u32[]{:S(2)}, u32[]{:S(2)}) async-start(f32[8,64,128]{2,1,0:T(8,128)} %shard_map.101), calls=%async_computation.5 | async-start | bytes 524288 | tf_op jit(solution)/shard_map/all_to_all | solution.py:42
  107.1 2.3 %shard_map.102.direct = f32[32,3,128]{2,1,0:T(4,128)S(1)} custom-call(s32[2057]{0:T(1024)S(1)} %shard_map.96.picked.ready, s32[3]{0:T(128)S(1)} %pad_add_fusion.1.places, f32[33,8,128]{2,1,0:T(8,128)S(1)} %get-tuple-element.21.own_j, f32[65,8,128]{2,1,0:T(8,128)S(1)} %get-tuple-element.20.pack_i, f32[16,2,8,128]{3,2,1,0:T(8,128)S(1)} %all-to-all-done.4.rad_j, ...), custom_call_target="tpu_custom_call" | custom-call | tf_op jit(solution)/shard_map/pallas_call | solution.py:46
  109.3 3.5 %all-to-all-done.5.parts = f32[8,64,128]{2,1,0:T(8,128)S(1)} async-done(((f32[8,64,128]{2,1,0:T(8,128)}), f32[8,64,128]{2,1,0:T(8,128)S(1)}, u32[]{:S(2)}, u32[]{:S(2)}) %all-to-all-start.5) | async-done | bytes 262176 | tf_op jit(solution)/shard_map/all_to_all | solution.py:42
  112.9 2.4 %shard_map.103 = (f32[16,24,128]{2,1,0:T(8,128)S(1)}, f32[2,128]{1,0:T(2,128)S(1)}) custom-call(s32[2057]{0:T(1024)S(1)} %shard_map.96.picked.ready, s32[3]{0:T(128)S(1)} %pad_add_fusion.1.places, f32[65,8,128]{2,1,0:T(8,128)S(1)} %get-tuple-element.20.pack_i, f32[33,8,128]{2,1,0:T(8,128)S(1)} %get-tuple-element.21.own_j, ...), custom_call_target="tpu_custom_call" | custom-call | tf_op jit(solution)/shard_map/pallas_call | solution.py:46
  115.3 17.7 %all_to_all.35.parts = f32[16,24,128]{2,1,0:T(8,128)S(1)} all-to-all(f32[16,24,128]{2,1,0:T(8,128)S(1)} %get-tuple-element.28), channel_id=1, replica_groups=mesh['zh'=4,'zl'=4,'yh'=2,'core'=2,'x'=4,'yl'=2] {'zl','yh','core'}, dimensions={0} | all-to-all | bytes 393216 | tf_op jit(solution)/shard_map/all_to_all | solution.py:42
  132.9 0.6 shard_map.104
  (14 shorter events, 0.1 us)
Async XLA Ops:
  0.6 0.7 copy-start.4
  1.3 0.7 copy-start.2
  1.3 0.7 copy-start.1
  1.4 0.7 copy-start.3
  2.0 0.8 copy-start
  4.1 27.1 %all-to-all-start = ((f32[4,3,4,128]{3,2,1,0:T(4,128)}), f32[4,3,4,128]{3,2,1,0:T(4,128)S(1)}, u32[]{:S(2)}, u32[]{:S(2)}) async-start(f32[4,3,4,128]{3,2,1,0:T(4,128)} %get-tuple-element.19), calls=%async_computation | async-start | bytes 49152 | tf_op jit(solution)/shard_map/all_to_all | solution.py:42
  31.9 10.6 %all-to-all-start.1 = ((f32[8,4,3,4,128]{4,3,2,1,0:T(4,128)}), f32[8,4,3,4,128]{4,3,2,1,0:T(4,128)S(1)}, u32[]{:S(2)}, u32[]{:S(2)}) async-start(f32[8,4,3,4,128]{4,3,2,1,0:T(4,128)} %broadcast_in_dim.41), calls=%async_computation.1 | async-start | bytes 393216 | tf_op jit(solution)/shard_map/all_to_all | solution.py:42
  43.8 20.7 %all-to-all-start.2 = ((f32[16,9,4,128]{3,2,1,0:T(4,128)}), f32[16,9,4,128]{3,2,1,0:T(4,128)S(1)}, u32[]{:S(2)}, u32[]{:S(2)}) async-start(f32[16,9,4,128]{3,2,1,0:T(4,128)} %shard_map.95), calls=%async_computation.2 | async-start | bytes 589824 | tf_op jit(solution)/shard_map/all_to_all | solution.py:42
  69.9 9.1 %all-to-all-start.3 = ((f32[8,64,128]{2,1,0:T(8,128)}), f32[8,64,128]{2,1,0:T(8,128)S(1)}, u32[]{:S(2)}, u32[]{:S(2)}) async-start(f32[8,64,128]{2,1,0:T(8,128)} %shard_map.99), calls=%async_computation.3 | async-start | bytes 524288 | tf_op jit(solution)/shard_map/all_to_all | solution.py:42
  80.3 17.0 %all-to-all-start.4 = ((f32[16,2,8,128]{3,2,1,0:T(8,128)}), f32[16,2,8,128]{3,2,1,0:T(8,128)S(1)}, u32[]{:S(2)}, u32[]{:S(2)}) async-start(f32[16,2,8,128]{3,2,1,0:T(8,128)} %get-tuple-element.25), calls=%async_computation.4 | async-start | bytes 262144 | tf_op jit(solution)/shard_map/all_to_all | solution.py:42
  103.2 9.7 %all-to-all-start.5 = ((f32[8,64,128]{2,1,0:T(8,128)}), f32[8,64,128]{2,1,0:T(8,128)S(1)}, u32[]{:S(2)}, u32[]{:S(2)}) async-start(f32[8,64,128]{2,1,0:T(8,128)} %shard_map.101), calls=%async_computation.5 | async-start | bytes 524288 | tf_op jit(solution)/shard_map/all_to_all | solution.py:42

commit v6 on v5

--- a/solution.py
+++ b/solution.py
@@ -45,7 +45,10 @@
 def called(kernel, outs, scratch, smem, vmem, inputs=VMEM, outputs=VMEM, kind=F32):
     return pl.pallas_call(
         kernel,
-        out_shape=[jax.ShapeDtypeStruct(s, kind) for s in outs],
+        out_shape=[
+            jax.ShapeDtypeStruct(*s) if isinstance(s[0], tuple) else jax.ShapeDtypeStruct(s, kind)
+            for s in outs
+        ],
         in_specs=[SMEM] * len(smem) + [inputs] * len(vmem),
         out_specs=[outputs] * len(outs),
         scratch_shapes=[pltpu.VMEM(*s) if isinstance(s, tuple) else s for s in scratch],
@@ -75,14 +78,14 @@
     mask_ref[1] = jnp.where(down == across, 0.0, 1.0)
 
 
-def write_spread(spread_ref):
-    row = lax.broadcasted_iota(jnp.int32, spread_ref.shape, 0)
-    lane = lax.broadcasted_iota(jnp.int32, spread_ref.shape, 1)
-    hit = (row % 8 == lane // TILE) & (row < 24)
-    spread_ref[...] = jnp.where(hit, 1.0, 0.0).astype(jnp.bfloat16)
-
-
-def columns(rows, spread_ref, count):
+def write_spread(spread_ref, rows):
+    at = lax.broadcasted_iota(jnp.int32, (32, TILE), 0)
+    for c, row in enumerate(rows):
+        hit = (at % 8 == row) & (at < 24)
+        spread_ref[:, c * TILE : (c + 1) * TILE] = jnp.where(hit, 1.0, 0.0).astype(jnp.bfloat16)
+
+
+def columns(rows, spread_ref):
     high = rows.astype(jnp.bfloat16).astype(F32)
     rest = rows - high
     middle = rest.astype(jnp.bfloat16).astype(F32)
@@ -227,7 +230,13 @@
     return rho, found[3:]
 
 
-def pack_kernel(table, side_i, pack_i, charge_i, more_i):
+def pack_kernel(
+    table, side_i, pack_i, charge_i, more_i, mask_ref, typed_ref, plain_ref, pair_ref
+):
+    write_mask(mask_ref)
+    typed_spread(table, typed_ref)
+    write_spread(plain_ref, range(6))
+    write_spread(pair_ref, (0, 1, 2, 4, 5, 6))
     for n in range(N_COLS):
         for z in range(N_REP):
             at = n * HELD + 2 * z
@@ -241,10 +250,8 @@
         more_i[n] = value
 
 
-def born_kernel(meta, table, pack_i, side_j, out_ref, acc, mask_ref, spread_ref):
+def born_kernel(meta, pack_i, side_j, mask_ref, spread_ref, out_ref, acc):
     acc[...] = jnp.zeros_like(acc)
-    write_mask(mask_ref)
-    typed_spread(table, spread_ref)
 
     def one_tile(ia, jb, same):
         col = typed_columns(j_atoms(side_j, jb), spread_ref)
@@ -293,9 +300,8 @@
         sent_ref[n, 1] = charges
 
 
-def slope_kernel(picked, places, table, pack_i, side_j, out_ref, own_j, force, spread_ref):
+def slope_kernel(meta, places, table, pack_i, side_j, spread_ref, out_ref, own_j, force):
     force[...] = jnp.zeros_like(force)
-    write_spread(spread_ref)
     for n in range(N_ROWS):
         for b in range(2):
             block = side_j[n, places[0] * 2 + b]
@@ -304,9 +310,9 @@
     own_j[2 * N_ROWS] = jnp.ones((8, TILE), F32)
     packed(table, own_j, 2 * N_ROWS, ())
 
-    def one_tile(at, jb, same):
-        col = columns(pack_i[jb], spread_ref, 6)
-        xi, yi, zi, rho = (own_j[at, c : c + 1, :] for c in range(4))
+    def one_tile(ia, jb, same):
+        col = typed_columns(j_atoms(side_j, jb), spread_ref)
+        xi, yi, zi, rho = (pack_i[ia, c : c + 1, :] for c in range(4))
         rho_sq, rho_gap = rho * rho, rho + NECK_GAP
         sums = [jnp.zeros((8, TILE), F32)] * 3
         for s in range(0, TILE, CHUNK):
@@ -324,19 +330,22 @@
 
         def add():
             for c in range(3):
-                force[at, c] += sums[c]
+                force[ia, c] += sums[c]
 
         return add
 
-    for_each_tile(picked, 0, picked[PICKED + UNROLL], one_tile)
-    out_ref[...] = jnp.sum(force[0 : 2 * N_ROWS], axis=2)
+    for_each_tile(meta, 0, meta[LISTED + 1], one_tile)
+    for n in range(N_COLS):
+        for b in range(2):
+            total = jnp.sum(force[n * HELD + places[0] * 2 + b], axis=1)
+            out_ref[n, 3 * b : 3 * b + 3, :] = total
+        out_ref[n, 6:8, :] = total[0:2]
 
 
 def direct_kernel(
-    picked, places, own_j, pack_i, rad_j, radius_i, charge_i, out_ref, force, spread_ref, sides, own
+    picked, places, own_j, pack_i, rad_j, radius_i, charge_i, spread_ref, out_ref, force, sides, own, own_q
 ):
     force[...] = jnp.zeros_like(force)
-    write_spread(spread_ref)
     sides[...] = pack_i[0:I_BLOCKS]
     radii = radius_i[0:I_BLOCKS]
     sides[:, 3, :] = radii
@@ -345,9 +354,10 @@
     own[...] = jnp.ones_like(own)
     for n in range(N_ROWS):
         own[2 * n : 2 * n + 2] = rad_j[n, 0, pl.ds(places[0] * 2, 2), :]
+        own_q[2 * n : 2 * n + 2] = rad_j[n, 1, pl.ds(places[0] * 2, 2), :]
 
     def one_tile(at, jb, same):
-        col = columns(sides[jb], spread_ref, 6)
+        col = columns(sides[jb], spread_ref)
         xi, yi, zi = (own_j[at, c : c + 1, :] for c in range(3))
         radius = own[pl.ds(at, 1), :]
         quarter = 0.25 / radius
@@ -368,25 +378,25 @@
         return add
 
     for_each_tile(picked, 0, picked[PICKED + UNROLL], one_tile)
-    out_ref[...] = jnp.sum(force[0 : 2 * N_ROWS], axis=2)
+    scale = (2.0 * COULOMB) * own_q[...]
+    for c in range(3):
+        out_ref[c] = scale * jnp.sum(force[0 : 2 * N_ROWS, c], axis=1)
 
 
 def pair_kernel(
-    meta, pack_i, side_j, rad_i, rad_j, ready, out_ref, acc, mask_ref, spread_ref, sides
+    meta, pack_i, side_j, rad_i, rad_j, slopes, mask_ref, spread_ref, out_ref, acc
 ):
     acc[...] = jnp.zeros_like(acc)
-    write_mask(mask_ref)
-    write_spread(spread_ref)
-    for n in range(N_ROWS):
-        here = slice(n * HELD, (n + 1) * HELD)
-        sides[here, 0:4, :] = side_j[n, 0:HELD]
-        sides[here, 4:8, :] = side_j[n, 0:HELD]
-        sides[here, 3, :] = rad_j[n, 0]
-        sides[here, 4, :] = 1.0 / rad_j[n, 0]
-        sides[here, 5, :] = rad_j[n, 1]
 
     def one_tile(ia, jb, same):
-        col = columns(sides[jb], spread_ref, 6)
+        n, b = jb // HELD, jb % HELD
+        radius_j, charge_j = (rad_j[n, k, pl.ds(b, 1), :] for k in range(2))
+        col = columns(
+            jnp.concatenate(
+                [side_j[n, b], radius_j, 1.0 / radius_j, charge_j, charge_j], axis=0
+            ),
+            spread_ref,
+        )
         xi, yi, zi = (pack_i[ia, c : c + 1, :] for c in range(3))
         radius_i = rad_i[pl.ds(ia, 1), :]
         quarter_i = 0.25 / radius_i
@@ -409,28 +419,28 @@
     for_each_tile(meta, 0, meta[LISTED], one_tile)
     grads = jnp.sum(acc[0:I_BLOCKS], axis=1)
     for n in range(N_COLS):
-        out_ref[n] = grads
+        out_ref[n, 0:I_BLOCKS] = grads
+        out_ref[n, I_BLOCKS : I_BLOCKS + 8] = slopes[n]
 
 
 def chain_kernel(
-    picked, places, pack_i, own_j, parts, charge, radius, rate, direct, slopes, out_ref, own_ref, force, spread_ref, sides
+    picked, places, pack_i, own_j, parts, charge, radius, rate, direct, spread_ref, out_ref, own_ref, force, chain_ref
 ):
     force[...] = jnp.zeros_like(force)
-    write_spread(spread_ref)
     total = parts[0]
     for n in range(1, N_COLS):
         total = total + parts[n]
     charges, radii = charge[...], radius[0:I_BLOCKS]
-    grad = -0.5 * charges * total
+    grad = -0.5 * charges * total[0:I_BLOCKS]
     chain = (COULOMB * charges * charges / (2.0 * radii * radii) - COULOMB * grad) * rate[...]
-    sides[...] = pack_i[0:I_BLOCKS]
-    sides[:, 4, :] = chain
-    first = places[2] * HELD + places[0] * 2
+    chain_ref[...] = chain
+    own_ref[0:8] = total[I_BLOCKS : I_BLOCKS + 8]
     for b in range(2):
-        own_ref[b : b + 1] = sides[first + b, 4:5, :]
+        own_ref[8 + b : 9 + b] = chain_ref[pl.ds(places[2] * HELD + places[0] * 2 + b, 1), :]
+    fifth = lax.broadcasted_iota(jnp.int32, (8, TILE), 0) == 4
 
     def one_tile(at, jb, same):
-        col = columns(sides[jb], spread_ref, 5)
+        col = columns(jnp.where(fifth, chain_ref[pl.ds(jb, 1), :], pack_i[jb]), spread_ref)
         xi, yi, zi, rho, vol, neck = (own_j[at, c : c + 1, :] for c in range(6))
         rho_gap = rho + NECK_GAP
         sums = [jnp.zeros((8, TILE), F32)] * 3
@@ -456,13 +466,12 @@
         return add
 
     for_each_tile(picked, 0, picked[PICKED + UNROLL], one_tile)
-    chained = jnp.sum(force[0 : 2 * N_ROWS], axis=2)
-    for n in range(N_ROWS):
-        for b in range(2):
-            at = 2 * n + b
-            for c, value in enumerate((chained, direct, slopes)):
-                out_ref[n, 12 * b + 4 * c : 12 * b + 4 * c + 3, :] = value[at]
-                out_ref[n, 12 * b + 4 * c + 3 : 12 * b + 4 * c + 4, :] = value[at, 0:1, :]
+    for k in range(3):
+        value = direct[k] - 2.0 * jnp.sum(force[0 : 2 * N_ROWS, k], axis=1)
+        for n in range(N_ROWS):
+            out_ref[n, 2 * k : 2 * k + 2, :] = value[2 * n : 2 * n + 2]
+            if k == 2:
+                out_ref[n, 6:8, :] = value[2 * n : 2 * n + 2]
 
 
 def last_kernel(parts, own, kept, vel_ref, force_ref):
@@ -471,12 +480,13 @@
         total = total + parts[n]
     for b in range(2):
         here = slice(b * TILE, (b + 1) * TILE)
-        chained, direct, slopes = (total[12 * b + 4 * c : 12 * b + 4 * c + 3] for c in range(3))
-        force = (2.0 * COULOMB) * kept[4:5, here] * direct - 2.0 * (
-            chained + own[b : b + 1, :] * slopes
-        )
-        force_ref[:, here] = force
-        vel_ref[:, here] = kept[0:3, here] + kept[3:4, here] * force
+        for k in range(3):
+            row = slice(k, k + 1)
+            force = total[2 * k + b : 2 * k + b + 1] - 2.0 * (
+                own[8 + b : 9 + b, :] * own[3 * b + k : 3 * b + k + 1, :]
+            )
+            force_ref[row, here] = force
+            vel_ref[row, here] = kept[row, here] + kept[3:4, here] * force
 
 
 def transposed_keys(lists, places):
@@ -490,7 +500,7 @@
     return jnp.where(mine, key.astype(F32), NO_KEY).reshape(2 * N_ROWS, TILE)
 
 
-def tile_codes(lists, row_at, col_at):
+def tile_codes(lists, rep_at, row_at, col_at):
     list_a, list_g = lists[:, 0].astype(jnp.int32), lists[:, 1].astype(jnp.int32)
     reps = jnp.arange(N_REP, dtype=jnp.int32)[:, None]
     live = list_a >= 0
@@ -501,12 +511,14 @@
     same = (j_row == reps * N_ROWS + row_at) & (list_a == col_at * 2 + list_g % 2)
     none = I_BLOCKS * 256
     codes = place_i * 256 + place_j * 2 + same.astype(jnp.int32) - none
-    before = jnp.sum(jnp.where(reps < reps.T, counts[:, None], 0), axis=0)
+    turn = (reps - rep_at) & (N_REP - 1)
+    before = jnp.sum(jnp.where(turn < turn.T, counts[:, None], 0), axis=0)
     target = before[:, None] + jnp.arange(SLOTS, dtype=jnp.int32)[None, :]
     target = jnp.where(live, target, -1).reshape(1, LISTED)
     hit = target == jnp.arange(LISTED, dtype=jnp.int32)[:, None]
     placed = none + jnp.sum(jnp.where(hit, codes.reshape(1, LISTED), 0), axis=1)
-    return jnp.concatenate([placed, jnp.sum(counts)[None]]).astype(jnp.int32)
+    own = jnp.sum(jnp.where(turn[:, 0] == 0, counts, 0))
+    return jnp.concatenate([placed, jnp.stack([jnp.sum(counts), own])]).astype(jnp.int32)
 
 
 def body(positions, velocities, old_forces, charges, atom_types, table, tile_pairs):
@@ -534,20 +546,25 @@
         [joined],
     )
     held = exchanged(sent, REP)
-    meta = tile_codes(held[:, 2, 0:2, 0:SLOTS], row_at, col_at)
+    meta = tile_codes(held[:, 2, 0:2, 0:SLOTS], rep_at, row_at, col_at)
     side_i = exchanged(jnp.broadcast_to(held, (N_COLS, *held.shape)), COLS)
     [sent] = called(row_kernel, [(N_ROWS, 9, 4, TILE)], [], [places], [side_i])
     side_j = exchanged(sent, ROWS)
 
-    mask = ((2, TILE, TILE), F32)
-    spread_5, spread_6 = (((32, n * TILE), jnp.bfloat16) for n in (5, 6))
-    typed = ((48, 6 * TILE), jnp.bfloat16)
     sums = ((I_BLOCKS + 1, 8, TILE), F32)
     forces = ((2 * N_ROWS + 1, 3, 8, TILE), F32)
-    held_sides = ((I_BLOCKS, 8, TILE), F32)
-    pack_i, charge_i, more_i = called(
+    bf16 = jnp.bfloat16
+    pack_i, charge_i, more_i, mask, typed, plain, paired = called(
         pack_kernel,
-        [(I_BLOCKS + 1, 8, TILE), (I_BLOCKS, TILE), (5, I_BLOCKS, TILE)],
+        [
+            (I_BLOCKS + 1, 8, TILE),
+            (I_BLOCKS, TILE),
+            (5, I_BLOCKS, TILE),
+            (2, TILE, TILE),
+            ((48, 6 * TILE), bf16),
+            ((32, 6 * TILE), bf16),
+            ((32, 6 * TILE), bf16),
+        ],
         [],
         [table],
         [side_i],
@@ -555,9 +572,9 @@
     [born_parts] = called(
         born_kernel,
         [(N_COLS, I_BLOCKS, TILE)],
-        [sums, mask, typed],
-        [meta, table],
-        [pack_i, side_j],
+        [sums],
+        [meta],
+        [pack_i, side_j, mask, typed],
     )
     born_parts = exchanged(born_parts, COLS)
     [picked] = called(
@@ -579,32 +596,37 @@
     rad_j = exchanged(sent, ROWS)
     slopes, own_j = called(
         slope_kernel,
-        [(2 * N_ROWS, 3, TILE), (2 * N_ROWS + 1, 8, TILE)],
-        [forces, spread_6],
-        [picked, places, table],
-        [pack_i, side_j],
+        [(N_COLS, 8, TILE), (2 * N_ROWS + 1, 8, TILE)],
+        [((I_BLOCKS + 1, 3, 8, TILE), F32)],
+        [meta, places, table],
+        [pack_i, side_j, typed],
     )
     [grads] = called(
         pair_kernel,
-        [(N_COLS, I_BLOCKS, TILE)],
-        [sums, mask, spread_6, ((J_BLOCKS, 8, TILE), F32)],
+        [(N_COLS, I_BLOCKS + 8, TILE)],
+        [sums],
         [meta],
-        [pack_i, side_j, radius_i, rad_j, slopes],
+        [pack_i, side_j, radius_i, rad_j, slopes, mask, paired],
     )
     grads = exchanged(grads, COLS)
     [direct] = called(
         direct_kernel,
-        [(2 * N_ROWS, 3, TILE)],
-        [forces, spread_6, held_sides, ((2 * N_ROWS + 8, TILE), F32)],
+        [(3, 2 * N_ROWS, TILE)],
+        [
+            forces,
+            ((I_BLOCKS, 8, TILE), F32),
+            ((2 * N_ROWS + 8, TILE), F32),
+            ((2 * N_ROWS, TILE), F32),
+        ],
         [picked, places],
-        [own_j, pack_i, rad_j, radius_i, charge_i],
+        [own_j, pack_i, rad_j, radius_i, charge_i, plain],
     )
     parts, own = called(
         chain_kernel,
-        [(N_ROWS, 24, TILE), (2, TILE)],
-        [forces, spread_5, held_sides],
+        [(N_ROWS, 8, TILE), (10, TILE)],
+        [forces, ((I_BLOCKS, TILE), F32)],
         [picked, places],
-        [pack_i, own_j, grads, charge_i, radius_i, rate_i, direct, slopes],
+        [pack_i, own_j, grads, charge_i, radius_i, rate_i, direct, plain],
     )
     parts = exchanged(parts, ROWS)
     new_velocities, new_forces = called(

time: 134 us -> 129 us (0.963)
  blocking collectives: 17.7 us -> 11.1 us
  other arithmetic: 2.61 us -> 4.09 us
    all_to_all x1, blocking collectives: 17.7 us -> 11.1 us  [exchanged(): return lax.all_to_all(pieces, axes, 0, 0, tiled=True)]
  transfers between devices with their start and end apart: 6 -> 6, of which waited for: 6 -> 6; matrix products, arithmetic and copies ran while one was open for 2% -> 3% of each run, Pallas kernels for 7% -> 7%
where the time goes in v6:
time: 129 us
  starting transfers between devices  44.9 us (35%)
  waiting for transfers between devices  38 us (29%)
  Pallas kernels  26.9 us (21%)
  blocking collectives  11.1 us (9%)
  other arithmetic  4.09 us (3%)
  local copies, waits for them, and re-layouts  2.72 us (2%)
    all_to_all x6, starting transfers between devices, exchanged(): return lax.all_to_all(pieces, axes, 0, 0, tiled=True)  44.9 us
    all_to_all x6, waiting for transfers between devices, exchanged(): return lax.all_to_all(pieces, axes, 0, 0, tiled=True)  38 us
    pallas_call x11, Pallas kernels, called(): pl.pallas_call(kernel, out_shape=[jax.ShapeDtypeStruct(*s) if isinstance(...  26.9 us
    all_to_all x1, blocking collectives, exchanged(): return lax.all_to_all(pieces, axes, 0, 0, tiled=True)  11.1 us
  transfers between devices with their start and end apart: 6, of which 6 were waited for; matrix products, arithmetic and copies ran while one was open for 3% of the time, Pallas kernels for 7%

profile of v6, /device:TPU:1, one launch (start us, length us, event | category | flops | bytes accessed | tf_op | source)
XLA Modules:
  0.0 128.5 jit_solution(10420475286696264323)
XLA Ops:
  0.6 0.0 copy-start.4
  0.6 0.7 convert_bitcast_fusion
  1.3 0.0 copy-done.4
  1.3 0.0 copy-start.1
  1.4 0.0 copy-start.3
  1.4 0.6 copy-done.2
  2.0 0.0 copy-done.1
  2.0 0.0 copy-done.3
  2.0 0.8 concatenate.6.joined
  2.9 1.2 shard_map.94
  4.1 15.6 %all-to-all-start = ((f32[4,3,4,128]{3,2,1,0:T(4,128)}), f32[4,3,4,128]{3,2,1,0:T(4,128)S(1)}, u32[]{:S(2)}, u32[]{:S(2)}) async-start(f32[4,3,4,128]{3,2,1,0:T(4,128)} %get-tuple-element.23), calls=%async_computation | async-start | bytes 49152 | tf_op jit(solution)/shard_map/all_to_all | solution.py:42
  19.8 0.1 eq.65
  19.9 0.1 eq.66
  20.0 0.1 add.217
  20.0 0.1 pad_add_fusion.1.places
  20.1 11.1 %all-to-all-done = f32[4,3,4,128]{3,2,1,0:T(4,128)S(1)} async-done(((f32[4,3,4,128]{3,2,1,0:T(4,128)}), f32[4,3,4,128]{3,2,1,0:T(4,128)S(1)}, u32[]{:S(2)}, u32[]{:S(2)}) %all-to-all-start) | async-done | bytes 24608 | tf_op jit(solution)/shard_map/all_to_all | solution.py:42
  31.2 0.7 broadcast_in_dim.40
  31.9 5.0 %all-to-all-start.1 = ((f32[8,4,3,4,128]{4,3,2,1,0:T(4,128)}), f32[8,4,3,4,128]{4,3,2,1,0:T(4,128)S(1)}, u32[]{:S(2)}, u32[]{:S(2)}) async-start(f32[8,4,3,4,128]{4,3,2,1,0:T(4,128)} %broadcast_in_dim.40), calls=%async_computation.1 | async-start | bytes 393216 | tf_op jit(solution)/shard_map/all_to_all | solution.py:42
  37.0 0.8 fusion.4
  37.7 4.7 %all-to-all-done.1.side_i = f32[8,4,3,4,128]{4,3,2,1,0:T(4,128)S(1)} async-done(((f32[8,4,3,4,128]{4,3,2,1,0:T(4,128)}), f32[8,4,3,4,128]{4,3,2,1,0:T(4,128)S(1)}, u32[]{:S(2)}, u32[]{:S(2)}) %all-to-all-start.1) | async-done | bytes 196640 | tf_op jit(solution)/shard_map/all_to_all | solution.py:42
  42.5 1.3 %shard_map.95 = f32[16,9,4,128]{3,2,1,0:T(4,128)} custom-call(s32[3]{0:T(128)S(1)} %pad_add_fusion.1.places, f32[8,4,3,4,128]{4,3,2,1,0:T(4,128)S(1)} %all-to-all-done.1.side_i), custom_call_target="tpu_custom_call" | custom-call | tf_op jit(solution)/shard_map/pallas_call | solution.py:46
  43.8 9.1 %all-to-all-start.2 = ((f32[16,9,4,128]{3,2,1,0:T(4,128)}), f32[16,9,4,128]{3,2,1,0:T(4,128)S(1)}, u32[]{:S(2)}, u32[]{:S(2)}) async-start(f32[16,9,4,128]{3,2,1,0:T(4,128)} %shard_map.95), calls=%async_computation.2 | async-start | bytes 589824 | tf_op jit(solution)/shard_map/all_to_all | solution.py:42
  52.9 0.6 fusion.10
  53.6 0.1 select_reduce_fusion.1
  53.7 0.1 iota_add_fusion
  53.7 0.1 add.215
  53.8 0.1 convert_element_type.66
  53.9 0.1 convert_element_type.69
  54.0 0.1 select_reduce_fusion
  54.1 1.3 %pad_add_fusion.meta = s32[130]{0:T(256)S(1)} fusion(s32[1]{0:T(128)} %bitcast.10, s32[1]{0:T(128)} %bitcast.9, s32[128]{0:T(128)S(1)} %broadcast_add_fusion), kind=kLoop, calls=%fused_computation.52 | loop fusion | flops 260 | bytes 1040 | tf_op jit(solution)/shard_map/concatenate | solution.py:521
  55.5 1.8 %shard_map.97 = (f32[65,8,128]{2,1,0:T(8,128)S(1)}, f32[64,128]{1,0:T(8,128)S(1)}, f32[5,64,128]{2,1,0:T(8,128)S(1)}, f32[2,128,128]{2,1,0:T(8,128)S(1)}, bf16[4...) custom-call(f32[7,8]{1,0:T(8,128)S(1)} %copy-done, ...), custom_call_target="tpu_custom_call" | custom-call | tf_op jit(solution)/shard_map/pallas_call | solution.py:46
  57.3 7.2 %all-to-all-done.2.side_j = f32[16,9,4,128]{3,2,1,0:T(4,128)S(1)} async-done(((f32[16,9,4,128]{3,2,1,0:T(4,128)}), f32[16,9,4,128]{3,2,1,0:T(4,128)S(1)}, u32[]{:S(2)}, u32[]{:S(2)}) %all-to-all-start.2) | async-done | bytes 294944 | tf_op jit(solution)/shard_map/all_to_all | solution.py:42
  64.5 5.4 %shard_map.99 = f32[8,64,128]{2,1,0:T(8,128)} custom-call(s32[130]{0:T(256)S(1)} %pad_add_fusion.meta, f32[65,8,128]{2,1,0:T(8,128)S(1)} %get-tuple-element.24.pack_i, f32[16,9,4,128]{3,2,1,0:T(4,128)S(1)} %all-to-all-done.2.side_j, f32[2,128,128]{2,1,0:T(8,128)S(1)} %get-tuple-element.27.mask_ref, bf16[48,768]{1,0:T(8,128)(2,1)S(1)} %get-tuple-element.25.spread_ref), custom_call_target="tpu_custom_call" | custom-call | tf_op jit(solution)/shard_map/pallas_call | solution.py:46
  69.8 4.7 %all-to-all-start.3 = ((f32[8,64,128]{2,1,0:T(8,128)}), f32[8,64,128]{2,1,0:T(8,128)S(1)}, u32[]{:S(2)}, u32[]{:S(2)}) async-start(f32[8,64,128]{2,1,0:T(8,128)} %shard_map.99), calls=%async_computation.3 | async-start | bytes 524288 | tf_op jit(solution)/shard_map/all_to_all | solution.py:42
  74.5 0.2 and_select_fusion.3
  74.8 2.6 %shard_map.96.ready.picked = s32[2057]{0:T(1024)S(1)} custom-call(f32[32,128]{1,0:T(8,128)S(1)} %bitcast.14), custom_call_target="tpu_custom_call" | custom-call | tf_op jit(solution)/shard_map/pallas_call | solution.py:46
  77.4 3.7 %all-to-all-done.3.parts = f32[8,64,128]{2,1,0:T(8,128)S(1)} async-done(((f32[8,64,128]{2,1,0:T(8,128)}), f32[8,64,128]{2,1,0:T(8,128)S(1)}, u32[]{:S(2)}, u32[]{:S(2)}) %all-to-all-start.3) | async-done | bytes 262176 | tf_op jit(solution)/shard_map/all_to_all | solution.py:42
  81.1 1.3 shard_map.100
  82.3 4.8 %all-to-all-start.4 = ((f32[16,2,8,128]{3,2,1,0:T(8,128)}), f32[16,2,8,128]{3,2,1,0:T(8,128)S(1)}, u32[]{:S(2)}, u32[]{:S(2)}) async-start(f32[16,2,8,128]{3,2,1,0:T(8,128)} %get-tuple-element.31), calls=%async_computation.4 | async-start | bytes 262144 | tf_op jit(solution)/shard_map/all_to_all | solution.py:42
  87.2 1.5 %shard_map.98 = (f32[8,8,128]{2,1,0:T(8,128)S(1)}, f32[33,8,128]{2,1,0:T(8,128)S(1)}) custom-call(s32[130]{0:T(256)S(1)} %pad_add_fusion.meta, s32[3]{0:T(128)S(1)} %pad_add_fusion.1.places, f32[7,8]{1,0:T(8,128)S(1)} %copy-done, f32[65,8,128]{2,1,0:T(8,128)S(1)} %get-tuple-element.24.pack_i, f32[16,9,4,128]{3,2,1,0:T(4,128)S(1)} %all-to-all-done.2.side_j, ...), custom_call_target="tpu_custom_call" | custom-call | tf_op jit(solution)/shard_map/pallas_call | solution.py:46
  88.7 6.8 %all-to-all-done.4.rad_j = f32[16,2,8,128]{3,2,1,0:T(8,128)S(1)} async-done(((f32[16,2,8,128]{3,2,1,0:T(8,128)}), f32[16,2,8,128]{3,2,1,0:T(8,128)S(1)}, u32[]{:S(2)}, u32[]{:S(2)}) %all-to-all-start.4) | async-done | bytes 131104 | tf_op jit(solution)/shard_map/all_to_all | solution.py:42
  95.6 5.8 %shard_map.101 = f32[8,72,128]{2,1,0:T(8,128)} custom-call(s32[130]{0:T(256)S(1)} %pad_add_fusion.meta, f32[65,8,128]{2,1,0:T(8,128)S(1)} %get-tuple-element.24.pack_i, f32[16,9,4,128]{3,2,1,0:T(4,128)S(1)} %all-to-all-done.2.side_j, f32[72,128]{1,0:T(8,128)S(1)} %get-tuple-element.30.rad_i.radius_i.radius, f32[16,2,8,128]{3,2,1,0:T(8,128)S(1)} %all-to-all-done.4.rad_j, ...), custom_call_target="tpu_custom_call" | custom-call | tf_op jit(solution)/shard_map/pallas_call | solution.py:46
  101.4 5.6 %all-to-all-start.5 = ((f32[8,72,128]{2,1,0:T(8,128)}), f32[8,72,128]{2,1,0:T(8,128)S(1)}, u32[]{:S(2)}, u32[]{:S(2)}) async-start(f32[8,72,128]{2,1,0:T(8,128)} %shard_map.101), calls=%async_computation.5 | async-start | bytes 589824 | tf_op jit(solution)/shard_map/all_to_all | solution.py:42
  106.9 2.6 %shard_map.102.direct = f32[3,32,128]{2,1,0:T(8,128)S(1)} custom-call(s32[2057]{0:T(1024)S(1)} %shard_map.96.ready.picked, s32[3]{0:T(128)S(1)} %pad_add_fusion.1.places, f32[33,8,128]{2,1,0:T(8,128)S(1)} %get-tuple-element.26.own_j, f32[65,8,128]{2,1,0:T(8,128)S(1)} %get-tuple-element.24.pack_i, f32[16,2,8,128]{3,2,1,0:T(8,128)S(1)} %all-to-all-done.4.rad_j, ...), custom_call_target="tpu_custom_call" | custom-call | tf_op jit(solution)/shard_map/pallas_call | solution.py:46
  109.6 4.4 %all-to-all-done.5.parts = f32[8,72,128]{2,1,0:T(8,128)S(1)} async-done(((f32[8,72,128]{2,1,0:T(8,128)}), f32[8,72,128]{2,1,0:T(8,128)S(1)}, u32[]{:S(2)}, u32[]{:S(2)}) %all-to-all-start.5) | async-done | bytes 294944 | tf_op jit(solution)/shard_map/all_to_all | solution.py:42
  114.0 2.8 %shard_map.103 = (f32[16,8,128]{2,1,0:T(8,128)S(1)}, f32[10,128]{1,0:T(8,128)S(1)}) custom-call(s32[2057]{0:T(1024)S(1)} %shard_map.96.ready.picked, s32[3]{0:T(128)S(1)} %pad_add_fusion.1.places, f32[65,8,128]{2,1,0:T(8,128)S(1)} %get-tuple-element.24.pack_i, f32[33,8,128]{2,1,0:T(8,128)S(1)} %get-tuple-element.26.own_j, ...), custom_call_target="tpu_custom_call" | custom-call | tf_op jit(solution)/shard_map/pallas_call | solution.py:46
  116.8 11.1 %all_to_all.35.parts = f32[16,8,128]{2,1,0:T(8,128)S(1)} all-to-all(f32[16,8,128]{2,1,0:T(8,128)S(1)} %get-tuple-element.36), channel_id=1, replica_groups=mesh['zh'=4,'zl'=4,'yh'=2,'core'=2,'x'=4,'yl'=2] {'zl','yh','core'}, dimensions={0} | all-to-all | bytes 131072 | tf_op jit(solution)/shard_map/all_to_all | solution.py:42
  127.9 0.6 shard_map.104
  (15 shorter events, 0.1 us)
Async XLA Ops:
  0.6 0.7 copy-start.4
  1.3 0.7 copy-start.2
  1.3 0.7 copy-start.1
  1.4 0.7 copy-start.3
  2.0 0.8 copy-start
  4.1 27.1 %all-to-all-start = ((f32[4,3,4,128]{3,2,1,0:T(4,128)}), f32[4,3,4,128]{3,2,1,0:T(4,128)S(1)}, u32[]{:S(2)}, u32[]{:S(2)}) async-start(f32[4,3,4,128]{3,2,1,0:T(4,128)} %get-tuple-element.23), calls=%async_computation | async-start | bytes 49152 | tf_op jit(solution)/shard_map/all_to_all | solution.py:42
  31.9 10.6 %all-to-all-start.1 = ((f32[8,4,3,4,128]{4,3,2,1,0:T(4,128)}), f32[8,4,3,4,128]{4,3,2,1,0:T(4,128)S(1)}, u32[]{:S(2)}, u32[]{:S(2)}) async-start(f32[8,4,3,4,128]{4,3,2,1,0:T(4,128)} %broadcast_in_dim.40), calls=%async_computation.1 | async-start | bytes 393216 | tf_op jit(solution)/shard_map/all_to_all | solution.py:42
  43.8 20.7 %all-to-all-start.2 = ((f32[16,9,4,128]{3,2,1,0:T(4,128)}), f32[16,9,4,128]{3,2,1,0:T(4,128)S(1)}, u32[]{:S(2)}, u32[]{:S(2)}) async-start(f32[16,9,4,128]{3,2,1,0:T(4,128)} %shard_map.95), calls=%async_computation.2 | async-start | bytes 589824 | tf_op jit(solution)/shard_map/all_to_all | solution.py:42
  69.8 11.2 %all-to-all-start.3 = ((f32[8,64,128]{2,1,0:T(8,128)}), f32[8,64,128]{2,1,0:T(8,128)S(1)}, u32[]{:S(2)}, u32[]{:S(2)}) async-start(f32[8,64,128]{2,1,0:T(8,128)} %shard_map.99), calls=%async_computation.3 | async-start | bytes 524288 | tf_op jit(solution)/shard_map/all_to_all | solution.py:42
  82.3 13.2 %all-to-all-start.4 = ((f32[16,2,8,128]{3,2,1,0:T(8,128)}), f32[16,2,8,128]{3,2,1,0:T(8,128)S(1)}, u32[]{:S(2)}, u32[]{:S(2)}) async-start(f32[16,2,8,128]{3,2,1,0:T(8,128)} %get-tuple-element.31), calls=%async_computation.4 | async-start | bytes 262144 | tf_op jit(solution)/shard_map/all_to_all | solution.py:42
  101.4 12.6 %all-to-all-start.5 = ((f32[8,72,128]{2,1,0:T(8,128)}), f32[8,72,128]{2,1,0:T(8,128)S(1)}, u32[]{:S(2)}, u32[]{:S(2)}) async-start(f32[8,72,128]{2,1,0:T(8,128)} %shard_map.101), calls=%async_computation.5 | async-start | bytes 589824 | tf_op jit(solution)/shard_map/all_to_all | solution.py:42

commit v7 on v6

--- a/solution.py
+++ b/solution.py
@@ -250,6 +250,18 @@
         more_i[n] = value
 
 
+def keep_kernel(meta, read, kept):
+    def step(k, count):
+        code = meta[k]
+        kept[count] = code
+        return count + read[code >> 8]
+
+    count = lax.fori_loop(0, meta[LISTED], step, 0)
+    for n in range(UNROLL):
+        kept[count + n] = I_BLOCKS * 256
+    kept[LISTED + UNROLL] = count
+
+
 def born_kernel(meta, pack_i, side_j, mask_ref, spread_ref, out_ref, acc):
     acc[...] = jnp.zeros_like(acc)
 
@@ -279,7 +291,7 @@
         out_ref[n] = born
 
 
-def radius_kernel(places, parts, pack_i, more_i, charge, ready, radius_ref, sent_ref, rate_ref):
+def radius_kernel(places, parts, pack_i, more_i, charge, ready, ready_too, radius_ref, sent_ref, rate_ref):
     born = parts[0]
     for n in range(1, N_COLS):
         born = born + parts[n]
@@ -416,7 +428,7 @@
 
         return add
 
-    for_each_tile(meta, 0, meta[LISTED], one_tile)
+    for_each_tile(meta, 0, meta[LISTED + UNROLL], one_tile)
     grads = jnp.sum(acc[0:I_BLOCKS], axis=1)
     for n in range(N_COLS):
         out_ref[n, 0:I_BLOCKS] = grads
@@ -493,11 +505,15 @@
     list_a, list_g = lists[:, 0:2].astype(jnp.int32), lists[:, 2:4].astype(jnp.int32)
     source, half, lane = (lax.broadcasted_iota(jnp.int32, list_a.shape, n) for n in range(3))
     j_col, j_row = half * 4 + lane // SLOTS, list_g // 2
-    mine = (list_a >= 0) & (list_a // 2 == places[2]) & (j_row % N_ROWS == places[1])
+    known = (list_a >= 0) & (j_row % N_ROWS == places[1])
     place_j = (j_col * N_REP + j_row // N_ROWS) * 2 + list_g % 2
     key = ((source * 2 + list_a % 2) * I_BLOCKS + place_j) * 4096
     key = key + (source * 2 + half) * TILE + lane
-    return jnp.where(mine, key.astype(F32), NO_KEY).reshape(2 * N_ROWS, TILE)
+    keys = jnp.where(known & (list_a // 2 == places[2]), key.astype(F32), NO_KEY)
+    named = jnp.where(known, place_j, -1).reshape(1, 2 * N_ROWS, TILE)
+    blocks = jnp.arange(I_BLOCKS, dtype=jnp.int32)
+    read = jnp.any(named == blocks[:, None, None], axis=(1, 2)) | (blocks // 2 % N_REP == places[0])
+    return keys.reshape(2 * N_ROWS, TILE), read.astype(jnp.int32)
 
 
 def tile_codes(lists, rep_at, row_at, col_at):
@@ -577,12 +593,16 @@
         [pack_i, side_j, mask, typed],
     )
     born_parts = exchanged(born_parts, COLS)
+    keys, read = transposed_keys(side_j[:, HELD], places)
+    [kept_tiles] = called(
+        keep_kernel, [(LISTED + UNROLL + 1,)], [], [meta, read], [], outputs=SMEM, kind=jnp.int32
+    )
     [picked] = called(
         pick_kernel,
         [(PICKED + UNROLL + 1,)],
         [],
         [],
-        [transposed_keys(side_j[:, HELD], places)],
+        [keys],
         outputs=SMEM,
         kind=jnp.int32,
     )
@@ -591,7 +611,7 @@
         [(I_BLOCKS + 8, TILE), (N_ROWS, 2, HELD, TILE), (I_BLOCKS, TILE)],
         [],
         [places],
-        [born_parts, pack_i, more_i, charge_i, picked],
+        [born_parts, pack_i, more_i, charge_i, picked, kept_tiles],
     )
     rad_j = exchanged(sent, ROWS)
     slopes, own_j = called(
@@ -605,7 +625,7 @@
         pair_kernel,
         [(N_COLS, I_BLOCKS + 8, TILE)],
         [sums],
-        [meta],
+        [kept_tiles],
         [pack_i, side_j, radius_i, rad_j, slopes, mask, paired],
     )
     grads = exchanged(grads, COLS)

time: 129 us -> 129 us (level)
  waiting for transfers between devices: 38 us -> 34.3 us
  starting transfers between devices: 44.9 us -> 47.4 us
  Pallas kernels: 26.9 us -> 25.5 us
    all_to_all x6, waiting for transfers between devices: 38 us -> 34.3 us  [exchanged(): return lax.all_to_all(pieces, axes, 0, 0, tiled=True)]
    all_to_all x6, starting transfers between devices: 44.9 us -> 47.4 us  [exchanged(): return lax.all_to_all(pieces, axes, 0, 0, tiled=True)]
    pallas_call x11 -> x12, Pallas kernels: 26.9 us -> 25.5 us  [called(): pl.pallas_call(kernel, out_shape=[jax.ShapeDtypeStruct(*s) if isinstance(...]
  transfers between devices with their start and end apart: 6 -> 6, of which waited for: 6 -> 6; matrix products, arithmetic and copies ran while one was open for 3% -> 4% of each run, Pallas kernels for 7% -> 8%
where the time goes in v7:
time: 129 us; the launch traced here: 128 us
  starting transfers between devices  47.4 us (37%)
  waiting for transfers between devices  34.3 us (27%)
  Pallas kernels  25.5 us (20%)
  blocking collectives  11.9 us (9%)
  other arithmetic  5.32 us (4%)
  local copies, waits for them, and re-layouts  2.72 us (2%)
    all_to_all x6, starting transfers between devices, exchanged(): return lax.all_to_all(pieces, axes, 0, 0, tiled=True)  47.4 us
    all_to_all x6, waiting for transfers between devices, exchanged(): return lax.all_to_all(pieces, axes, 0, 0, tiled=True)  34.3 us
    pallas_call x12, Pallas kernels, called(): pl.pallas_call(kernel, out_shape=[jax.ShapeDtypeStruct(*s) if isinstance(...  25.5 us
    all_to_all x1, blocking collectives, exchanged(): return lax.all_to_all(pieces, axes, 0, 0, tiled=True)  11.9 us
  transfers between devices with their start and end apart: 6, of which 6 were waited for; matrix products, arithmetic and copies ran while one was open for 4% of the time, Pallas kernels for 8%

profile of v7, /device:TPU:1, one launch (start us, length us, event | category | flops | bytes accessed | tf_op | source)
XLA Modules:
  0.0 128.0 jit_solution(9312517203479152232)
XLA Ops:
  0.6 0.7 convert_bitcast_fusion
  1.3 0.0 copy-start.1
  1.4 0.6 copy-done.2
  2.0 0.0 copy-done.1
  2.0 0.0 copy-done.3
  2.0 0.8 concatenate.6.joined
  2.9 1.2 shard_map.94
  4.1 15.6 %all-to-all-start = ((f32[4,3,4,128]{3,2,1,0:T(4,128)}), f32[4,3,4,128]{3,2,1,0:T(4,128)S(1)}, u32[]{:S(2)}, u32[]{:S(2)}) async-start(f32[4,3,4,128]{3,2,1,0:T(4,128)} %get-tuple-element.23), calls=%async_computation | async-start | bytes 49152 | tf_op jit(solution)/shard_map/all_to_all | solution.py:42
  19.8 0.1 eq.88
  19.9 0.1 eq.89
  20.0 0.1 add.224
  20.0 0.1 pad_add_fusion.1.places
  20.1 11.1 %all-to-all-done = f32[4,3,4,128]{3,2,1,0:T(4,128)S(1)} async-done(((f32[4,3,4,128]{3,2,1,0:T(4,128)}), f32[4,3,4,128]{3,2,1,0:T(4,128)S(1)}, u32[]{:S(2)}, u32[]{:S(2)}) %all-to-all-start) | async-done | bytes 24608 | tf_op jit(solution)/shard_map/all_to_all | solution.py:42
  31.2 0.7 broadcast_in_dim.43
  31.9 5.0 %all-to-all-start.1 = ((f32[8,4,3,4,128]{4,3,2,1,0:T(4,128)}), f32[8,4,3,4,128]{4,3,2,1,0:T(4,128)S(1)}, u32[]{:S(2)}, u32[]{:S(2)}) async-start(f32[8,4,3,4,128]{4,3,2,1,0:T(4,128)} %broadcast_in_dim.43), calls=%async_computation.1 | async-start | bytes 393216 | tf_op jit(solution)/shard_map/all_to_all | solution.py:42
  37.0 0.8 fusion.5
  37.7 4.7 %all-to-all-done.1.side_i = f32[8,4,3,4,128]{4,3,2,1,0:T(4,128)S(1)} async-done(((f32[8,4,3,4,128]{4,3,2,1,0:T(4,128)}), f32[8,4,3,4,128]{4,3,2,1,0:T(4,128)S(1)}, u32[]{:S(2)}, u32[]{:S(2)}) %all-to-all-start.1) | async-done | bytes 196640 | tf_op jit(solution)/shard_map/all_to_all | solution.py:42
  42.5 1.3 %shard_map.95 = f32[16,9,4,128]{3,2,1,0:T(4,128)} custom-call(s32[3]{0:T(128)S(1)} %pad_add_fusion.1.places, f32[8,4,3,4,128]{4,3,2,1,0:T(4,128)S(1)} %all-to-all-done.1.side_i), custom_call_target="tpu_custom_call" | custom-call | tf_op jit(solution)/shard_map/pallas_call | solution.py:46
  43.8 9.1 %all-to-all-start.2 = ((f32[16,9,4,128]{3,2,1,0:T(4,128)}), f32[16,9,4,128]{3,2,1,0:T(4,128)S(1)}, u32[]{:S(2)}, u32[]{:S(2)}) async-start(f32[16,9,4,128]{3,2,1,0:T(4,128)} %shard_map.95), calls=%async_computation.2 | async-start | bytes 589824 | tf_op jit(solution)/shard_map/all_to_all | solution.py:42
  53.0 0.6 fusion.11
  53.6 0.1 select_reduce_fusion.1
  53.7 0.1 iota_add_fusion
  53.8 0.1 add.222
  53.8 0.1 convert_element_type.69
  53.9 0.1 convert_element_type.72
  54.0 0.1 select_reduce_fusion
  54.2 1.3 %pad_add_fusion.meta = s32[130]{0:T(256)S(1)} fusion(s32[1]{0:T(128)} %bitcast.10, s32[1]{0:T(128)} %bitcast.9, s32[128]{0:T(128)S(1)} %broadcast_add_fusion), kind=kLoop, calls=%fused_computation.64 | loop fusion | flops 260 | bytes 1040 | tf_op jit(solution)/shard_map/concatenate | solution.py:537
  55.5 1.8 %shard_map.97 = (f32[65,8,128]{2,1,0:T(8,128)S(1)}, f32[64,128]{1,0:T(8,128)S(1)}, f32[5,64,128]{2,1,0:T(8,128)S(1)}, f32[2,128,128]{2,1,0:T(8,128)S(1)}, bf16[4...) custom-call(f32[7,8]{1,0:T(8,128)S(1)} %copy-done, ...), custom_call_target="tpu_custom_call" | custom-call | tf_op jit(solution)/shard_map/pallas_call | solution.py:46
  57.3 7.2 %all-to-all-done.2.side_j = f32[16,9,4,128]{3,2,1,0:T(4,128)S(1)} async-done(((f32[16,9,4,128]{3,2,1,0:T(4,128)}), f32[16,9,4,128]{3,2,1,0:T(4,128)S(1)}, u32[]{:S(2)}, u32[]{:S(2)}) %all-to-all-start.2) | async-done | bytes 294944 | tf_op jit(solution)/shard_map/all_to_all | solution.py:42
  64.5 6.0 %shard_map.100 = f32[8,64,128]{2,1,0:T(8,128)} custom-call(s32[130]{0:T(256)S(1)} %pad_add_fusion.meta, f32[65,8,128]{2,1,0:T(8,128)S(1)} %get-tuple-element.24.pack_i, f32[16,9,4,128]{3,2,1,0:T(4,128)S(1)} %all-to-all-done.2.side_j, f32[2,128,128]{2,1,0:T(8,128)S(1)} %get-tuple-element.27.mask_ref, bf16[48,768]{1,0:T(8,128)(2,1)S(1)} %get-tuple-element.25.spread_ref), custom_call_target="tpu_custom_call" | custom-call | tf_op jit(solution)/shard_map/pallas_call | solution.py:46
  70.5 5.4 %all-to-all-start.3 = ((f32[8,64,128]{2,1,0:T(8,128)}), f32[8,64,128]{2,1,0:T(8,128)S(1)}, u32[]{:S(2)}, u32[]{:S(2)}) async-start(f32[8,64,128]{2,1,0:T(8,128)} %shard_map.100), calls=%async_computation.3 | async-start | bytes 524288 | tf_op jit(solution)/shard_map/all_to_all | solution.py:42
  76.0 0.2 broadcast_select_fusion
  76.1 1.2 fusion
  77.4 1.6 %shard_map.99.ready_too.meta = s32[137]{0:T(256)S(1)} custom-call(s32[130]{0:T(256)S(1)} %pad_add_fusion.meta, s32[64]{0:T(128)S(1)} %or_convert_fusion.read), custom_call_target="tpu_custom_call" | custom-call | tf_op jit(solution)/shard_map/pallas_call | solution.py:46
  78.9 0.1 and_select_fusion.3
  79.0 2.6 %shard_map.96.ready.picked = s32[2057]{0:T(1024)S(1)} custom-call(f32[32,128]{1,0:T(8,128)S(1)} %bitcast.15), custom_call_target="tpu_custom_call" | custom-call | tf_op jit(solution)/shard_map/pallas_call | solution.py:46
  81.6 0.2 all-to-all-done.3.parts
  81.8 1.3 shard_map.101
  83.0 3.5 %all-to-all-start.4 = ((f32[16,2,8,128]{3,2,1,0:T(8,128)}), f32[16,2,8,128]{3,2,1,0:T(8,128)S(1)}, u32[]{:S(2)}, u32[]{:S(2)}) async-start(f32[16,2,8,128]{3,2,1,0:T(8,128)} %get-tuple-element.31), calls=%async_computation.4 | async-start | bytes 262144 | tf_op jit(solution)/shard_map/all_to_all | solution.py:42
  86.5 1.5 %shard_map.98 = (f32[8,8,128]{2,1,0:T(8,128)S(1)}, f32[33,8,128]{2,1,0:T(8,128)S(1)}) custom-call(s32[130]{0:T(256)S(1)} %pad_add_fusion.meta, s32[3]{0:T(128)S(1)} %pad_add_fusion.1.places, f32[7,8]{1,0:T(8,128)S(1)} %copy-done, f32[65,8,128]{2,1,0:T(8,128)S(1)} %get-tuple-element.24.pack_i, f32[16,9,4,128]{3,2,1,0:T(4,128)S(1)} %all-to-all-done.2.side_j, ...), custom_call_target="tpu_custom_call" | custom-call | tf_op jit(solution)/shard_map/pallas_call | solution.py:46
  88.1 6.8 %all-to-all-done.4.rad_j = f32[16,2,8,128]{3,2,1,0:T(8,128)S(1)} async-done(((f32[16,2,8,128]{3,2,1,0:T(8,128)}), f32[16,2,8,128]{3,2,1,0:T(8,128)S(1)}, u32[]{:S(2)}, u32[]{:S(2)}) %all-to-all-start.4) | async-done | bytes 131104 | tf_op jit(solution)/shard_map/all_to_all | solution.py:42
  94.9 2.1 %shard_map.102 = f32[8,72,128]{2,1,0:T(8,128)} custom-call(s32[137]{0:T(256)S(1)} %shard_map.99.ready_too.meta, f32[65,8,128]{2,1,0:T(8,128)S(1)} %get-tuple-element.24.pack_i, f32[16,9,4,128]{3,2,1,0:T(4,128)S(1)} %all-to-all-done.2.side_j, f32[72,128]{1,0:T(8,128)S(1)} %get-tuple-element.30.rad_i.radius_i.radius, ...), custom_call_target="tpu_custom_call" | custom-call | tf_op jit(solution)/shard_map/pallas_call | solution.py:46
  97.1 8.7 %all-to-all-start.5 = ((f32[8,72,128]{2,1,0:T(8,128)}), f32[8,72,128]{2,1,0:T(8,128)S(1)}, u32[]{:S(2)}, u32[]{:S(2)}) async-start(f32[8,72,128]{2,1,0:T(8,128)} %shard_map.102), calls=%async_computation.5 | async-start | bytes 589824 | tf_op jit(solution)/shard_map/all_to_all | solution.py:42
  105.8 2.6 %shard_map.103.direct = f32[3,32,128]{2,1,0:T(8,128)S(1)} custom-call(s32[2057]{0:T(1024)S(1)} %shard_map.96.ready.picked, s32[3]{0:T(128)S(1)} %pad_add_fusion.1.places, f32[33,8,128]{2,1,0:T(8,128)S(1)} %get-tuple-element.26.own_j, f32[65,8,128]{2,1,0:T(8,128)S(1)} %get-tuple-element.24.pack_i, f32[16,2,8,128]{3,2,1,0:T(8,128)S(1)} %all-to-all-done.4.rad_j, ...), custom_call_target="tpu_custom_call" | custom-call | tf_op jit(solution)/shard_map/pallas_call | solution.py:46
  108.4 4.3 %all-to-all-done.5.parts = f32[8,72,128]{2,1,0:T(8,128)S(1)} async-done(((f32[8,72,128]{2,1,0:T(8,128)}), f32[8,72,128]{2,1,0:T(8,128)S(1)}, u32[]{:S(2)}, u32[]{:S(2)}) %all-to-all-start.5) | async-done | bytes 294944 | tf_op jit(solution)/shard_map/all_to_all | solution.py:42
  112.7 2.8 %shard_map.104 = (f32[16,8,128]{2,1,0:T(8,128)S(1)}, f32[10,128]{1,0:T(8,128)S(1)}) custom-call(s32[2057]{0:T(1024)S(1)} %shard_map.96.ready.picked, s32[3]{0:T(128)S(1)} %pad_add_fusion.1.places, f32[65,8,128]{2,1,0:T(8,128)S(1)} %get-tuple-element.24.pack_i, f32[33,8,128]{2,1,0:T(8,128)S(1)} %get-tuple-element.26.own_j, ...), custom_call_target="tpu_custom_call" | custom-call | tf_op jit(solution)/shard_map/pallas_call | solution.py:46
  115.5 11.9 %all_to_all.35.parts = f32[16,8,128]{2,1,0:T(8,128)S(1)} all-to-all(f32[16,8,128]{2,1,0:T(8,128)S(1)} %get-tuple-element.36), channel_id=1, replica_groups=mesh['zh'=4,'zl'=4,'yh'=2,'core'=2,'x'=4,'yl'=2] {'zl','yh','core'}, dimensions={0} | all-to-all | bytes 131072 | tf_op jit(solution)/shard_map/all_to_all | solution.py:42
  127.4 0.6 shard_map.105
  (19 shorter events, 0.1 us)
Async XLA Ops:
  0.6 0.7 copy-start.4
  1.3 0.7 copy-start.2
  1.3 0.7 copy-start.1
  1.4 0.7 copy-start.3
  2.0 0.8 copy-start
  4.1 27.1 %all-to-all-start = ((f32[4,3,4,128]{3,2,1,0:T(4,128)}), f32[4,3,4,128]{3,2,1,0:T(4,128)S(1)}, u32[]{:S(2)}, u32[]{:S(2)}) async-start(f32[4,3,4,128]{3,2,1,0:T(4,128)} %get-tuple-element.23), calls=%async_computation | async-start | bytes 49152 | tf_op jit(solution)/shard_map/all_to_all | solution.py:42
  31.9 10.6 %all-to-all-start.1 = ((f32[8,4,3,4,128]{4,3,2,1,0:T(4,128)}), f32[8,4,3,4,128]{4,3,2,1,0:T(4,128)S(1)}, u32[]{:S(2)}, u32[]{:S(2)}) async-start(f32[8,4,3,4,128]{4,3,2,1,0:T(4,128)} %broadcast_in_dim.43), calls=%async_computation.1 | async-start | bytes 393216 | tf_op jit(solution)/shard_map/all_to_all | solution.py:42
  43.8 20.7 %all-to-all-start.2 = ((f32[16,9,4,128]{3,2,1,0:T(4,128)}), f32[16,9,4,128]{3,2,1,0:T(4,128)S(1)}, u32[]{:S(2)}, u32[]{:S(2)}) async-start(f32[16,9,4,128]{3,2,1,0:T(4,128)} %shard_map.95), calls=%async_computation.2 | async-start | bytes 589824 | tf_op jit(solution)/shard_map/all_to_all | solution.py:42
  70.5 11.2 %all-to-all-start.3 = ((f32[8,64,128]{2,1,0:T(8,128)}), f32[8,64,128]{2,1,0:T(8,128)S(1)}, u32[]{:S(2)}, u32[]{:S(2)}) async-start(f32[8,64,128]{2,1,0:T(8,128)} %shard_map.100), calls=%async_computation.3 | async-start | bytes 524288 | tf_op jit(solution)/shard_map/all_to_all | solution.py:42
  83.0 11.9 %all-to-all-start.4 = ((f32[16,2,8,128]{3,2,1,0:T(8,128)}), f32[16,2,8,128]{3,2,1,0:T(8,128)S(1)}, u32[]{:S(2)}, u32[]{:S(2)}) async-start(f32[16,2,8,128]{3,2,1,0:T(8,128)} %get-tuple-element.31), calls=%async_computation.4 | async-start | bytes 262144 | tf_op jit(solution)/shard_map/all_to_all | solution.py:42
  97.1 15.6 %all-to-all-start.5 = ((f32[8,72,128]{2,1,0:T(8,128)}), f32[8,72,128]{2,1,0:T(8,128)S(1)}, u32[]{:S(2)}, u32[]{:S(2)}) async-start(f32[8,72,128]{2,1,0:T(8,128)} %shard_map.102), calls=%async_computation.5 | async-start | bytes 589824 | tf_op jit(solution)/shard_map/all_to_all | solution.py:42

commit v8 on v7

--- a/solution.py
+++ b/solution.py
@@ -19,7 +19,8 @@
 OFFSET = 0.09
 NECK_GAP = 0.5
 NECK_WIDTH = 16.0
-INV_SQ = 1.0 / (CUTOFF * CUTOFF)
+CUT_SQ = CUTOFF * CUTOFF
+TAPER = 1.0 / (CUT_SQ * CUT_SQ)
 LOG2E = 1.4426950408889634
 NO_KEY = 16777216.0
 
@@ -272,7 +273,7 @@
         total = jnp.zeros((8, TILE), F32)
         for s in range(0, TILE, CHUNK):
             _, _, _, q = offsets(xi, yi, zi, col, s)
-            base = jnp.maximum(1.0 - q * INV_SQ, 0.0)
+            base = jnp.maximum(CUT_SQ - q, 0.0)
             weight = base * base * mask_ref[same, s : s + CHUNK, :]
             inv = 1.0 / (q + rho_sq)
             gap = rho_gap + col(s, 3)
@@ -286,12 +287,12 @@
         return add
 
     for_each_tile(meta, 0, meta[LISTED], one_tile)
-    born = jnp.sum(acc[0:I_BLOCKS], axis=1)
+    born = TAPER * jnp.sum(acc[0:I_BLOCKS], axis=1)
     for n in range(N_COLS):
         out_ref[n] = born
 
 
-def radius_kernel(places, parts, pack_i, more_i, charge, ready, ready_too, radius_ref, sent_ref, rate_ref):
+def radius_kernel(places, parts, pack_i, more_i, charge, ready, radius_ref, sent_ref, rate_ref):
     born = parts[0]
     for n in range(1, N_COLS):
         born = born + parts[n]
@@ -329,15 +330,14 @@
         sums = [jnp.zeros((8, TILE), F32)] * 3
         for s in range(0, TILE, CHUNK):
             dx, dy, dz, q = offsets(xi, yi, zi, col, s)
-            base = jnp.maximum(1.0 - q * INV_SQ, 0.0)
-            weight = base * base
-            w_slope = (-2.0 * INV_SQ) * base
+            base = jnp.maximum(CUT_SQ - q, 0.0)
             gap = rho_gap + col(s, 3)
             off = q - gap * gap
             bump = jnp.exp2(off * off * (-LOG2E / NECK_WIDTH))
-            bump = bump * (w_slope - weight * off * (2.0 / NECK_WIDTH))
+            bump = bump * (2.0 + base * off * (2.0 / NECK_WIDTH))
             inv = 1.0 / (q + rho_sq)
-            slope = col(s, 4) * (inv * inv) * (w_slope - 2.0 * weight * inv) + col(s, 5) * bump
+            slope = col(s, 4) * (inv * inv) * (2.0 + (base + base) * inv) + col(s, 5) * bump
+            slope = slope * base
             sums = [a + folded(slope * d) for a, d in zip(sums, (dx, dy, dz))]
 
         def add():
@@ -350,6 +350,7 @@
     for n in range(N_COLS):
         for b in range(2):
             total = jnp.sum(force[n * HELD + places[0] * 2 + b], axis=1)
+            total = -TAPER * total
             out_ref[n, 3 * b : 3 * b + 3, :] = total
         out_ref[n, 6:8, :] = total[0:2]
 
@@ -376,11 +377,11 @@
         sums = [jnp.zeros((8, TILE), F32)] * 3
         for s in range(0, TILE, CHUNK):
             dx, dy, dz, q = offsets(xi, yi, zi, col, s)
-            base = jnp.maximum(1.0 - q * INV_SQ, 0.0)
+            base = jnp.maximum(CUT_SQ - q, 0.0)
             decay = jnp.exp2(q * (quarter * col(s, 4)) * -LOG2E)
             inv = lax.rsqrt(q + radius * col(s, 3) * decay)
-            slope = (-2.0 * INV_SQ) * base - base * base * (inv * inv) * (0.5 - 0.125 * decay)
-            slope = slope * (inv * col(s, 5))
+            slope = 2.0 + base * (inv * inv) * (0.5 - 0.125 * decay)
+            slope = slope * (base * (inv * col(s, 5)))
             sums = [a + folded(slope * d) for a, d in zip(sums, (dx, dy, dz))]
 
         def add():
@@ -390,13 +391,13 @@
         return add
 
     for_each_tile(picked, 0, picked[PICKED + UNROLL], one_tile)
-    scale = (2.0 * COULOMB) * own_q[...]
+    scale = (-2.0 * COULOMB * TAPER) * own_q[...]
     for c in range(3):
         out_ref[c] = scale * jnp.sum(force[0 : 2 * N_ROWS, c], axis=1)
 
 
 def pair_kernel(
-    meta, pack_i, side_j, rad_i, rad_j, slopes, mask_ref, spread_ref, out_ref, acc
+    meta, pack_i, side_j, rad_i, rad_j, slopes, ready, mask_ref, spread_ref, out_ref, acc
 ):
     acc[...] = jnp.zeros_like(acc)
 
@@ -415,7 +416,7 @@
         total = jnp.zeros((8, TILE), F32)
         for s in range(0, TILE, CHUNK):
             _, _, _, q = offsets(xi, yi, zi, col, s)
-            base = jnp.maximum(1.0 - q * INV_SQ, 0.0)
+            base = jnp.maximum(CUT_SQ - q, 0.0)
             weight = base * base * mask_ref[same, s : s + CHUNK, :]
             arg = q * (quarter_i * col(s, 4))
             decay = jnp.exp2(arg * -LOG2E)
@@ -429,7 +430,7 @@
         return add
 
     for_each_tile(meta, 0, meta[LISTED + UNROLL], one_tile)
-    grads = jnp.sum(acc[0:I_BLOCKS], axis=1)
+    grads = TAPER * jnp.sum(acc[0:I_BLOCKS], axis=1)
     for n in range(N_COLS):
         out_ref[n, 0:I_BLOCKS] = grads
         out_ref[n, I_BLOCKS : I_BLOCKS + 8] = slopes[n]
@@ -458,17 +459,15 @@
         sums = [jnp.zeros((8, TILE), F32)] * 3
         for s in range(0, TILE, CHUNK):
             dx, dy, dz, q = offsets(xi, yi, zi, col, s)
-            base = jnp.maximum(1.0 - q * INV_SQ, 0.0)
-            weight = base * base
-            w_slope = (-2.0 * INV_SQ) * base
+            base = jnp.maximum(CUT_SQ - q, 0.0)
             rho_j = col(s, 3)
             gap = rho_gap + rho_j
             off = q - gap * gap
             bump = jnp.exp2(off * off * (-LOG2E / NECK_WIDTH))
-            bump = bump * (w_slope - weight * off * (2.0 / NECK_WIDTH))
+            bump = bump * (2.0 + base * off * (2.0 / NECK_WIDTH))
             inv = 1.0 / (q + rho_j * rho_j)
-            slope = vol * (inv * inv) * (w_slope - 2.0 * weight * inv) + neck * bump
-            slope = slope * col(s, 4)
+            slope = vol * (inv * inv) * (2.0 + (base + base) * inv) + neck * bump
+            slope = slope * (base * col(s, 4))
             sums = [a + folded(slope * d) for a, d in zip(sums, (dx, dy, dz))]
 
         def add():
@@ -479,7 +478,7 @@
 
     for_each_tile(picked, 0, picked[PICKED + UNROLL], one_tile)
     for k in range(3):
-        value = direct[k] - 2.0 * jnp.sum(force[0 : 2 * N_ROWS, k], axis=1)
+        value = direct[k] + (2.0 * TAPER) * jnp.sum(force[0 : 2 * N_ROWS, k], axis=1)
         for n in range(N_ROWS):
             out_ref[n, 2 * k : 2 * k + 2, :] = value[2 * n : 2 * n + 2]
             if k == 2:
@@ -611,7 +610,7 @@
         [(I_BLOCKS + 8, TILE), (N_ROWS, 2, HELD, TILE), (I_BLOCKS, TILE)],
         [],
         [places],
-        [born_parts, pack_i, more_i, charge_i, picked, kept_tiles],
+        [born_parts, pack_i, more_i, charge_i, kept_tiles],
     )
     rad_j = exchanged(sent, ROWS)
     slopes, own_j = called(
@@ -626,7 +625,7 @@
         [(N_COLS, I_BLOCKS + 8, TILE)],
         [sums],
         [kept_tiles],
-        [pack_i, side_j, radius_i, rad_j, slopes, mask, paired],
+        [pack_i, side_j, radius_i, rad_j, slopes, picked, mask, paired],
     )
     grads = exchanged(grads, COLS)
     [direct] = called(

time: 129 us -> 128 us (level)
  Pallas kernels: 25.5 us -> 21.2 us
  blocking collectives: 11.9 us -> 14.6 us
  starting transfers between devices: 47.4 us -> 48.8 us
    pallas_call x12, Pallas kernels: 25.5 us -> 21.2 us  [called(): pl.pallas_call(kernel, out_shape=[jax.ShapeDtypeStruct(*s) if isinstance(...]
    all_to_all x1, blocking collectives: 11.9 us -> 14.6 us  [exchanged(): return lax.all_to_all(pieces, axes, 0, 0, tiled=True)]
    all_to_all x6, starting transfers between devices: 47.4 us -> 48.8 us  [exchanged(): return lax.all_to_all(pieces, axes, 0, 0, tiled=True)]
  transfers between devices with their start and end apart: 6 -> 6, of which waited for: 6 -> 6; matrix products, arithmetic and copies ran while one was open for 4% -> 4% of each run, Pallas kernels for 8% -> 7%
where the time goes in v8:
time: 128 us
  starting transfers between devices  48.8 us (38%)
  waiting for transfers between devices  34.3 us (27%)
  Pallas kernels  21.2 us (17%)
  blocking collectives  14.6 us (11%)
  other arithmetic  5.32 us (4%)
  local copies, waits for them, and re-layouts  2.72 us (2%)
    all_to_all x6, starting transfers between devices, exchanged(): return lax.all_to_all(pieces, axes, 0, 0, tiled=True)  48.8 us
    all_to_all x6, waiting for transfers between devices, exchanged(): return lax.all_to_all(pieces, axes, 0, 0, tiled=True)  34.3 us
    pallas_call x12, Pallas kernels, called(): pl.pallas_call(kernel, out_shape=[jax.ShapeDtypeStruct(*s) if isinstance(...  21.2 us
    all_to_all x1, blocking collectives, exchanged(): return lax.all_to_all(pieces, axes, 0, 0, tiled=True)  14.6 us
  transfers between devices with their start and end apart: 6, of which 6 were waited for; matrix products, arithmetic and copies ran while one was open for 4% of the time, Pallas kernels for 7%

profile of v8, /device:TPU:1, one launch (start us, length us, event | category | flops | bytes accessed | tf_op | source)
XLA Modules:
  0.0 127.7 jit_solution(10965038129686066589)
XLA Ops:
  0.6 0.7 convert_bitcast_fusion
  1.3 0.0 copy-start.1
  1.4 0.6 copy-done.2
  2.0 0.0 copy-done.1
  2.0 0.0 copy-done.3
  2.0 0.8 concatenate.6.joined
  2.9 1.2 shard_map.94
  4.1 15.6 %all-to-all-start = ((f32[4,3,4,128]{3,2,1,0:T(4,128)}), f32[4,3,4,128]{3,2,1,0:T(4,128)S(1)}, u32[]{:S(2)}, u32[]{:S(2)}) async-start(f32[4,3,4,128]{3,2,1,0:T(4,128)} %get-tuple-element.23), calls=%async_computation | async-start | bytes 49152 | tf_op jit(solution)/shard_map/all_to_all | solution.py:43
  19.8 0.1 eq.88
  19.9 0.1 eq.89
  19.9 0.1 add.224
  20.0 0.1 pad_add_fusion.1.places
  20.1 11.1 %all-to-all-done = f32[4,3,4,128]{3,2,1,0:T(4,128)S(1)} async-done(((f32[4,3,4,128]{3,2,1,0:T(4,128)}), f32[4,3,4,128]{3,2,1,0:T(4,128)S(1)}, u32[]{:S(2)}, u32[]{:S(2)}) %all-to-all-start) | async-done | bytes 24608 | tf_op jit(solution)/shard_map/all_to_all | solution.py:43
  31.2 0.7 broadcast_in_dim.43
  31.9 5.0 %all-to-all-start.1 = ((f32[8,4,3,4,128]{4,3,2,1,0:T(4,128)}), f32[8,4,3,4,128]{4,3,2,1,0:T(4,128)S(1)}, u32[]{:S(2)}, u32[]{:S(2)}) async-start(f32[8,4,3,4,128]{4,3,2,1,0:T(4,128)} %broadcast_in_dim.43), calls=%async_computation.1 | async-start | bytes 393216 | tf_op jit(solution)/shard_map/all_to_all | solution.py:43
  37.0 0.8 fusion.5
  37.7 4.7 %all-to-all-done.1.side_i = f32[8,4,3,4,128]{4,3,2,1,0:T(4,128)S(1)} async-done(((f32[8,4,3,4,128]{4,3,2,1,0:T(4,128)}), f32[8,4,3,4,128]{4,3,2,1,0:T(4,128)S(1)}, u32[]{:S(2)}, u32[]{:S(2)}) %all-to-all-start.1) | async-done | bytes 196640 | tf_op jit(solution)/shard_map/all_to_all | solution.py:43
  42.5 1.3 %shard_map.95 = f32[16,9,4,128]{3,2,1,0:T(4,128)} custom-call(s32[3]{0:T(128)S(1)} %pad_add_fusion.1.places, f32[8,4,3,4,128]{4,3,2,1,0:T(4,128)S(1)} %all-to-all-done.1.side_i), custom_call_target="tpu_custom_call" | custom-call | tf_op jit(solution)/shard_map/pallas_call | solution.py:47
  43.8 9.1 %all-to-all-start.2 = ((f32[16,9,4,128]{3,2,1,0:T(4,128)}), f32[16,9,4,128]{3,2,1,0:T(4,128)S(1)}, u32[]{:S(2)}, u32[]{:S(2)}) async-start(f32[16,9,4,128]{3,2,1,0:T(4,128)} %shard_map.95), calls=%async_computation.2 | async-start | bytes 589824 | tf_op jit(solution)/shard_map/all_to_all | solution.py:43
  53.0 0.6 fusion.11
  53.6 0.1 select_reduce_fusion.1
  53.7 0.1 iota_add_fusion
  53.8 0.1 add.222
  53.8 0.1 convert_element_type.69
  53.9 0.1 convert_element_type.72
  54.0 0.1 select_reduce_fusion
  54.2 1.3 %pad_add_fusion.meta = s32[130]{0:T(256)S(1)} fusion(s32[1]{0:T(128)} %bitcast.10, s32[1]{0:T(128)} %bitcast.9, s32[128]{0:T(128)S(1)} %broadcast_add_fusion), kind=kLoop, calls=%fused_computation.64 | loop fusion | flops 260 | bytes 1040 | tf_op jit(solution)/shard_map/concatenate | solution.py:536
  55.5 1.8 %shard_map.97 = (f32[65,8,128]{2,1,0:T(8,128)S(1)}, f32[64,128]{1,0:T(8,128)S(1)}, f32[5,64,128]{2,1,0:T(8,128)S(1)}, f32[2,128,128]{2,1,0:T(8,128)S(1)}, bf16[4...) custom-call(f32[7,8]{1,0:T(8,128)S(1)} %copy-done, ...), custom_call_target="tpu_custom_call" | custom-call | tf_op jit(solution)/shard_map/pallas_call | solution.py:47
  57.3 7.2 %all-to-all-done.2.side_j = f32[16,9,4,128]{3,2,1,0:T(4,128)S(1)} async-done(((f32[16,9,4,128]{3,2,1,0:T(4,128)}), f32[16,9,4,128]{3,2,1,0:T(4,128)S(1)}, u32[]{:S(2)}, u32[]{:S(2)}) %all-to-all-start.2) | async-done | bytes 294944 | tf_op jit(solution)/shard_map/all_to_all | solution.py:43
  64.5 3.2 %shard_map.100 = f32[8,64,128]{2,1,0:T(8,128)} custom-call(s32[130]{0:T(256)S(1)} %pad_add_fusion.meta, f32[65,8,128]{2,1,0:T(8,128)S(1)} %get-tuple-element.24.pack_i, f32[16,9,4,128]{3,2,1,0:T(4,128)S(1)} %all-to-all-done.2.side_j, f32[2,128,128]{2,1,0:T(8,128)S(1)} %get-tuple-element.27.mask_ref, bf16[48,768]{1,0:T(8,128)(2,1)S(1)} %get-tuple-element.25.spread_ref), custom_call_target="tpu_custom_call" | custom-call | tf_op jit(solution)/shard_map/pallas_call | solution.py:47
  67.7 5.2 %all-to-all-start.3 = ((f32[8,64,128]{2,1,0:T(8,128)}), f32[8,64,128]{2,1,0:T(8,128)S(1)}, u32[]{:S(2)}, u32[]{:S(2)}) async-start(f32[8,64,128]{2,1,0:T(8,128)} %shard_map.100), calls=%async_computation.3 | async-start | bytes 524288 | tf_op jit(solution)/shard_map/all_to_all | solution.py:43
  72.9 0.2 broadcast_select_fusion
  73.1 1.2 fusion
  74.3 1.3 %shard_map.99.ready.meta = s32[137]{0:T(256)S(1)} custom-call(s32[130]{0:T(256)S(1)} %pad_add_fusion.meta, s32[64]{0:T(128)S(1)} %or_convert_fusion.read), custom_call_target="tpu_custom_call" | custom-call | tf_op jit(solution)/shard_map/pallas_call | solution.py:47
  75.6 3.1 %all-to-all-done.3.parts = f32[8,64,128]{2,1,0:T(8,128)S(1)} async-done(((f32[8,64,128]{2,1,0:T(8,128)}), f32[8,64,128]{2,1,0:T(8,128)S(1)}, u32[]{:S(2)}, u32[]{:S(2)}) %all-to-all-start.3) | async-done | bytes 262176 | tf_op jit(solution)/shard_map/all_to_all | solution.py:43
  78.7 1.3 shard_map.101
  79.9 7.9 %all-to-all-start.4 = ((f32[16,2,8,128]{3,2,1,0:T(8,128)}), f32[16,2,8,128]{3,2,1,0:T(8,128)S(1)}, u32[]{:S(2)}, u32[]{:S(2)}) async-start(f32[16,2,8,128]{3,2,1,0:T(8,128)} %get-tuple-element.31), calls=%async_computation.4 | async-start | bytes 262144 | tf_op jit(solution)/shard_map/all_to_all | solution.py:43
  87.8 0.1 and_select_fusion.3
  87.9 2.3 %shard_map.96.ready.picked = s32[2057]{0:T(1024)S(1)} custom-call(f32[32,128]{1,0:T(8,128)S(1)} %bitcast.15), custom_call_target="tpu_custom_call" | custom-call | tf_op jit(solution)/shard_map/pallas_call | solution.py:47
  90.2 1.5 %shard_map.98 = (f32[8,8,128]{2,1,0:T(8,128)S(1)}, f32[33,8,128]{2,1,0:T(8,128)S(1)}) custom-call(s32[130]{0:T(256)S(1)} %pad_add_fusion.meta, s32[3]{0:T(128)S(1)} %pad_add_fusion.1.places, f32[7,8]{1,0:T(8,128)S(1)} %copy-done, f32[65,8,128]{2,1,0:T(8,128)S(1)} %get-tuple-element.24.pack_i, f32[16,9,4,128]{3,2,1,0:T(4,128)S(1)} %all-to-all-done.2.side_j, ...), custom_call_target="tpu_custom_call" | custom-call | tf_op jit(solution)/shard_map/pallas_call | solution.py:47
  91.8 4.5 %all-to-all-done.4.rad_j = f32[16,2,8,128]{3,2,1,0:T(8,128)S(1)} async-done(((f32[16,2,8,128]{3,2,1,0:T(8,128)}), f32[16,2,8,128]{3,2,1,0:T(8,128)S(1)}, u32[]{:S(2)}, u32[]{:S(2)}) %all-to-all-start.4) | async-done | bytes 131104 | tf_op jit(solution)/shard_map/all_to_all | solution.py:43
  96.3 2.1 %shard_map.102 = f32[8,72,128]{2,1,0:T(8,128)} custom-call(s32[137]{0:T(256)S(1)} %shard_map.99.ready.meta, f32[65,8,128]{2,1,0:T(8,128)S(1)} %get-tuple-element.24.pack_i, f32[16,9,4,128]{3,2,1,0:T(4,128)S(1)} %all-to-all-done.2.side_j, f32[72,128]{1,0:T(8,128)S(1)} %get-tuple-element.30.rad_i.radius_i.radius, f32[16,2,8,128]{3,2,1,0:T(8,128)S(1)} %all-to-all-done.4.rad_j, ...), custom_call_target="tpu_custom_call" | custom-call | tf_op jit(solution)/shard_map/pallas_call | solution.py:47
  98.4 5.9 %all-to-all-start.5 = ((f32[8,72,128]{2,1,0:T(8,128)}), f32[8,72,128]{2,1,0:T(8,128)S(1)}, u32[]{:S(2)}, u32[]{:S(2)}) async-start(f32[8,72,128]{2,1,0:T(8,128)} %shard_map.102), calls=%async_computation.5 | async-start | bytes 589824 | tf_op jit(solution)/shard_map/all_to_all | solution.py:43
  104.3 2.2 %shard_map.103.direct = f32[3,32,128]{2,1,0:T(8,128)S(1)} custom-call(s32[2057]{0:T(1024)S(1)} %shard_map.96.ready.picked, s32[3]{0:T(128)S(1)} %pad_add_fusion.1.places, f32[33,8,128]{2,1,0:T(8,128)S(1)} %get-tuple-element.26.own_j, f32[65,8,128]{2,1,0:T(8,128)S(1)} %get-tuple-element.24.pack_i, f32[16,2,8,128]{3,2,1,0:T(8,128)S(1)} %all-to-all-done.4.rad_j, ...), custom_call_target="tpu_custom_call" | custom-call | tf_op jit(solution)/shard_map/pallas_call | solution.py:47
  106.5 3.7 %all-to-all-done.5.parts = f32[8,72,128]{2,1,0:T(8,128)S(1)} async-done(((f32[8,72,128]{2,1,0:T(8,128)}), f32[8,72,128]{2,1,0:T(8,128)S(1)}, u32[]{:S(2)}, u32[]{:S(2)}) %all-to-all-start.5) | async-done | bytes 294944 | tf_op jit(solution)/shard_map/all_to_all | solution.py:43
  110.2 2.3 %shard_map.104 = (f32[16,8,128]{2,1,0:T(8,128)S(1)}, f32[10,128]{1,0:T(8,128)S(1)}) custom-call(s32[2057]{0:T(1024)S(1)} %shard_map.96.ready.picked, s32[3]{0:T(128)S(1)} %pad_add_fusion.1.places, f32[65,8,128]{2,1,0:T(8,128)S(1)} %get-tuple-element.24.pack_i, f32[33,8,128]{2,1,0:T(8,128)S(1)} %get-tuple-element.26.own_j, ...), custom_call_target="tpu_custom_call" | custom-call | tf_op jit(solution)/shard_map/pallas_call | solution.py:47
  112.5 14.6 %all_to_all.35.parts = f32[16,8,128]{2,1,0:T(8,128)S(1)} all-to-all(f32[16,8,128]{2,1,0:T(8,128)S(1)} %get-tuple-element.36), channel_id=1, replica_groups=mesh['zh'=4,'zl'=4,'yh'=2,'core'=2,'x'=4,'yl'=2] {'zl','yh','core'}, dimensions={0} | all-to-all | bytes 131072 | tf_op jit(solution)/shard_map/all_to_all | solution.py:43
  127.1 0.6 shard_map.105
  (19 shorter events, 0.1 us)
Async XLA Ops:
  0.6 0.7 copy-start.4
  1.3 0.7 copy-start.2
  1.3 0.7 copy-start.1
  1.4 0.7 copy-start.3
  2.0 0.8 copy-start
  4.1 27.1 %all-to-all-start = ((f32[4,3,4,128]{3,2,1,0:T(4,128)}), f32[4,3,4,128]{3,2,1,0:T(4,128)S(1)}, u32[]{:S(2)}, u32[]{:S(2)}) async-start(f32[4,3,4,128]{3,2,1,0:T(4,128)} %get-tuple-element.23), calls=%async_computation | async-start | bytes 49152 | tf_op jit(solution)/shard_map/all_to_all | solution.py:43
  31.9 10.6 %all-to-all-start.1 = ((f32[8,4,3,4,128]{4,3,2,1,0:T(4,128)}), f32[8,4,3,4,128]{4,3,2,1,0:T(4,128)S(1)}, u32[]{:S(2)}, u32[]{:S(2)}) async-start(f32[8,4,3,4,128]{4,3,2,1,0:T(4,128)} %broadcast_in_dim.43), calls=%async_computation.1 | async-start | bytes 393216 | tf_op jit(solution)/shard_map/all_to_all | solution.py:43
  43.8 20.7 %all-to-all-start.2 = ((f32[16,9,4,128]{3,2,1,0:T(4,128)}), f32[16,9,4,128]{3,2,1,0:T(4,128)S(1)}, u32[]{:S(2)}, u32[]{:S(2)}) async-start(f32[16,9,4,128]{3,2,1,0:T(4,128)} %shard_map.95), calls=%async_computation.2 | async-start | bytes 589824 | tf_op jit(solution)/shard_map/all_to_all | solution.py:43
  67.7 11.0 %all-to-all-start.3 = ((f32[8,64,128]{2,1,0:T(8,128)}), f32[8,64,128]{2,1,0:T(8,128)S(1)}, u32[]{:S(2)}, u32[]{:S(2)}) async-start(f32[8,64,128]{2,1,0:T(8,128)} %shard_map.100), calls=%async_computation.3 | async-start | bytes 524288 | tf_op jit(solution)/shard_map/all_to_all | solution.py:43
  79.9 16.3 %all-to-all-start.4 = ((f32[16,2,8,128]{3,2,1,0:T(8,128)}), f32[16,2,8,128]{3,2,1,0:T(8,128)S(1)}, u32[]{:S(2)}, u32[]{:S(2)}) async-start(f32[16,2,8,128]{3,2,1,0:T(8,128)} %get-tuple-element.31), calls=%async_computation.4 | async-start | bytes 262144 | tf_op jit(solution)/shard_map/all_to_all | solution.py:43
  98.4 11.8 %all-to-all-start.5 = ((f32[8,72,128]{2,1,0:T(8,128)}), f32[8,72,128]{2,1,0:T(8,128)S(1)}, u32[]{:S(2)}, u32[]{:S(2)}) async-start(f32[8,72,128]{2,1,0:T(8,128)} %shard_map.102), calls=%async_computation.5 | async-start | bytes 589824 | tf_op jit(solution)/shard_map/all_to_all | solution.py:43

commit v9 on v8

--- a/solution.py
+++ b/solution.py
@@ -143,23 +143,23 @@
         spread_ref[:, (3 + c) * TILE : (4 + c) * TILE] = part.astype(jnp.bfloat16)
 
 
-def typed_columns(atoms, spread_ref):
+def typed_columns(atoms, spread):
     high = atoms.astype(jnp.bfloat16).astype(F32)
     rest = atoms - high
     middle = rest.astype(jnp.bfloat16).astype(F32)
     kinds = lax.broadcasted_iota(jnp.int32, (8, TILE), 0).astype(F32)
     hot = jnp.where(atoms[3:4, :] == kinds, 1.0, 0.0)
     parts = jnp.concatenate(
-        [high, middle, rest - middle, jnp.zeros((4, TILE), F32), hot, hot, hot, jnp.zeros((8, TILE), F32)],
+        [high, middle, rest - middle, jnp.ones((4, TILE), F32), hot, hot, hot, jnp.zeros((8, TILE), F32)],
         axis=0,
     )
-    spread = lax.dot_general(
+    given = lax.dot_general(
         parts.astype(jnp.bfloat16),
-        spread_ref[...],
+        spread,
         (((0,), (0,)), ((), ())),
         preferred_element_type=F32,
     )
-    return lambda s, c: spread[s : s + CHUNK, c * TILE : (c + 1) * TILE]
+    return lambda s, c: given[s : s + CHUNK, c * TILE : (c + 1) * TILE]
 
 
 def j_atoms(side_j, jb):
@@ -232,7 +232,7 @@
 
 
 def pack_kernel(
-    table, side_i, pack_i, charge_i, more_i, mask_ref, typed_ref, plain_ref, pair_ref
+    table, side_i, pack_i, charge_i, more_i, mask_ref, typed_ref, plain_ref, pair_ref, near_i
 ):
     write_mask(mask_ref)
     typed_spread(table, typed_ref)
@@ -249,6 +249,19 @@
     rho, more = packed(table, pack_i, I_BLOCKS, (3, 4, 5))
     for n, value in enumerate((*more, 1.0 / rho, 1.0 / (rho + OFFSET))):
         more_i[n] = value
+    near_i[...] = jnp.zeros_like(near_i)
+    for c in range(4):
+        here = slice(c * TILE, (c + 1) * TILE)
+        value = rho + NECK_GAP
+        if c < 3:
+            value = -pack_i[0:I_BLOCKS, c, :]
+            near_i[0:I_BLOCKS, c, here] = jnp.ones((I_BLOCKS, TILE), F32)
+        high = value.astype(jnp.bfloat16).astype(F32)
+        rest = value - high
+        middle = rest.astype(jnp.bfloat16).astype(F32)
+        near_i[0:I_BLOCKS, 4, here] = high
+        near_i[0:I_BLOCKS, 5, here] = middle
+        near_i[0:I_BLOCKS, 6, here] = rest - middle
 
 
 def keep_kernel(meta, read, kept):
@@ -263,20 +276,24 @@
     kept[LISTED + UNROLL] = count
 
 
-def born_kernel(meta, pack_i, side_j, mask_ref, spread_ref, out_ref, acc):
+def born_kernel(meta, pack_i, near_i, side_j, mask_ref, spread_ref, out_ref, acc):
     acc[...] = jnp.zeros_like(acc)
+    first_rows = spread_ref[0:16, 0 : 4 * TILE].astype(F32)[0:8]
 
     def one_tile(ia, jb, same):
-        col = typed_columns(j_atoms(side_j, jb), spread_ref)
-        xi, yi, zi, rho = (pack_i[ia, c : c + 1, :] for c in range(4))
-        rho_sq, rho_gap = rho * rho, rho + NECK_GAP
+        rows = jnp.concatenate([first_rows, near_i[ia]], axis=0).astype(jnp.bfloat16)
+        rows = jnp.concatenate([rows, spread_ref[0:16, 4 * TILE :]], axis=1)
+        spread = jnp.concatenate([rows, spread_ref[16:, :]], axis=0)
+        col = typed_columns(j_atoms(side_j, jb), spread)
+        rho = pack_i[ia, 3:4, :]
+        rho_sq = rho * rho
         total = jnp.zeros((8, TILE), F32)
         for s in range(0, TILE, CHUNK):
-            _, _, _, q = offsets(xi, yi, zi, col, s)
+            dx, dy, dz, gap = (col(s, c) for c in range(4))
+            q = dx * dx + dy * dy + dz * dz
             base = jnp.maximum(CUT_SQ - q, 0.0)
             weight = base * base * mask_ref[same, s : s + CHUNK, :]
             inv = 1.0 / (q + rho_sq)
-            gap = rho_gap + col(s, 3)
             off = q - gap * gap
             bump = jnp.exp2(off * off * (-LOG2E / NECK_WIDTH))
             total += folded(weight * (col(s, 4) * (inv * inv) + col(s, 5) * bump))
@@ -324,7 +341,7 @@
     packed(table, own_j, 2 * N_ROWS, ())
 
     def one_tile(ia, jb, same):
-        col = typed_columns(j_atoms(side_j, jb), spread_ref)
+        col = typed_columns(j_atoms(side_j, jb), spread_ref[...])
         xi, yi, zi, rho = (pack_i[ia, c : c + 1, :] for c in range(4))
         rho_sq, rho_gap = rho * rho, rho + NECK_GAP
         sums = [jnp.zeros((8, TILE), F32)] * 3
@@ -569,7 +586,7 @@
     sums = ((I_BLOCKS + 1, 8, TILE), F32)
     forces = ((2 * N_ROWS + 1, 3, 8, TILE), F32)
     bf16 = jnp.bfloat16
-    pack_i, charge_i, more_i, mask, typed, plain, paired = called(
+    pack_i, charge_i, more_i, mask, typed, plain, paired, near_i = called(
         pack_kernel,
         [
             (I_BLOCKS + 1, 8, TILE),
@@ -579,6 +596,7 @@
             ((48, 6 * TILE), bf16),
             ((32, 6 * TILE), bf16),
             ((32, 6 * TILE), bf16),
+            (I_BLOCKS + 1, 8, 4 * TILE),
         ],
         [],
         [table],
@@ -589,7 +607,7 @@
         [(N_COLS, I_BLOCKS, TILE)],
         [sums],
         [meta],
-        [pack_i, side_j, mask, typed],
+        [pack_i, near_i, side_j, mask, typed],
     )
     born_parts = exchanged(born_parts, COLS)
     keys, read = transposed_keys(side_j[:, HELD], places)

time: 128 us -> 129 us (level)
  Pallas kernels: 21.2 us -> 25.9 us
  starting transfers between devices: 48.8 us -> 44.1 us
  local copies, waits for them, and re-layouts: 2.72 us -> 4.08 us
  waiting for transfers between devices: 34.3 us -> 33 us
    all_to_all x6, starting transfers between devices: 48.8 us -> 44.1 us  [exchanged(): return lax.all_to_all(pieces, axes, 0, 0, tiled=True)]
    pallas_call x12, Pallas kernels: 21.2 us -> 25.9 us  [called(): pl.pallas_call(kernel, out_shape=[jax.ShapeDtypeStruct(*s) if isinstance(...]
    concatenate x1, local copies, waits for them, and re-layouts: 0.83 us -> 2.2 us  [body(): jnp.concatenate([positions, velocities, old_forces, charges.reshape(row),...]
  transfers between devices with their start and end apart: 6 -> 6, of which waited for: 6 -> 6; matrix products, arithmetic and copies ran while one was open for 4% -> 4% of each run, Pallas kernels for 7% -> 9%
where the time goes in v9:
time: 129 us
  starting transfers between devices  44.1 us (34%)
  waiting for transfers between devices  33 us (26%)
  Pallas kernels  25.9 us (20%)
  blocking collectives  14.9 us (12%)
  other arithmetic  5.88 us (5%)
  local copies, waits for them, and re-layouts  4.08 us (3%)
    all_to_all x6, starting transfers between devices, exchanged(): return lax.all_to_all(pieces, axes, 0, 0, tiled=True)  44.1 us
    all_to_all x6, waiting for transfers between devices, exchanged(): return lax.all_to_all(pieces, axes, 0, 0, tiled=True)  33 us
    pallas_call x12, Pallas kernels, called(): pl.pallas_call(kernel, out_shape=[jax.ShapeDtypeStruct(*s) if isinstance(...  25.9 us
    all_to_all x1, blocking collectives, exchanged(): return lax.all_to_all(pieces, axes, 0, 0, tiled=True)  14.9 us
  transfers between devices with their start and end apart: 6, of which 6 were waited for; matrix products, arithmetic and copies ran while one was open for 4% of the time, Pallas kernels for 9%

profile of v9, /device:TPU:1, one launch (start us, length us, event | category | flops | bytes accessed | tf_op | source)
XLA Modules:
  0.0 128.6 jit_solution(1295219256778867872)
XLA Ops:
  0.6 0.0 copy-start.1
  0.6 0.7 convert_bitcast_fusion
  1.3 0.7 convert_element_type.61
  2.0 2.2 %concatenate.6.joined = f32[13,256]{1,0:T(8,128)S(1)} concatenate(f32[3,256]{1,0:T(4,128)} %param.7, f32[3,256]{1,0:T(4,128)} %param.8, f32[3,256]{1,0:T(4,128)} %param.9, f32[1,256]{1,0:T(1,128)} %bitcast.18, f32[1,256]{1,0:T(1,128)S(1)} %bitcast.17, f32[2,256]{1,0:T(2,128)S(1)} %pad.4), dimensions={0} | concatenate | bytes 26624 | tf_op jit(solution)/shard_map/concatenate | solution.py:562
  4.2 0.7 copy-done
  4.9 1.2 shard_map.94
  6.1 15.6 %all-to-all-start = ((f32[4,3,4,128]{3,2,1,0:T(4,128)}), f32[4,3,4,128]{3,2,1,0:T(4,128)S(1)}, u32[]{:S(2)}, u32[]{:S(2)}) async-start(f32[4,3,4,128]{3,2,1,0:T(4,128)} %get-tuple-element.24), calls=%async_computation | async-start | bytes 49152 | tf_op jit(solution)/shard_map/all_to_all | solution.py:43
  21.8 0.1 eq.88
  21.9 0.1 eq.89
  22.0 0.1 add.224
  22.1 0.1 pad_add_fusion.1.places
  22.1 11.1 %all-to-all-done = f32[4,3,4,128]{3,2,1,0:T(4,128)S(1)} async-done(((f32[4,3,4,128]{3,2,1,0:T(4,128)}), f32[4,3,4,128]{3,2,1,0:T(4,128)S(1)}, u32[]{:S(2)}, u32[]{:S(2)}) %all-to-all-start) | async-done | bytes 24608 | tf_op jit(solution)/shard_map/all_to_all | solution.py:43
  33.2 0.7 broadcast_in_dim.43
  33.9 5.0 %all-to-all-start.1 = ((f32[8,4,3,4,128]{4,3,2,1,0:T(4,128)}), f32[8,4,3,4,128]{4,3,2,1,0:T(4,128)S(1)}, u32[]{:S(2)}, u32[]{:S(2)}) async-start(f32[8,4,3,4,128]{4,3,2,1,0:T(4,128)} %broadcast_in_dim.43), calls=%async_computation.1 | async-start | bytes 393216 | tf_op jit(solution)/shard_map/all_to_all | solution.py:43
  39.0 0.7 fusion.5
  39.7 4.8 %all-to-all-done.1.side_i = f32[8,4,3,4,128]{4,3,2,1,0:T(4,128)S(1)} async-done(((f32[8,4,3,4,128]{4,3,2,1,0:T(4,128)}), f32[8,4,3,4,128]{4,3,2,1,0:T(4,128)S(1)}, u32[]{:S(2)}, u32[]{:S(2)}) %all-to-all-start.1) | async-done | bytes 196640 | tf_op jit(solution)/shard_map/all_to_all | solution.py:43
  44.5 1.3 %shard_map.95 = f32[16,9,4,128]{3,2,1,0:T(4,128)} custom-call(s32[3]{0:T(128)S(1)} %pad_add_fusion.1.places, f32[8,4,3,4,128]{4,3,2,1,0:T(4,128)S(1)} %all-to-all-done.1.side_i), custom_call_target="tpu_custom_call" | custom-call | tf_op jit(solution)/shard_map/pallas_call | solution.py:47
  45.8 9.1 %all-to-all-start.2 = ((f32[16,9,4,128]{3,2,1,0:T(4,128)}), f32[16,9,4,128]{3,2,1,0:T(4,128)S(1)}, u32[]{:S(2)}, u32[]{:S(2)}) async-start(f32[16,9,4,128]{3,2,1,0:T(4,128)} %shard_map.95), calls=%async_computation.2 | async-start | bytes 589824 | tf_op jit(solution)/shard_map/all_to_all | solution.py:43
  55.0 0.6 fusion.11
  55.6 0.1 select_reduce_fusion.1
  55.7 0.1 iota_add_fusion
  55.8 0.1 add.222
  55.8 0.1 convert_element_type.69
  55.9 0.1 convert_element_type.72
  56.0 0.1 select_reduce_fusion
  56.2 1.3 pad_add_fusion.meta
  57.4 0.0 copy-done.1
  57.4 2.6 %shard_map.97 = (f32[65,8,128]{2,1,0:T(8,128)S(1)}, f32[64,128]{1,0:T(8,128)S(1)}, f32[5,64,128]{2,1,0:T(8,128)S(1)}, f32[2,128,128]{2,1,0:T(8,128)S(1)}, bf16[4...) custom-call(f32[7,8]{1,0:T(8,128)S(1)} %copy-done.1, ...), custom_call_target="tpu_custom_call" | custom-call | tf_op jit(solution)/shard_map/pallas_call | solution.py:47
  60.0 6.5 %all-to-all-done.2.side_j = f32[16,9,4,128]{3,2,1,0:T(4,128)S(1)} async-done(((f32[16,9,4,128]{3,2,1,0:T(4,128)}), f32[16,9,4,128]{3,2,1,0:T(4,128)S(1)}, u32[]{:S(2)}, u32[]{:S(2)}) %all-to-all-start.2) | async-done | bytes 294944 | tf_op jit(solution)/shard_map/all_to_all | solution.py:43
  66.5 4.5 %shard_map.100 = f32[8,64,128]{2,1,0:T(8,128)} custom-call(s32[130]{0:T(256)S(1)} %pad_add_fusion.meta, f32[65,8,128]{2,1,0:T(8,128)S(1)} %get-tuple-element.25.pack_i, f32[65,8,512]{2,1,0:T(8,128)S(1)} %get-tuple-element.28.near_i, f32[16,9,4,128]{3,2,1,0:T(4,128)S(1)} %all-to-all-done.2.side_j, f32[2,128,128]{2,1,0:T(8,128)S(1)} %get-tuple-element.29.mask_ref, ...), custom_call_target="tpu_custom_call" | custom-call | tf_op jit(solution)/shard_map/pallas_call | solution.py:47
  71.0 4.5 %all-to-all-start.3 = ((f32[8,64,128]{2,1,0:T(8,128)}), f32[8,64,128]{2,1,0:T(8,128)S(1)}, u32[]{:S(2)}, u32[]{:S(2)}) async-start(f32[8,64,128]{2,1,0:T(8,128)} %shard_map.100), calls=%async_computation.3 | async-start | bytes 524288 | tf_op jit(solution)/shard_map/all_to_all | solution.py:43
  75.5 0.2 broadcast_select_fusion
  75.7 1.2 fusion
  76.9 1.5 %shard_map.99.ready.meta = s32[137]{0:T(256)S(1)} custom-call(s32[130]{0:T(256)S(1)} %pad_add_fusion.meta, s32[64]{0:T(128)S(1)} %or_convert_fusion.read), custom_call_target="tpu_custom_call" | custom-call | tf_op jit(solution)/shard_map/pallas_call | solution.py:47
  78.4 4.0 %all-to-all-done.3.parts = f32[8,64,128]{2,1,0:T(8,128)S(1)} async-done(((f32[8,64,128]{2,1,0:T(8,128)}), f32[8,64,128]{2,1,0:T(8,128)S(1)}, u32[]{:S(2)}, u32[]{:S(2)}) %all-to-all-start.3) | async-done | bytes 262176 | tf_op jit(solution)/shard_map/all_to_all | solution.py:43
  82.4 1.2 shard_map.101
  83.7 5.5 %all-to-all-start.4 = ((f32[16,2,8,128]{3,2,1,0:T(8,128)}), f32[16,2,8,128]{3,2,1,0:T(8,128)S(1)}, u32[]{:S(2)}, u32[]{:S(2)}) async-start(f32[16,2,8,128]{3,2,1,0:T(8,128)} %get-tuple-element.33), calls=%async_computation.4 | async-start | bytes 262144 | tf_op jit(solution)/shard_map/all_to_all | solution.py:43
  89.2 0.1 and_select_fusion.3
  89.3 2.7 %shard_map.96.ready.picked = s32[2057]{0:T(1024)S(1)} custom-call(f32[32,128]{1,0:T(8,128)S(1)} %bitcast.15), custom_call_target="tpu_custom_call" | custom-call | tf_op jit(solution)/shard_map/pallas_call | solution.py:47
  92.0 2.4 %shard_map.98 = (f32[8,8,128]{2,1,0:T(8,128)S(1)}, f32[33,8,128]{2,1,0:T(8,128)S(1)}) custom-call(s32[130]{0:T(256)S(1)} %pad_add_fusion.meta, s32[3]{0:T(128)S(1)} %pad_add_fusion.1.places, f32[7,8]{1,0:T(8,128)S(1)} %copy-done.1, f32[65,8,128]{2,1,0:T(8,128)S(1)} %get-tuple-element.25.pack_i, f32[16,9,4,128]{3,2,1,0:T(4,128)S(1)} %all-to-all-done.2.side_j, ...), custom_call_target="tpu_custom_call" | custom-call | tf_op jit(solution)/shard_map/pallas_call | solution.py:47
  94.4 3.1 %all-to-all-done.4.rad_j = f32[16,2,8,128]{3,2,1,0:T(8,128)S(1)} async-done(((f32[16,2,8,128]{3,2,1,0:T(8,128)}), f32[16,2,8,128]{3,2,1,0:T(8,128)S(1)}, u32[]{:S(2)}, u32[]{:S(2)}) %all-to-all-start.4) | async-done | bytes 131104 | tf_op jit(solution)/shard_map/all_to_all | solution.py:43
  97.5 2.6 %shard_map.102 = f32[8,72,128]{2,1,0:T(8,128)} custom-call(s32[137]{0:T(256)S(1)} %shard_map.99.ready.meta, f32[65,8,128]{2,1,0:T(8,128)S(1)} %get-tuple-element.25.pack_i, f32[16,9,4,128]{3,2,1,0:T(4,128)S(1)} %all-to-all-done.2.side_j, f32[72,128]{1,0:T(8,128)S(1)} %get-tuple-element.32.rad_i.radius_i.radius, f32[16,2,8,128]{3,2,1,0:T(8,128)S(1)} %all-to-all-done.4.rad_j, ...), custom_call_target="tpu_custom_call" | custom-call | tf_op jit(solution)/shard_map/pallas_call | solution.py:47
  100.1 4.3 %all-to-all-start.5 = ((f32[8,72,128]{2,1,0:T(8,128)}), f32[8,72,128]{2,1,0:T(8,128)S(1)}, u32[]{:S(2)}, u32[]{:S(2)}) async-start(f32[8,72,128]{2,1,0:T(8,128)} %shard_map.102), calls=%async_computation.5 | async-start | bytes 589824 | tf_op jit(solution)/shard_map/all_to_all | solution.py:43
  104.4 2.6 %shard_map.103.direct = f32[3,32,128]{2,1,0:T(8,128)S(1)} custom-call(s32[2057]{0:T(1024)S(1)} %shard_map.96.ready.picked, s32[3]{0:T(128)S(1)} %pad_add_fusion.1.places, f32[33,8,128]{2,1,0:T(8,128)S(1)} %get-tuple-element.27.own_j, f32[65,8,128]{2,1,0:T(8,128)S(1)} %get-tuple-element.25.pack_i, f32[16,2,8,128]{3,2,1,0:T(8,128)S(1)} %all-to-all-done.4.rad_j, ...), custom_call_target="tpu_custom_call" | custom-call | tf_op jit(solution)/shard_map/pallas_call | solution.py:47
  107.0 3.4 %all-to-all-done.5.parts = f32[8,72,128]{2,1,0:T(8,128)S(1)} async-done(((f32[8,72,128]{2,1,0:T(8,128)}), f32[8,72,128]{2,1,0:T(8,128)S(1)}, u32[]{:S(2)}, u32[]{:S(2)}) %all-to-all-start.5) | async-done | bytes 294944 | tf_op jit(solution)/shard_map/all_to_all | solution.py:43
  110.4 2.7 %shard_map.104 = (f32[16,8,128]{2,1,0:T(8,128)S(1)}, f32[10,128]{1,0:T(8,128)S(1)}) custom-call(s32[2057]{0:T(1024)S(1)} %shard_map.96.ready.picked, s32[3]{0:T(128)S(1)} %pad_add_fusion.1.places, f32[65,8,128]{2,1,0:T(8,128)S(1)} %get-tuple-element.25.pack_i, f32[33,8,128]{2,1,0:T(8,128)S(1)} %get-tuple-element.27.own_j, ...), custom_call_target="tpu_custom_call" | custom-call | tf_op jit(solution)/shard_map/pallas_call | solution.py:47
  113.1 14.9 %all_to_all.35.parts = f32[16,8,128]{2,1,0:T(8,128)S(1)} all-to-all(f32[16,8,128]{2,1,0:T(8,128)S(1)} %get-tuple-element.38), channel_id=1, replica_groups=mesh['zh'=4,'zl'=4,'yh'=2,'core'=2,'x'=4,'yl'=2] {'zl','yh','core'}, dimensions={0} | all-to-all | bytes 131072 | tf_op jit(solution)/shard_map/all_to_all | solution.py:43
  128.0 0.6 shard_map.105
  (13 shorter events, 0.1 us)
Async XLA Ops:
  0.6 56.8 %copy-start.1 = (f32[7,8]{1,0:T(8,128)S(1)}, f32[7,8]{1,0:T(8,128)}, u32[]{:S(2)}) copy-start(f32[7,8]{1,0:T(8,128)} %table.5) | copy-start | bytes 676
  4.2 0.7 copy-start
  6.1 27.1 %all-to-all-start = ((f32[4,3,4,128]{3,2,1,0:T(4,128)}), f32[4,3,4,128]{3,2,1,0:T(4,128)S(1)}, u32[]{:S(2)}, u32[]{:S(2)}) async-start(f32[4,3,4,128]{3,2,1,0:T(4,128)} %get-tuple-element.24), calls=%async_computation | async-start | bytes 49152 | tf_op jit(solution)/shard_map/all_to_all | solution.py:43
  33.9 10.6 %all-to-all-start.1 = ((f32[8,4,3,4,128]{4,3,2,1,0:T(4,128)}), f32[8,4,3,4,128]{4,3,2,1,0:T(4,128)S(1)}, u32[]{:S(2)}, u32[]{:S(2)}) async-start(f32[8,4,3,4,128]{4,3,2,1,0:T(4,128)} %broadcast_in_dim.43), calls=%async_computation.1 | async-start | bytes 393216 | tf_op jit(solution)/shard_map/all_to_all | solution.py:43
  45.8 20.7 %all-to-all-start.2 = ((f32[16,9,4,128]{3,2,1,0:T(4,128)}), f32[16,9,4,128]{3,2,1,0:T(4,128)S(1)}, u32[]{:S(2)}, u32[]{:S(2)}) async-start(f32[16,9,4,128]{3,2,1,0:T(4,128)} %shard_map.95), calls=%async_computation.2 | async-start | bytes 589824 | tf_op jit(solution)/shard_map/all_to_all | solution.py:43
  71.0 11.4 %all-to-all-start.3 = ((f32[8,64,128]{2,1,0:T(8,128)}), f32[8,64,128]{2,1,0:T(8,128)S(1)}, u32[]{:S(2)}, u32[]{:S(2)}) async-start(f32[8,64,128]{2,1,0:T(8,128)} %shard_map.100), calls=%async_computation.3 | async-start | bytes 524288 | tf_op jit(solution)/shard_map/all_to_all | solution.py:43
  83.7 13.8 %all-to-all-start.4 = ((f32[16,2,8,128]{3,2,1,0:T(8,128)}), f32[16,2,8,128]{3,2,1,0:T(8,128)S(1)}, u32[]{:S(2)}, u32[]{:S(2)}) async-start(f32[16,2,8,128]{3,2,1,0:T(8,128)} %get-tuple-element.33), calls=%async_computation.4 | async-start | bytes 262144 | tf_op jit(solution)/shard_map/all_to_all | solution.py:43
  100.1 10.3 %all-to-all-start.5 = ((f32[8,72,128]{2,1,0:T(8,128)}), f32[8,72,128]{2,1,0:T(8,128)S(1)}, u32[]{:S(2)}, u32[]{:S(2)}) async-start(f32[8,72,128]{2,1,0:T(8,128)} %shard_map.102), calls=%async_computation.5 | async-start | bytes 589824 | tf_op jit(solution)/shard_map/all_to_all | solution.py:43

commit v10 on v9

--- a/solution.py
+++ b/solution.py
@@ -255,13 +255,12 @@
         value = rho + NECK_GAP
         if c < 3:
             value = -pack_i[0:I_BLOCKS, c, :]
-            near_i[0:I_BLOCKS, c, here] = jnp.ones((I_BLOCKS, TILE), F32)
         high = value.astype(jnp.bfloat16).astype(F32)
         rest = value - high
         middle = rest.astype(jnp.bfloat16).astype(F32)
-        near_i[0:I_BLOCKS, 4, here] = high
-        near_i[0:I_BLOCKS, 5, here] = middle
-        near_i[0:I_BLOCKS, 6, here] = rest - middle
+        near_i[0:I_BLOCKS, 0, here] = high
+        near_i[0:I_BLOCKS, 1, here] = middle
+        near_i[0:I_BLOCKS, 2, here] = rest - middle
 
 
 def keep_kernel(meta, read, kept):
@@ -278,7 +277,7 @@
 
 def born_kernel(meta, pack_i, near_i, side_j, mask_ref, spread_ref, out_ref, acc):
     acc[...] = jnp.zeros_like(acc)
-    first_rows = spread_ref[0:16, 0 : 4 * TILE].astype(F32)[0:8]
+    first_rows = spread_ref[0:16, 0 : 4 * TILE].astype(F32)[0:12]
 
     def one_tile(ia, jb, same):
         rows = jnp.concatenate([first_rows, near_i[ia]], axis=0).astype(jnp.bfloat16)
@@ -596,7 +595,7 @@
             ((48, 6 * TILE), bf16),
             ((32, 6 * TILE), bf16),
             ((32, 6 * TILE), bf16),
-            (I_BLOCKS + 1, 8, 4 * TILE),
+            (I_BLOCKS + 1, 4, 4 * TILE),
         ],
         [],
         [table],

time: 129 us -> 127 us (0.984)
  Pallas kernels: 25.9 us -> 28.3 us
  starting transfers between devices: 44.1 us -> 42.1 us
  local copies, waits for them, and re-layouts: 4.08 us -> 2.72 us
    pallas_call x12, Pallas kernels: 25.9 us -> 28.3 us  [called(): pl.pallas_call(kernel, out_shape=[jax.ShapeDtypeStruct(*s) if isinstance(...]
    all_to_all x6, starting transfers between devices: 44.1 us -> 42.1 us  [exchanged(): return lax.all_to_all(pieces, axes, 0, 0, tiled=True)]
    concatenate x1, local copies, waits for them, and re-layouts: 2.2 us -> 0.83 us  [body(): jnp.concatenate([positions, velocities, old_forces, charges.reshape(row),...]
where the time goes in v10:
time: 127 us
  starting transfers between devices  42.1 us (33%)
  waiting for transfers between devices  32.5 us (26%)
  Pallas kernels  28.3 us (22%)
  blocking collectives  14.7 us (12%)
  other arithmetic  5.32 us (4%)
  local copies, waits for them, and re-layouts  2.72 us (2%)
    all_to_all x6, starting transfers between devices, exchanged(): return lax.all_to_all(pieces, axes, 0, 0, tiled=True)  42.1 us
    all_to_all x6, waiting for transfers between devices, exchanged(): return lax.all_to_all(pieces, axes, 0, 0, tiled=True)  32.5 us
    pallas_call x12, Pallas kernels, called(): pl.pallas_call(kernel, out_shape=[jax.ShapeDtypeStruct(*s) if isinstance(...  28.3 us
    all_to_all x1, blocking collectives, exchanged(): return lax.all_to_all(pieces, axes, 0, 0, tiled=True)  14.7 us
  transfers between devices with their start and end apart: 6, of which 6 were waited for; matrix products, arithmetic and copies ran while one was open for 4% of the time, Pallas kernels for 9%

profile of v10, /device:TPU:1, one launch (start us, length us, event | category | flops | bytes accessed | tf_op | source)
XLA Modules:
  0.0 126.5 jit_solution(17351765244522123765)
XLA Ops:
  0.6 0.7 convert_bitcast_fusion
  1.3 0.0 copy-start.1
  1.4 0.6 copy-done.2
  2.0 0.0 copy-done.1
  2.0 0.0 copy-done.3
  2.0 0.8 concatenate.6.joined
  2.9 1.2 shard_map.94
  4.1 15.6 %all-to-all-start = ((f32[4,3,4,128]{3,2,1,0:T(4,128)}), f32[4,3,4,128]{3,2,1,0:T(4,128)S(1)}, u32[]{:S(2)}, u32[]{:S(2)}) async-start(f32[4,3,4,128]{3,2,1,0:T(4,128)} %get-tuple-element.24), calls=%async_computation | async-start | bytes 49152 | tf_op jit(solution)/shard_map/all_to_all | solution.py:43
  19.8 0.1 eq.88
  19.9 0.1 eq.89
  19.9 0.1 add.224
  20.0 0.1 pad_add_fusion.1.places
  20.1 11.1 %all-to-all-done = f32[4,3,4,128]{3,2,1,0:T(4,128)S(1)} async-done(((f32[4,3,4,128]{3,2,1,0:T(4,128)}), f32[4,3,4,128]{3,2,1,0:T(4,128)S(1)}, u32[]{:S(2)}, u32[]{:S(2)}) %all-to-all-start) | async-done | bytes 24608 | tf_op jit(solution)/shard_map/all_to_all | solution.py:43
  31.2 0.7 broadcast_in_dim.43
  31.9 5.0 %all-to-all-start.1 = ((f32[8,4,3,4,128]{4,3,2,1,0:T(4,128)}), f32[8,4,3,4,128]{4,3,2,1,0:T(4,128)S(1)}, u32[]{:S(2)}, u32[]{:S(2)}) async-start(f32[8,4,3,4,128]{4,3,2,1,0:T(4,128)} %broadcast_in_dim.43), calls=%async_computation.1 | async-start | bytes 393216 | tf_op jit(solution)/shard_map/all_to_all | solution.py:43
  37.0 0.8 fusion.5
  37.7 4.7 %all-to-all-done.1.side_i = f32[8,4,3,4,128]{4,3,2,1,0:T(4,128)S(1)} async-done(((f32[8,4,3,4,128]{4,3,2,1,0:T(4,128)}), f32[8,4,3,4,128]{4,3,2,1,0:T(4,128)S(1)}, u32[]{:S(2)}, u32[]{:S(2)}) %all-to-all-start.1) | async-done | bytes 196640 | tf_op jit(solution)/shard_map/all_to_all | solution.py:43
  42.5 1.3 %shard_map.95 = f32[16,9,4,128]{3,2,1,0:T(4,128)} custom-call(s32[3]{0:T(128)S(1)} %pad_add_fusion.1.places, f32[8,4,3,4,128]{4,3,2,1,0:T(4,128)S(1)} %all-to-all-done.1.side_i), custom_call_target="tpu_custom_call" | custom-call | tf_op jit(solution)/shard_map/pallas_call | solution.py:47
  43.8 9.1 %all-to-all-start.2 = ((f32[16,9,4,128]{3,2,1,0:T(4,128)}), f32[16,9,4,128]{3,2,1,0:T(4,128)S(1)}, u32[]{:S(2)}, u32[]{:S(2)}) async-start(f32[16,9,4,128]{3,2,1,0:T(4,128)} %shard_map.95), calls=%async_computation.2 | async-start | bytes 589824 | tf_op jit(solution)/shard_map/all_to_all | solution.py:43
  53.0 0.6 fusion.11
  53.6 0.1 select_reduce_fusion.1
  53.7 0.1 iota_add_fusion
  53.8 0.1 add.222
  53.8 0.1 convert_element_type.69
  53.9 0.1 convert_element_type.72
  54.0 0.1 select_reduce_fusion
  54.2 1.3 %pad_add_fusion.meta = s32[130]{0:T(256)S(1)} fusion(s32[1]{0:T(128)} %bitcast.10, s32[1]{0:T(128)} %bitcast.9, s32[128]{0:T(128)S(1)} %broadcast_add_fusion), kind=kLoop, calls=%fused_computation.64 | loop fusion | flops 260 | bytes 1040 | tf_op jit(solution)/shard_map/concatenate | solution.py:552
  55.5 2.3 %shard_map.97 = (f32[65,8,128]{2,1,0:T(8,128)S(1)}, f32[64,128]{1,0:T(8,128)S(1)}, f32[5,64,128]{2,1,0:T(8,128)S(1)}, f32[2,128,128]{2,1,0:T(8,128)S(1)}, bf16[4...) custom-call(f32[7,8]{1,0:T(8,128)S(1)} %copy-done, ...), custom_call_target="tpu_custom_call" | custom-call | tf_op jit(solution)/shard_map/pallas_call | solution.py:47
  57.8 6.8 %all-to-all-done.2.side_j = f32[16,9,4,128]{3,2,1,0:T(4,128)S(1)} async-done(((f32[16,9,4,128]{3,2,1,0:T(4,128)}), f32[16,9,4,128]{3,2,1,0:T(4,128)S(1)}, u32[]{:S(2)}, u32[]{:S(2)}) %all-to-all-start.2) | async-done | bytes 294944 | tf_op jit(solution)/shard_map/all_to_all | solution.py:43
  64.5 6.2 %shard_map.100 = f32[8,64,128]{2,1,0:T(8,128)} custom-call(s32[130]{0:T(256)S(1)} %pad_add_fusion.meta, f32[65,8,128]{2,1,0:T(8,128)S(1)} %get-tuple-element.25.pack_i, f32[65,4,512]{2,1,0:T(4,128)S(1)} %get-tuple-element.28.near_i, f32[16,9,4,128]{3,2,1,0:T(4,128)S(1)} %all-to-all-done.2.side_j, f32[2,128,128]{2,1,0:T(8,128)S(1)} %get-tuple-element.29.mask_ref, ...), custom_call_target="tpu_custom_call" | custom-call | tf_op jit(solution)/shard_map/pallas_call | solution.py:47
  70.7 3.4 %all-to-all-start.3 = ((f32[8,64,128]{2,1,0:T(8,128)}), f32[8,64,128]{2,1,0:T(8,128)S(1)}, u32[]{:S(2)}, u32[]{:S(2)}) async-start(f32[8,64,128]{2,1,0:T(8,128)} %shard_map.100), calls=%async_computation.3 | async-start | bytes 524288 | tf_op jit(solution)/shard_map/all_to_all | solution.py:43
  74.1 0.2 broadcast_select_fusion
  74.3 1.2 fusion
  75.5 1.6 %shard_map.99.ready.meta = s32[137]{0:T(256)S(1)} custom-call(s32[130]{0:T(256)S(1)} %pad_add_fusion.meta, s32[64]{0:T(128)S(1)} %or_convert_fusion.read), custom_call_target="tpu_custom_call" | custom-call | tf_op jit(solution)/shard_map/pallas_call | solution.py:47
  77.2 2.9 %all-to-all-done.3.parts = f32[8,64,128]{2,1,0:T(8,128)S(1)} async-done(((f32[8,64,128]{2,1,0:T(8,128)}), f32[8,64,128]{2,1,0:T(8,128)S(1)}, u32[]{:S(2)}, u32[]{:S(2)}) %all-to-all-start.3) | async-done | bytes 262176 | tf_op jit(solution)/shard_map/all_to_all | solution.py:43
  80.0 1.3 shard_map.101
  81.3 5.4 %all-to-all-start.4 = ((f32[16,2,8,128]{3,2,1,0:T(8,128)}), f32[16,2,8,128]{3,2,1,0:T(8,128)S(1)}, u32[]{:S(2)}, u32[]{:S(2)}) async-start(f32[16,2,8,128]{3,2,1,0:T(8,128)} %get-tuple-element.33), calls=%async_computation.4 | async-start | bytes 262144 | tf_op jit(solution)/shard_map/all_to_all | solution.py:43
  86.7 0.1 and_select_fusion.3
  86.8 1.7 %shard_map.96.ready.picked = s32[2057]{0:T(1024)S(1)} custom-call(f32[32,128]{1,0:T(8,128)S(1)} %bitcast.15), custom_call_target="tpu_custom_call" | custom-call | tf_op jit(solution)/shard_map/pallas_call | solution.py:47
  88.6 3.7 %shard_map.98 = (f32[8,8,128]{2,1,0:T(8,128)S(1)}, f32[33,8,128]{2,1,0:T(8,128)S(1)}) custom-call(s32[130]{0:T(256)S(1)} %pad_add_fusion.meta, s32[3]{0:T(128)S(1)} %pad_add_fusion.1.places, f32[7,8]{1,0:T(8,128)S(1)} %copy-done, f32[65,8,128]{2,1,0:T(8,128)S(1)} %get-tuple-element.25.pack_i, f32[16,9,4,128]{3,2,1,0:T(4,128)S(1)} %all-to-all-done.2.side_j, ...), custom_call_target="tpu_custom_call" | custom-call | tf_op jit(solution)/shard_map/pallas_call | solution.py:47
  92.2 2.9 %all-to-all-done.4.rad_j = f32[16,2,8,128]{3,2,1,0:T(8,128)S(1)} async-done(((f32[16,2,8,128]{3,2,1,0:T(8,128)}), f32[16,2,8,128]{3,2,1,0:T(8,128)S(1)}, u32[]{:S(2)}, u32[]{:S(2)}) %all-to-all-start.4) | async-done | bytes 131104 | tf_op jit(solution)/shard_map/all_to_all | solution.py:43
  95.2 4.9 %shard_map.102 = f32[8,72,128]{2,1,0:T(8,128)} custom-call(s32[137]{0:T(256)S(1)} %shard_map.99.ready.meta, f32[65,8,128]{2,1,0:T(8,128)S(1)} %get-tuple-element.25.pack_i, f32[16,9,4,128]{3,2,1,0:T(4,128)S(1)} %all-to-all-done.2.side_j, f32[72,128]{1,0:T(8,128)S(1)} %get-tuple-element.32.rad_i.radius_i.radius, f32[16,2,8,128]{3,2,1,0:T(8,128)S(1)} %all-to-all-done.4.rad_j, ...), custom_call_target="tpu_custom_call" | custom-call | tf_op jit(solution)/shard_map/pallas_call | solution.py:47
  100.1 3.4 %all-to-all-start.5 = ((f32[8,72,128]{2,1,0:T(8,128)}), f32[8,72,128]{2,1,0:T(8,128)S(1)}, u32[]{:S(2)}, u32[]{:S(2)}) async-start(f32[8,72,128]{2,1,0:T(8,128)} %shard_map.102), calls=%async_computation.5 | async-start | bytes 589824 | tf_op jit(solution)/shard_map/all_to_all | solution.py:43
  103.6 1.7 %shard_map.103.direct = f32[3,32,128]{2,1,0:T(8,128)S(1)} custom-call(s32[2057]{0:T(1024)S(1)} %shard_map.96.ready.picked, s32[3]{0:T(128)S(1)} %pad_add_fusion.1.places, f32[33,8,128]{2,1,0:T(8,128)S(1)} %get-tuple-element.27.own_j, f32[65,8,128]{2,1,0:T(8,128)S(1)} %get-tuple-element.25.pack_i, f32[16,2,8,128]{3,2,1,0:T(8,128)S(1)} %all-to-all-done.4.rad_j, ...), custom_call_target="tpu_custom_call" | custom-call | tf_op jit(solution)/shard_map/pallas_call | solution.py:47
  105.3 4.1 %all-to-all-done.5.parts = f32[8,72,128]{2,1,0:T(8,128)S(1)} async-done(((f32[8,72,128]{2,1,0:T(8,128)}), f32[8,72,128]{2,1,0:T(8,128)S(1)}, u32[]{:S(2)}, u32[]{:S(2)}) %all-to-all-start.5) | async-done | bytes 294944 | tf_op jit(solution)/shard_map/all_to_all | solution.py:43
  109.4 1.8 %shard_map.104 = (f32[16,8,128]{2,1,0:T(8,128)S(1)}, f32[10,128]{1,0:T(8,128)S(1)}) custom-call(s32[2057]{0:T(1024)S(1)} %shard_map.96.ready.picked, s32[3]{0:T(128)S(1)} %pad_add_fusion.1.places, f32[65,8,128]{2,1,0:T(8,128)S(1)} %get-tuple-element.25.pack_i, f32[33,8,128]{2,1,0:T(8,128)S(1)} %get-tuple-element.27.own_j, ...), custom_call_target="tpu_custom_call" | custom-call | tf_op jit(solution)/shard_map/pallas_call | solution.py:47
  111.2 14.7 %all_to_all.35.parts = f32[16,8,128]{2,1,0:T(8,128)S(1)} all-to-all(f32[16,8,128]{2,1,0:T(8,128)S(1)} %get-tuple-element.38), channel_id=1, replica_groups=mesh['zh'=4,'zl'=4,'yh'=2,'core'=2,'x'=4,'yl'=2] {'zl','yh','core'}, dimensions={0} | all-to-all | bytes 131072 | tf_op jit(solution)/shard_map/all_to_all | solution.py:43
  125.9 0.6 shard_map.105
  (19 shorter events, 0.1 us)
Async XLA Ops:
  0.6 0.7 copy-start.4
  1.3 0.7 copy-start.2
  1.3 0.7 copy-start.1
  1.4 0.7 copy-start.3
  2.0 0.8 copy-start
  4.1 27.1 %all-to-all-start = ((f32[4,3,4,128]{3,2,1,0:T(4,128)}), f32[4,3,4,128]{3,2,1,0:T(4,128)S(1)}, u32[]{:S(2)}, u32[]{:S(2)}) async-start(f32[4,3,4,128]{3,2,1,0:T(4,128)} %get-tuple-element.24), calls=%async_computation | async-start | bytes 49152 | tf_op jit(solution)/shard_map/all_to_all | solution.py:43
  31.9 10.6 %all-to-all-start.1 = ((f32[8,4,3,4,128]{4,3,2,1,0:T(4,128)}), f32[8,4,3,4,128]{4,3,2,1,0:T(4,128)S(1)}, u32[]{:S(2)}, u32[]{:S(2)}) async-start(f32[8,4,3,4,128]{4,3,2,1,0:T(4,128)} %broadcast_in_dim.43), calls=%async_computation.1 | async-start | bytes 393216 | tf_op jit(solution)/shard_map/all_to_all | solution.py:43
  43.8 20.7 %all-to-all-start.2 = ((f32[16,9,4,128]{3,2,1,0:T(4,128)}), f32[16,9,4,128]{3,2,1,0:T(4,128)S(1)}, u32[]{:S(2)}, u32[]{:S(2)}) async-start(f32[16,9,4,128]{3,2,1,0:T(4,128)} %shard_map.95), calls=%async_computation.2 | async-start | bytes 589824 | tf_op jit(solution)/shard_map/all_to_all | solution.py:43
  70.7 9.3 %all-to-all-start.3 = ((f32[8,64,128]{2,1,0:T(8,128)}), f32[8,64,128]{2,1,0:T(8,128)S(1)}, u32[]{:S(2)}, u32[]{:S(2)}) async-start(f32[8,64,128]{2,1,0:T(8,128)} %shard_map.100), calls=%async_computation.3 | async-start | bytes 524288 | tf_op jit(solution)/shard_map/all_to_all | solution.py:43
  81.3 13.9 %all-to-all-start.4 = ((f32[16,2,8,128]{3,2,1,0:T(8,128)}), f32[16,2,8,128]{3,2,1,0:T(8,128)S(1)}, u32[]{:S(2)}, u32[]{:S(2)}) async-start(f32[16,2,8,128]{3,2,1,0:T(8,128)} %get-tuple-element.33), calls=%async_computation.4 | async-start | bytes 262144 | tf_op jit(solution)/shard_map/all_to_all | solution.py:43
  100.1 9.3 %all-to-all-start.5 = ((f32[8,72,128]{2,1,0:T(8,128)}), f32[8,72,128]{2,1,0:T(8,128)S(1)}, u32[]{:S(2)}, u32[]{:S(2)}) async-start(f32[8,72,128]{2,1,0:T(8,128)} %shard_map.102), calls=%async_computation.5 | async-start | bytes 589824 | tf_op jit(solution)/shard_map/all_to_all | solution.py:43

commit v11 on v10

--- a/solution.py
+++ b/solution.py
@@ -86,18 +86,18 @@
         spread_ref[:, c * TILE : (c + 1) * TILE] = jnp.where(hit, 1.0, 0.0).astype(jnp.bfloat16)
 
 
-def columns(rows, spread_ref):
+def columns(rows, spread):
     high = rows.astype(jnp.bfloat16).astype(F32)
     rest = rows - high
     middle = rest.astype(jnp.bfloat16).astype(F32)
-    parts = jnp.concatenate([high, middle, rest - middle, jnp.zeros_like(rows)], axis=0)
-    spread = lax.dot_general(
+    parts = jnp.concatenate([high, middle, rest - middle, jnp.ones_like(rows)], axis=0)
+    given = lax.dot_general(
         parts.astype(jnp.bfloat16),
-        spread_ref[...],
+        spread,
         (((0,), (0,)), ((), ())),
         preferred_element_type=F32,
     )
-    return lambda s, c: spread[s : s + CHUNK, c * TILE : (c + 1) * TILE]
+    return lambda s, c: given[s : s + CHUNK, c * TILE : (c + 1) * TILE]
 
 
 def offsets(xi, yi, zi, col, s):
@@ -386,7 +386,7 @@
         own_q[2 * n : 2 * n + 2] = rad_j[n, 1, pl.ds(places[0] * 2, 2), :]
 
     def one_tile(at, jb, same):
-        col = columns(sides[jb], spread_ref)
+        col = columns(sides[jb], spread_ref[...])
         xi, yi, zi = (own_j[at, c : c + 1, :] for c in range(3))
         radius = own[pl.ds(at, 1), :]
         quarter = 0.25 / radius
@@ -413,25 +413,30 @@
 
 
 def pair_kernel(
-    meta, pack_i, side_j, rad_i, rad_j, slopes, ready, mask_ref, spread_ref, out_ref, acc
+    meta, near_i, side_j, rad_i, rad_j, slopes, ready, mask_ref, spread_ref, out_ref, acc
 ):
     acc[...] = jnp.zeros_like(acc)
+    xyz = 3 * TILE
+    low_rows = spread_ref[16:32, 0:xyz].astype(F32)[0:8]
+    no_rows = jnp.zeros((4, xyz), F32)
 
     def one_tile(ia, jb, same):
         n, b = jb // HELD, jb % HELD
         radius_j, charge_j = (rad_j[n, k, pl.ds(b, 1), :] for k in range(2))
+        rows = jnp.concatenate([low_rows, near_i[ia, :, 0:xyz], no_rows], axis=0)
+        rows = jnp.concatenate([rows.astype(jnp.bfloat16), spread_ref[16:32, xyz:]], axis=1)
         col = columns(
             jnp.concatenate(
                 [side_j[n, b], radius_j, 1.0 / radius_j, charge_j, charge_j], axis=0
             ),
-            spread_ref,
+            jnp.concatenate([spread_ref[0:16, :], rows], axis=0),
         )
-        xi, yi, zi = (pack_i[ia, c : c + 1, :] for c in range(3))
         radius_i = rad_i[pl.ds(ia, 1), :]
         quarter_i = 0.25 / radius_i
         total = jnp.zeros((8, TILE), F32)
         for s in range(0, TILE, CHUNK):
-            _, _, _, q = offsets(xi, yi, zi, col, s)
+            dx, dy, dz = (col(s, c) for c in range(3))
+            q = dx * dx + dy * dy + dz * dz
             base = jnp.maximum(CUT_SQ - q, 0.0)
             weight = base * base * mask_ref[same, s : s + CHUNK, :]
             arg = q * (quarter_i * col(s, 4))
@@ -469,7 +474,7 @@
     fifth = lax.broadcasted_iota(jnp.int32, (8, TILE), 0) == 4
 
     def one_tile(at, jb, same):
-        col = columns(jnp.where(fifth, chain_ref[pl.ds(jb, 1), :], pack_i[jb]), spread_ref)
+        col = columns(jnp.where(fifth, chain_ref[pl.ds(jb, 1), :], pack_i[jb]), spread_ref[...])
         xi, yi, zi, rho, vol, neck = (own_j[at, c : c + 1, :] for c in range(6))
         rho_gap = rho + NECK_GAP
         sums = [jnp.zeros((8, TILE), F32)] * 3
@@ -642,7 +647,7 @@
         [(N_COLS, I_BLOCKS + 8, TILE)],
         [sums],
         [kept_tiles],
-        [pack_i, side_j, radius_i, rad_j, slopes, picked, mask, paired],
+        [near_i, side_j, radius_i, rad_j, slopes, picked, mask, paired],
     )
     grads = exchanged(grads, COLS)
     [direct] = called(

time: 127 us -> 127 us (level)
  blocking collectives: 14.7 us -> 11.9 us
    all_to_all x1, blocking collectives: 14.7 us -> 11.9 us  [exchanged(): return lax.all_to_all(pieces, axes, 0, 0, tiled=True)]
where the time goes in v11:
time: 127 us; the launch traced here: 126 us
  starting transfers between devices  42.8 us (34%)
  waiting for transfers between devices  33.2 us (26%)
  Pallas kernels  28.9 us (23%)
  blocking collectives  11.9 us (9%)
  other arithmetic  5.32 us (4%)
  local copies, waits for them, and re-layouts  2.72 us (2%)
    all_to_all x6, starting transfers between devices, exchanged(): return lax.all_to_all(pieces, axes, 0, 0, tiled=True)  42.8 us
    all_to_all x6, waiting for transfers between devices, exchanged(): return lax.all_to_all(pieces, axes, 0, 0, tiled=True)  33.2 us
    pallas_call x12, Pallas kernels, called(): pl.pallas_call(kernel, out_shape=[jax.ShapeDtypeStruct(*s) if isinstance(...  28.9 us
    all_to_all x1, blocking collectives, exchanged(): return lax.all_to_all(pieces, axes, 0, 0, tiled=True)  11.9 us
  transfers between devices with their start and end apart: 6, of which 6 were waited for; matrix products, arithmetic and copies ran while one was open for 4% of the time, Pallas kernels for 9%

profile of v11, /device:TPU:1, one launch (start us, length us, event | category | flops | bytes accessed | tf_op | source)
XLA Modules:
  0.0 125.8 jit_solution(9503608263611933600)
XLA Ops:
  0.6 0.7 convert_bitcast_fusion
  1.3 0.0 copy-start.1
  1.4 0.6 copy-done.2
  2.0 0.0 copy-done.1
  2.0 0.0 copy-done.3
  2.0 0.8 concatenate.6.joined
  2.9 1.2 shard_map.94
  4.1 15.6 %all-to-all-start = ((f32[4,3,4,128]{3,2,1,0:T(4,128)}), f32[4,3,4,128]{3,2,1,0:T(4,128)S(1)}, u32[]{:S(2)}, u32[]{:S(2)}) async-start(f32[4,3,4,128]{3,2,1,0:T(4,128)} %get-tuple-element.24), calls=%async_computation | async-start | bytes 49152 | tf_op jit(solution)/shard_map/all_to_all | solution.py:43
  19.8 0.1 eq.88
  19.9 0.1 eq.89
  19.9 0.1 add.224
  20.0 0.1 pad_add_fusion.1.places
  20.1 11.1 %all-to-all-done = f32[4,3,4,128]{3,2,1,0:T(4,128)S(1)} async-done(((f32[4,3,4,128]{3,2,1,0:T(4,128)}), f32[4,3,4,128]{3,2,1,0:T(4,128)S(1)}, u32[]{:S(2)}, u32[]{:S(2)}) %all-to-all-start) | async-done | bytes 24608 | tf_op jit(solution)/shard_map/all_to_all | solution.py:43
  31.2 0.7 broadcast_in_dim.43
  31.9 5.0 %all-to-all-start.1 = ((f32[8,4,3,4,128]{4,3,2,1,0:T(4,128)}), f32[8,4,3,4,128]{4,3,2,1,0:T(4,128)S(1)}, u32[]{:S(2)}, u32[]{:S(2)}) async-start(f32[8,4,3,4,128]{4,3,2,1,0:T(4,128)} %broadcast_in_dim.43), calls=%async_computation.1 | async-start | bytes 393216 | tf_op jit(solution)/shard_map/all_to_all | solution.py:43
  37.0 0.8 fusion.5
  37.7 4.7 %all-to-all-done.1.side_i = f32[8,4,3,4,128]{4,3,2,1,0:T(4,128)S(1)} async-done(((f32[8,4,3,4,128]{4,3,2,1,0:T(4,128)}), f32[8,4,3,4,128]{4,3,2,1,0:T(4,128)S(1)}, u32[]{:S(2)}, u32[]{:S(2)}) %all-to-all-start.1) | async-done | bytes 196640 | tf_op jit(solution)/shard_map/all_to_all | solution.py:43
  42.5 1.3 %shard_map.95 = f32[16,9,4,128]{3,2,1,0:T(4,128)} custom-call(s32[3]{0:T(128)S(1)} %pad_add_fusion.1.places, f32[8,4,3,4,128]{4,3,2,1,0:T(4,128)S(1)} %all-to-all-done.1.side_i), custom_call_target="tpu_custom_call" | custom-call | tf_op jit(solution)/shard_map/pallas_call | solution.py:47
  43.8 9.1 %all-to-all-start.2 = ((f32[16,9,4,128]{3,2,1,0:T(4,128)}), f32[16,9,4,128]{3,2,1,0:T(4,128)S(1)}, u32[]{:S(2)}, u32[]{:S(2)}) async-start(f32[16,9,4,128]{3,2,1,0:T(4,128)} %shard_map.95), calls=%async_computation.2 | async-start | bytes 589824 | tf_op jit(solution)/shard_map/all_to_all | solution.py:43
  53.0 0.6 fusion.11
  53.6 0.1 select_reduce_fusion.1
  53.7 0.1 iota_add_fusion
  53.8 0.1 add.222
  53.8 0.1 convert_element_type.69
  53.9 0.1 convert_element_type.72
  54.0 0.1 select_reduce_fusion
  54.2 1.3 %pad_add_fusion.meta = s32[130]{0:T(256)S(1)} fusion(s32[1]{0:T(128)} %bitcast.10, s32[1]{0:T(128)} %bitcast.9, s32[128]{0:T(128)S(1)} %broadcast_add_fusion), kind=kLoop, calls=%fused_computation.64 | loop fusion | flops 260 | bytes 1040 | tf_op jit(solution)/shard_map/concatenate | solution.py:557
  55.5 2.3 %shard_map.97 = (f32[65,8,128]{2,1,0:T(8,128)S(1)}, f32[64,128]{1,0:T(8,128)S(1)}, f32[5,64,128]{2,1,0:T(8,128)S(1)}, f32[2,128,128]{2,1,0:T(8,128)S(1)}, bf16[4...) custom-call(f32[7,8]{1,0:T(8,128)S(1)} %copy-done, ...), custom_call_target="tpu_custom_call" | custom-call | tf_op jit(solution)/shard_map/pallas_call | solution.py:47
  57.8 6.8 %all-to-all-done.2.side_j = f32[16,9,4,128]{3,2,1,0:T(4,128)S(1)} async-done(((f32[16,9,4,128]{3,2,1,0:T(4,128)}), f32[16,9,4,128]{3,2,1,0:T(4,128)S(1)}, u32[]{:S(2)}, u32[]{:S(2)}) %all-to-all-start.2) | async-done | bytes 294944 | tf_op jit(solution)/shard_map/all_to_all | solution.py:43
  64.5 5.6 %shard_map.100 = f32[8,64,128]{2,1,0:T(8,128)} custom-call(s32[130]{0:T(256)S(1)} %pad_add_fusion.meta, f32[65,8,128]{2,1,0:T(8,128)S(1)} %get-tuple-element.25.pack_i, f32[65,4,512]{2,1,0:T(4,128)S(1)} %get-tuple-element.28.near_i, f32[16,9,4,128]{3,2,1,0:T(4,128)S(1)} %all-to-all-done.2.side_j, f32[2,128,128]{2,1,0:T(8,128)S(1)} %get-tuple-element.29.mask_ref, ...), custom_call_target="tpu_custom_call" | custom-call | tf_op jit(solution)/shard_map/pallas_call | solution.py:47
  70.1 3.4 %all-to-all-start.3 = ((f32[8,64,128]{2,1,0:T(8,128)}), f32[8,64,128]{2,1,0:T(8,128)S(1)}, u32[]{:S(2)}, u32[]{:S(2)}) async-start(f32[8,64,128]{2,1,0:T(8,128)} %shard_map.100), calls=%async_computation.3 | async-start | bytes 524288 | tf_op jit(solution)/shard_map/all_to_all | solution.py:43
  73.5 0.2 broadcast_select_fusion
  73.7 1.2 fusion
  74.9 1.6 %shard_map.99.ready.meta = s32[137]{0:T(256)S(1)} custom-call(s32[130]{0:T(256)S(1)} %pad_add_fusion.meta, s32[64]{0:T(128)S(1)} %or_convert_fusion.read), custom_call_target="tpu_custom_call" | custom-call | tf_op jit(solution)/shard_map/pallas_call | solution.py:47
  76.5 2.9 %all-to-all-done.3.parts = f32[8,64,128]{2,1,0:T(8,128)S(1)} async-done(((f32[8,64,128]{2,1,0:T(8,128)}), f32[8,64,128]{2,1,0:T(8,128)S(1)}, u32[]{:S(2)}, u32[]{:S(2)}) %all-to-all-start.3) | async-done | bytes 262176 | tf_op jit(solution)/shard_map/all_to_all | solution.py:43
  79.4 1.3 %shard_map.101 = (f32[72,128]{1,0:T(8,128)S(1)}, f32[16,2,8,128]{3,2,1,0:T(8,128)}, f32[64,128]{1,0:T(8,128)S(1)}) custom-call(s32[3]{0:T(128)S(1)} %pad_add_fusion.1.places, f32[8,64,128]{2,1,0:T(8,128)S(1)} %all-to-all-done.3.parts, f32[65,8,128]{2,1,0:T(8,128)S(1)} %get-tuple-element.25.pack_i, f32[5,64,128]{2,1,0:T(8,128)S(1)} %get-tuple-element.30.more_i, ...), custom_call_target="tpu_custom_call" | custom-call | tf_op jit(solution)/shard_map/pallas_call | solution.py:47
  80.6 6.2 %all-to-all-start.4 = ((f32[16,2,8,128]{3,2,1,0:T(8,128)}), f32[16,2,8,128]{3,2,1,0:T(8,128)S(1)}, u32[]{:S(2)}, u32[]{:S(2)}) async-start(f32[16,2,8,128]{3,2,1,0:T(8,128)} %get-tuple-element.33), calls=%async_computation.4 | async-start | bytes 262144 | tf_op jit(solution)/shard_map/all_to_all | solution.py:43
  86.8 0.1 and_select_fusion.3
  86.9 2.4 %shard_map.96.ready.picked = s32[2057]{0:T(1024)S(1)} custom-call(f32[32,128]{1,0:T(8,128)S(1)} %bitcast.15), custom_call_target="tpu_custom_call" | custom-call | tf_op jit(solution)/shard_map/pallas_call | solution.py:47
  89.4 2.4 %shard_map.98 = (f32[8,8,128]{2,1,0:T(8,128)S(1)}, f32[33,8,128]{2,1,0:T(8,128)S(1)}) custom-call(s32[130]{0:T(256)S(1)} %pad_add_fusion.meta, s32[3]{0:T(128)S(1)} %pad_add_fusion.1.places, f32[7,8]{1,0:T(8,128)S(1)} %copy-done, f32[65,8,128]{2,1,0:T(8,128)S(1)} %get-tuple-element.25.pack_i, f32[16,9,4,128]{3,2,1,0:T(4,128)S(1)} %all-to-all-done.2.side_j, ...), custom_call_target="tpu_custom_call" | custom-call | tf_op jit(solution)/shard_map/pallas_call | solution.py:47
  91.8 3.4 %all-to-all-done.4.rad_j = f32[16,2,8,128]{3,2,1,0:T(8,128)S(1)} async-done(((f32[16,2,8,128]{3,2,1,0:T(8,128)}), f32[16,2,8,128]{3,2,1,0:T(8,128)S(1)}, u32[]{:S(2)}, u32[]{:S(2)}) %all-to-all-start.4) | async-done | bytes 131104 | tf_op jit(solution)/shard_map/all_to_all | solution.py:43
  95.2 5.0 %shard_map.102 = f32[8,72,128]{2,1,0:T(8,128)} custom-call(s32[137]{0:T(256)S(1)} %shard_map.99.ready.meta, f32[65,4,512]{2,1,0:T(4,128)S(1)} %get-tuple-element.28.near_i, f32[16,9,4,128]{3,2,1,0:T(4,128)S(1)} %all-to-all-done.2.side_j, f32[72,128]{1,0:T(8,128)S(1)} %get-tuple-element.32.rad_i.radius_i.radius, f32[16,2,8,128]{3,2,1,0:T(8,128)S(1)} %all-to-all-done.4.rad_j, ...), custom_call_target="tpu_custom_call" | custom-call | tf_op jit(solution)/shard_map/pallas_call | solution.py:47
  100.2 3.4 %all-to-all-start.5 = ((f32[8,72,128]{2,1,0:T(8,128)}), f32[8,72,128]{2,1,0:T(8,128)S(1)}, u32[]{:S(2)}, u32[]{:S(2)}) async-start(f32[8,72,128]{2,1,0:T(8,128)} %shard_map.102), calls=%async_computation.5 | async-start | bytes 589824 | tf_op jit(solution)/shard_map/all_to_all | solution.py:43
  103.6 2.6 %shard_map.103.direct = f32[3,32,128]{2,1,0:T(8,128)S(1)} custom-call(s32[2057]{0:T(1024)S(1)} %shard_map.96.ready.picked, s32[3]{0:T(128)S(1)} %pad_add_fusion.1.places, f32[33,8,128]{2,1,0:T(8,128)S(1)} %get-tuple-element.27.own_j, f32[65,8,128]{2,1,0:T(8,128)S(1)} %get-tuple-element.25.pack_i, f32[16,2,8,128]{3,2,1,0:T(8,128)S(1)} %all-to-all-done.4.rad_j, ...), custom_call_target="tpu_custom_call" | custom-call | tf_op jit(solution)/shard_map/pallas_call | solution.py:47
  106.2 4.3 %all-to-all-done.5.parts = f32[8,72,128]{2,1,0:T(8,128)S(1)} async-done(((f32[8,72,128]{2,1,0:T(8,128)}), f32[8,72,128]{2,1,0:T(8,128)S(1)}, u32[]{:S(2)}, u32[]{:S(2)}) %all-to-all-start.5) | async-done | bytes 294944 | tf_op jit(solution)/shard_map/all_to_all | solution.py:43
  110.5 2.7 %shard_map.104 = (f32[16,8,128]{2,1,0:T(8,128)S(1)}, f32[10,128]{1,0:T(8,128)S(1)}) custom-call(s32[2057]{0:T(1024)S(1)} %shard_map.96.ready.picked, s32[3]{0:T(128)S(1)} %pad_add_fusion.1.places, f32[65,8,128]{2,1,0:T(8,128)S(1)} %get-tuple-element.25.pack_i, f32[33,8,128]{2,1,0:T(8,128)S(1)} %get-tuple-element.27.own_j, ...), custom_call_target="tpu_custom_call" | custom-call | tf_op jit(solution)/shard_map/pallas_call | solution.py:47
  113.2 11.9 %all_to_all.35.parts = f32[16,8,128]{2,1,0:T(8,128)S(1)} all-to-all(f32[16,8,128]{2,1,0:T(8,128)S(1)} %get-tuple-element.38), channel_id=1, replica_groups=mesh['zh'=4,'zl'=4,'yh'=2,'core'=2,'x'=4,'yl'=2] {'zl','yh','core'}, dimensions={0} | all-to-all | bytes 131072 | tf_op jit(solution)/shard_map/all_to_all | solution.py:43
  125.1 0.6 shard_map.105
  (19 shorter events, 0.1 us)
Async XLA Ops:
  0.6 0.7 copy-start.4
  1.3 0.7 copy-start.2
  1.3 0.7 copy-start.1
  1.4 0.7 copy-start.3
  2.0 0.8 copy-start
  4.1 27.1 %all-to-all-start = ((f32[4,3,4,128]{3,2,1,0:T(4,128)}), f32[4,3,4,128]{3,2,1,0:T(4,128)S(1)}, u32[]{:S(2)}, u32[]{:S(2)}) async-start(f32[4,3,4,128]{3,2,1,0:T(4,128)} %get-tuple-element.24), calls=%async_computation | async-start | bytes 49152 | tf_op jit(solution)/shard_map/all_to_all | solution.py:43
  31.9 10.6 %all-to-all-start.1 = ((f32[8,4,3,4,128]{4,3,2,1,0:T(4,128)}), f32[8,4,3,4,128]{4,3,2,1,0:T(4,128)S(1)}, u32[]{:S(2)}, u32[]{:S(2)}) async-start(f32[8,4,3,4,128]{4,3,2,1,0:T(4,128)} %broadcast_in_dim.43), calls=%async_computation.1 | async-start | bytes 393216 | tf_op jit(solution)/shard_map/all_to_all | solution.py:43
  43.8 20.7 %all-to-all-start.2 = ((f32[16,9,4,128]{3,2,1,0:T(4,128)}), f32[16,9,4,128]{3,2,1,0:T(4,128)S(1)}, u32[]{:S(2)}, u32[]{:S(2)}) async-start(f32[16,9,4,128]{3,2,1,0:T(4,128)} %shard_map.95), calls=%async_computation.2 | async-start | bytes 589824 | tf_op jit(solution)/shard_map/all_to_all | solution.py:43
  70.1 9.3 %all-to-all-start.3 = ((f32[8,64,128]{2,1,0:T(8,128)}), f32[8,64,128]{2,1,0:T(8,128)S(1)}, u32[]{:S(2)}, u32[]{:S(2)}) async-start(f32[8,64,128]{2,1,0:T(8,128)} %shard_map.100), calls=%async_computation.3 | async-start | bytes 524288 | tf_op jit(solution)/shard_map/all_to_all | solution.py:43
  80.6 14.6 %all-to-all-start.4 = ((f32[16,2,8,128]{3,2,1,0:T(8,128)}), f32[16,2,8,128]{3,2,1,0:T(8,128)S(1)}, u32[]{:S(2)}, u32[]{:S(2)}) async-start(f32[16,2,8,128]{3,2,1,0:T(8,128)} %get-tuple-element.33), calls=%async_computation.4 | async-start | bytes 262144 | tf_op jit(solution)/shard_map/all_to_all | solution.py:43
  100.2 10.3 %all-to-all-start.5 = ((f32[8,72,128]{2,1,0:T(8,128)}), f32[8,72,128]{2,1,0:T(8,128)S(1)}, u32[]{:S(2)}, u32[]{:S(2)}) async-start(f32[8,72,128]{2,1,0:T(8,128)} %shard_map.102), calls=%async_computation.5 | async-start | bytes 589824 | tf_op jit(solution)/shard_map/all_to_all | solution.py:43
